TPU v7x, 32 devices: a whole 2x2x4 slice. The times are simulated.
32 devices in a mesh: pair: 32 (over z, y, x, core), aux: 1.
Axes of the slice: x: 2, y: 2, z: 4, core: 2. Of those that a mesh axis runs over, the one named last changes fastest.
Arguments:
- amplitudes: bfloat16 [32, 256, 256], P('pair'), may hold values from -6 to 6
- ranks: int32 [32], P('pair'), may hold values from 64 to 256
- neighbours: int32 [32, 16], P('pair', 'aux'), may hold values from 0 to 31, as said below
- intersections: bfloat16 [32, 16, 256, 256], P('pair', 'aux'), may hold values from -0.375 to 0.375
- couplings: float32 [32, 16], P('pair', 'aux'), may hold values from -1 to 1
- energies: float32 [32, 256], P('pair'), may hold values from 0.5 to 4
- factors: bfloat16 [32, 2, 5120, 256], P('pair', None, 'aux'), may hold values from -1.75 to 1.75
Outputs:
- residual: float32 [32, 256, 256], P('pair', 'aux')
- updated: float32 [32, 256, 256], P('pair', 'aux')
Inputs may be any that keep to these rules, and one draw needn't show every extreme that they name: `neighbours`: the 16 coupled pairs of pair p are distinct and lie among the pairs p - 8 to p + 8, counted modulo 32.
All inputs are finite; a program needn't handle non-finite values.
Results may differ from a plain program's by a relative error of at most 0.0022.
Values may be sent and summed in bfloat16 or wider, within the bound.
No kernel may reach another device: no remote copies, remote signals or barrier semaphores. Data moves between devices by JAX's collectives and lax.ppermute only.
A program may use at most 64 MiB of HBM per device.

v0:
```python
import jax
import jax.numpy as jnp
from jax import lax
from jax.sharding import PartitionSpec as P

WIN = 8


def shifted(value, axis, steps):
    count = lax.axis_size(axis)
    pairs = [(source, (source + steps) % count) for source in range(count)]
    return lax.ppermute(value, axis, pairs)


def shards(amplitudes, ranks, neighbours, intersections, couplings, energies, factors):
    pair_dev = amplitudes.shape[0]
    pno_width = amplitudes.shape[1]
    aux_count = lax.axis_size("aux")
    pair_count = lax.axis_size("pair")
    row_span = pno_width // aux_count
    aux_index = lax.axis_index("aux")
    first_row = aux_index * row_span
    reach = (WIN + pair_dev - 1) // pair_dev
    positions = jnp.arange(pno_width)
    live_rows = positions[None, :] < ranks[:, None]
    square_mask = live_rows[:, :, None] & live_rows[:, None, :]
    masked = jnp.where(square_mask, amplitudes, jnp.zeros((), jnp.bfloat16))
    blocks = []
    for step in range(-reach, reach + 1):
        if step == 0:
            blocks.append(masked)
        else:
            blocks.append(shifted(masked, "pair", -step))
    extended = jnp.concatenate(blocks, axis=0)
    offset = lax.axis_index("pair") * pair_dev - reach * pair_dev
    nearby = (neighbours - offset) % (pair_dev * pair_count)
    partial_sum = jnp.einsum(
        "pqa,pqb->pab", factors[:, 0], factors[:, 1], preferred_element_type=jnp.float32
    )
    for column in range(neighbours.shape[1]):
        picked = extended[nearby[:, column]]
        intersection_now = intersections[:, column]
        half_product = jnp.einsum(
            "pac,pcd->pad", intersection_now, picked, preferred_element_type=jnp.float32
        ).astype(jnp.bfloat16)
        projected = jnp.einsum(
            "pad,pbd->pab", half_product, intersection_now, preferred_element_type=jnp.float32
        )
        partial_sum = partial_sum + couplings[:, column][:, None, None] * projected
    summed = lax.psum_scatter(partial_sum, "aux", scatter_dimension=1, tiled=True)
    row_energy = lax.dynamic_slice_in_dim(energies, first_row, row_span, 1)
    denominator = row_energy[:, :, None] + energies[:, None, :]
    row_amp = lax.dynamic_slice_in_dim(masked, first_row, row_span, 1).astype(jnp.float32)
    row_mask = lax.dynamic_slice_in_dim(square_mask, first_row, row_span, 1)
    residual = jnp.where(row_mask, summed + denominator * row_amp, jnp.zeros((), jnp.float32))
    return (residual, row_amp - residual / denominator)


def solution(mesh):
    return jax.shard_map(
        shards,
        mesh=mesh,
        in_specs=(
            P("pair", None, None),
            P("pair"),
            P("pair", "aux"),
            P("pair", "aux", None, None),
            P("pair", "aux"),
            P("pair", None),
            P("pair", None, "aux", None),
        ),
        out_specs=(P("pair", "aux", None), P("pair", "aux", None)),
        check_vma=False,
    )
```

profile of v0, /device:TPU:0, one launch (start us, length us, event | category | flops | bytes accessed | tf_op | source)
XLA Modules:
  0.0 113.8 jit_solution(2004513649793362825)
XLA Ops:
  1.3 1.0 and_select_fusion
  2.3 3.1 %collective-permute-start = (bf16[1,256,256]{2,1,0:T(8,128)(2,1)S(1)}, bf16[1,256,256]{2,1,0:T(8,128)(2,1)S(1)}, u32[]{:S(2)}, u32[]{:S(2)}) collective-permute-start(bf16[1,256,256]{2,1,0:T(8,128)(2,1)S(1)} %and_select_fusion), channel_id=1, source_target_pairs={{0,8},{1,9},{2,10},{3,11},{4,12},{5,13},{6,14},{7,15},{8,16},{9,17... | collective-permute-start | bytes 393224 | tf_op jit(solution)/shard_map/ppermute | solution.py:12
  5.4 1.6 %collective-permute-start.1 = (bf16[1,256,256]{2,1,0:T(8,128)(2,1)S(1)}, bf16[1,256,256]{2,1,0:T(8,128)(2,1)S(1)}, u32[]{:S(2)}, u32[]{:S(2)}) collective-permute-start(bf16[1,256,256]{2,1,0:T(8,128)(2,1)S(1)} %and_select_fusion), channel_id=1, source_target_pairs={{0,7},{1,8},{2,9},{3,10},{4,11},{5,12},{6,13},{7,14},{8,15},{9,16}... | collective-permute-start | bytes 393224 | tf_op jit(solution)/shard_map/ppermute | solution.py:12
  7.0 1.5 %collective-permute-start.2 = (bf16[1,256,256]{2,1,0:T(8,128)(2,1)S(1)}, bf16[1,256,256]{2,1,0:T(8,128)(2,1)S(1)}, u32[]{:S(2)}, u32[]{:S(2)}) collective-permute-start(bf16[1,256,256]{2,1,0:T(8,128)(2,1)S(1)} %and_select_fusion), channel_id=1, source_target_pairs={{0,6},{1,7},{2,8},{3,9},{4,10},{5,11},{6,12},{7,13},{8,14},{9,15},... | collective-permute-start | bytes 393224 | tf_op jit(solution)/shard_map/ppermute | solution.py:12
  8.5 1.8 %collective-permute-start.3 = (bf16[1,256,256]{2,1,0:T(8,128)(2,1)S(1)}, bf16[1,256,256]{2,1,0:T(8,128)(2,1)S(1)}, u32[]{:S(2)}, u32[]{:S(2)}) collective-permute-start(bf16[1,256,256]{2,1,0:T(8,128)(2,1)S(1)} %and_select_fusion), channel_id=1, source_target_pairs={{0,5},{1,6},{2,7},{3,8},{4,9},{5,10},{6,11},{7,12},{8,13},{9,14},{... | collective-permute-start | bytes 393224 | tf_op jit(solution)/shard_map/ppermute | solution.py:12
  10.4 1.5 %collective-permute-start.4 = (bf16[1,256,256]{2,1,0:T(8,128)(2,1)S(1)}, bf16[1,256,256]{2,1,0:T(8,128)(2,1)S(1)}, u32[]{:S(2)}, u32[]{:S(2)}) collective-permute-start(bf16[1,256,256]{2,1,0:T(8,128)(2,1)S(1)} %and_select_fusion), channel_id=1, source_target_pairs={{0,4},{1,5},{2,6},{3,7},{4,8},{5,9},{6,10},{7,11},{8,12},{9,13},{1... | collective-permute-start | bytes 393224 | tf_op jit(solution)/shard_map/ppermute | solution.py:12
  11.9 3.4 %fusion = f32[256,256]{1,0:T(8,128)S(1)} fusion(bf16[1,2,5120,256]{3,2,1,0:T(8,128)(2,1)} %param.13), kind=kOutput, calls=%fused_computation | convolution fusion | flops 671088640 | bytes 5505024 | tf_op jit(solution)/shard_map/pqa,pqb->pab/dot_general | solution.py:37
  48.0 1.8 %collective-permute-start.6 = (bf16[1,256,256]{2,1,0:T(8,128)(2,1)S(1)}, bf16[1,256,256]{2,1,0:T(8,128)(2,1)S(1)}, u32[]{:S(2)}, u32[]{:S(2)}) collective-permute-start(bf16[1,256,256]{2,1,0:T(8,128)(2,1)S(1)} %and_select_fusion), channel_id=1, source_target_pairs={{0,2},{1,3},{2,4},{3,5},{4,6},{5,7},{6,8},{7,9},{8,10},{9,11},{10,... | collective-permute-start | bytes 393224 | tf_op jit(solution)/shard_map/ppermute | solution.py:12
  51.1 5.3 %collective-permute-start.8 = (bf16[1,256,256]{2,1,0:T(8,128)(2,1)S(1)}, bf16[1,256,256]{2,1,0:T(8,128)(2,1)S(1)}, u32[]{:S(2)}, u32[]{:S(2)}) collective-permute-start(bf16[1,256,256]{2,1,0:T(8,128)(2,1)S(1)} %and_select_fusion), channel_id=1, source_target_pairs={{0,31},{1,0},{2,1},{3,2},{4,3},{5,4},{6,5},{7,6},{8,7},{9,8},{10,9... | collective-permute-start | bytes 393224 | tf_op jit(solution)/shard_map/ppermute | solution.py:12
  58.0 1.2 %collective-permute-start.10 = (bf16[1,256,256]{2,1,0:T(8,128)(2,1)S(1)}, bf16[1,256,256]{2,1,0:T(8,128)(2,1)S(1)}, u32[]{:S(2)}, u32[]{:S(2)}) collective-permute-start(bf16[1,256,256]{2,1,0:T(8,128)(2,1)S(1)} %and_select_fusion), channel_id=1, source_target_pairs={{0,29},{1,30},{2,31},{3,0},{4,1},{5,2},{6,3},{7,4},{8,5},{9,6},{10... | collective-permute-start | bytes 393224 | tf_op jit(solution)/shard_map/ppermute | solution.py:12
  60.1 1.2 %collective-permute-start.11 = (bf16[1,256,256]{2,1,0:T(8,128)(2,1)S(1)}, bf16[1,256,256]{2,1,0:T(8,128)(2,1)S(1)}, u32[]{:S(2)}, u32[]{:S(2)}) collective-permute-start(bf16[1,256,256]{2,1,0:T(8,128)(2,1)S(1)} %and_select_fusion), channel_id=1, source_target_pairs={{0,28},{1,29},{2,30},{3,31},{4,0},{5,1},{6,2},{7,3},{8,4},{9,5},{1... | collective-permute-start | bytes 393224 | tf_op jit(solution)/shard_map/ppermute | solution.py:12
  63.6 2.8 %collective-permute-start.13 = (bf16[1,256,256]{2,1,0:T(8,128)(2,1)S(1)}, bf16[1,256,256]{2,1,0:T(8,128)(2,1)S(1)}, u32[]{:S(2)}, u32[]{:S(2)}) collective-permute-start(bf16[1,256,256]{2,1,0:T(8,128)(2,1)S(1)} %and_select_fusion), channel_id=1, source_target_pairs={{0,26},{1,27},{2,28},{3,29},{4,30},{5,31},{6,0},{7,1},{8,2},{9,3},... | collective-permute-start | bytes 393224 | tf_op jit(solution)/shard_map/ppermute | solution.py:12
  67.7 1.4 %collective-permute-start.15 = (bf16[1,256,256]{2,1,0:T(8,128)(2,1)S(1)}, bf16[1,256,256]{2,1,0:T(8,128)(2,1)S(1)}, u32[]{:S(2)}, u32[]{:S(2)}) collective-permute-start(bf16[1,256,256]{2,1,0:T(8,128)(2,1)S(1)} %and_select_fusion), channel_id=1, source_target_pairs={{0,24},{1,25},{2,26},{3,27},{4,28},{5,29},{6,30},{7,31},{8,0},{9,1... | collective-permute-start | bytes 393224 | tf_op jit(solution)/shard_map/ppermute | solution.py:12
  70.5 3.0 %collective-permute-done.12 = bf16[1,256,256]{2,1,0:T(8,128)(2,1)S(1)} collective-permute-done((bf16[1,256,256]{2,1,0:T(8,128)(2,1)S(1)}, bf16[1,256,256]{2,1,0:T(8,128)(2,1)S(1)}, u32[]{:S(2)}, u32[]{:S(2)}) %collective-permute-start.12) | collective-permute-done | bytes 131104 | tf_op jit(solution)/shard_map/ppermute | solution.py:12
  74.8 1.5 %collective-permute-done.14 = bf16[1,256,256]{2,1,0:T(8,128)(2,1)S(1)} collective-permute-done((bf16[1,256,256]{2,1,0:T(8,128)(2,1)S(1)}, bf16[1,256,256]{2,1,0:T(8,128)(2,1)S(1)}, u32[]{:S(2)}, u32[]{:S(2)}) %collective-permute-start.14) | collective-permute-done | bytes 131104 | tf_op jit(solution)/shard_map/ppermute | solution.py:12
  77.0 3.1 %collective-permute-done.15 = bf16[1,256,256]{2,1,0:T(8,128)(2,1)S(1)} collective-permute-done((bf16[1,256,256]{2,1,0:T(8,128)(2,1)S(1)}, bf16[1,256,256]{2,1,0:T(8,128)(2,1)S(1)}, u32[]{:S(2)}, u32[]{:S(2)}) %collective-permute-start.15) | collective-permute-done | bytes 131104 | tf_op jit(solution)/shard_map/ppermute | solution.py:12
  80.8 2.0 %fusion.21 = f32[256,256]{1,0:T(8,128)S(1)} fusion(f32[256,256]{1,0:T(8,128)S(1)} %fusion, bf16[17,256,256]{2,1,0:T(8,128)(2,1)} %constant_dynamic-update-slice_fusion, s32[]{:T(128)} %bitcast.5, bf16[1,16,256,256]{3,2,1,0:T(8,128)(2,1)S(1)} %copy-done, f32[]{:T(128)} %bitcast.3), kind=kOutput, calls=%fused_computation.37 | convolution fusion | flops 67305472 | bytes 918528 | tf_op jit(solution)/shard_map/pad,pbd->pab/dot_general | solution.py:46
  82.8 1.9 %fusion.20 = f32[256,256]{1,0:T(8,128)S(1)} fusion(f32[256,256]{1,0:T(8,128)S(1)} %fusion.21, bf16[17,256,256]{2,1,0:T(8,128)(2,1)} %constant_dynamic-update-slice_fusion, s32[]{:T(128)} %bitcast.10, bf16[1,16,256,256]{3,2,1,0:T(8,128)(2,1)S(1)} %copy-done, f32[]{:T(128)} %bitcast.8), kind=kOutput, calls=%fused_computation.35 | convolution fusion | flops 67305472 | bytes 918528 | tf_op jit(solution)/shard_map/pad,pbd->pab/dot_general | solution.py:46
  84.7 1.9 %fusion.19 = f32[256,256]{1,0:T(8,128)S(1)} fusion(f32[256,256]{1,0:T(8,128)S(1)} %fusion.20, bf16[17,256,256]{2,1,0:T(8,128)(2,1)} %constant_dynamic-update-slice_fusion, s32[]{:T(128)} %bitcast.15, bf16[1,16,256,256]{3,2,1,0:T(8,128)(2,1)S(1)} %copy-done, f32[]{:T(128)} %bitcast.13), kind=kOutput, calls=%fused_computation.33 | convolution fusion | flops 67305472 | bytes 918528 | tf_op jit(solution)/shard_map/pad,pbd->pab/dot_general | solution.py:46
  86.6 2.0 %fusion.18 = f32[256,256]{1,0:T(8,128)S(1)} fusion(f32[256,256]{1,0:T(8,128)S(1)} %fusion.19, bf16[17,256,256]{2,1,0:T(8,128)(2,1)} %constant_dynamic-update-slice_fusion, s32[]{:T(128)} %bitcast.20, bf16[1,16,256,256]{3,2,1,0:T(8,128)(2,1)S(1)} %copy-done, f32[]{:T(128)} %bitcast.18), kind=kOutput, calls=%fused_computation.31 | convolution fusion | flops 67305472 | bytes 918528 | tf_op jit(solution)/shard_map/pad,pbd->pab/dot_general | solution.py:46
  88.6 1.9 %fusion.17 = f32[256,256]{1,0:T(8,128)S(1)} fusion(f32[256,256]{1,0:T(8,128)S(1)} %fusion.18, bf16[17,256,256]{2,1,0:T(8,128)(2,1)} %constant_dynamic-update-slice_fusion, s32[]{:T(128)} %bitcast.25, bf16[1,16,256,256]{3,2,1,0:T(8,128)(2,1)S(1)} %copy-done, f32[]{:T(128)} %bitcast.23), kind=kOutput, calls=%fused_computation.29 | convolution fusion | flops 67305472 | bytes 918528 | tf_op jit(solution)/shard_map/pad,pbd->pab/dot_general | solution.py:46
  90.6 2.1 %fusion.16 = f32[256,256]{1,0:T(8,128)S(1)} fusion(f32[256,256]{1,0:T(8,128)S(1)} %fusion.17, bf16[17,256,256]{2,1,0:T(8,128)(2,1)} %constant_dynamic-update-slice_fusion, s32[]{:T(128)} %bitcast.30, bf16[1,16,256,256]{3,2,1,0:T(8,128)(2,1)S(1)} %copy-done, f32[]{:T(128)} %bitcast.28), kind=kOutput, calls=%fused_computation.27 | convolution fusion | flops 67305472 | bytes 918528 | tf_op jit(solution)/shard_map/pad,pbd->pab/dot_general | solution.py:46
  92.7 1.9 %fusion.15 = f32[256,256]{1,0:T(8,128)S(1)} fusion(f32[256,256]{1,0:T(8,128)S(1)} %fusion.16, bf16[17,256,256]{2,1,0:T(8,128)(2,1)} %constant_dynamic-update-slice_fusion, s32[]{:T(128)} %bitcast.35, bf16[1,16,256,256]{3,2,1,0:T(8,128)(2,1)S(1)} %copy-done, f32[]{:T(128)} %bitcast.33), kind=kOutput, calls=%fused_computation.25 | convolution fusion | flops 67305472 | bytes 918528 | tf_op jit(solution)/shard_map/pad,pbd->pab/dot_general | solution.py:46
  94.6 2.0 %fusion.14 = f32[256,256]{1,0:T(8,128)S(1)} fusion(f32[256,256]{1,0:T(8,128)S(1)} %fusion.15, bf16[17,256,256]{2,1,0:T(8,128)(2,1)} %constant_dynamic-update-slice_fusion, s32[]{:T(128)} %bitcast.40, bf16[1,16,256,256]{3,2,1,0:T(8,128)(2,1)S(1)} %copy-done, f32[]{:T(128)} %bitcast.38), kind=kOutput, calls=%fused_computation.23 | convolution fusion | flops 67305472 | bytes 918528 | tf_op jit(solution)/shard_map/pad,pbd->pab/dot_general | solution.py:46
  96.7 2.1 %fusion.13 = f32[256,256]{1,0:T(8,128)S(1)} fusion(f32[256,256]{1,0:T(8,128)S(1)} %fusion.14, bf16[17,256,256]{2,1,0:T(8,128)(2,1)} %constant_dynamic-update-slice_fusion, s32[]{:T(128)} %bitcast.45, bf16[1,16,256,256]{3,2,1,0:T(8,128)(2,1)S(1)} %copy-done, f32[]{:T(128)} %bitcast.43), kind=kOutput, calls=%fused_computation.21 | convolution fusion | flops 67305472 | bytes 918528 | tf_op jit(solution)/shard_map/pad,pbd->pab/dot_general | solution.py:46
  98.8 2.0 %fusion.12 = f32[256,256]{1,0:T(8,128)S(1)} fusion(f32[256,256]{1,0:T(8,128)S(1)} %fusion.13, bf16[17,256,256]{2,1,0:T(8,128)(2,1)} %constant_dynamic-update-slice_fusion, s32[]{:T(128)} %bitcast.50, bf16[1,16,256,256]{3,2,1,0:T(8,128)(2,1)S(1)} %copy-done, f32[]{:T(128)} %bitcast.48), kind=kOutput, calls=%fused_computation.19 | convolution fusion | flops 67305472 | bytes 918528 | tf_op jit(solution)/shard_map/pad,pbd->pab/dot_general | solution.py:46
  100.8 2.1 %fusion.11 = f32[256,256]{1,0:T(8,128)S(1)} fusion(f32[256,256]{1,0:T(8,128)S(1)} %fusion.12, bf16[17,256,256]{2,1,0:T(8,128)(2,1)} %constant_dynamic-update-slice_fusion, s32[]{:T(128)} %bitcast.55, bf16[1,16,256,256]{3,2,1,0:T(8,128)(2,1)S(1)} %copy-done, f32[]{:T(128)} %bitcast.53), kind=kOutput, calls=%fused_computation.17 | convolution fusion | flops 67305472 | bytes 918528 | tf_op jit(solution)/shard_map/pad,pbd->pab/dot_general | solution.py:46
  102.9 2.1 %fusion.10 = f32[256,256]{1,0:T(8,128)S(1)} fusion(f32[256,256]{1,0:T(8,128)S(1)} %fusion.11, bf16[17,256,256]{2,1,0:T(8,128)(2,1)} %constant_dynamic-update-slice_fusion, s32[]{:T(128)} %bitcast.60, bf16[1,16,256,256]{3,2,1,0:T(8,128)(2,1)S(1)} %copy-done, f32[]{:T(128)} %bitcast.58), kind=kOutput, calls=%fused_computation.15 | convolution fusion | flops 67305472 | bytes 918528 | tf_op jit(solution)/shard_map/pad,pbd->pab/dot_general | solution.py:46
  104.9 2.0 %fusion.9 = f32[256,256]{1,0:T(8,128)S(1)} fusion(f32[256,256]{1,0:T(8,128)S(1)} %fusion.10, bf16[17,256,256]{2,1,0:T(8,128)(2,1)} %constant_dynamic-update-slice_fusion, s32[]{:T(128)} %bitcast.65, bf16[1,16,256,256]{3,2,1,0:T(8,128)(2,1)S(1)} %copy-done, f32[]{:T(128)} %bitcast.63), kind=kOutput, calls=%fused_computation.13 | convolution fusion | flops 67305472 | bytes 918528 | tf_op jit(solution)/shard_map/pad,pbd->pab/dot_general | solution.py:46
  107.0 1.9 %fusion.8 = f32[256,256]{1,0:T(8,128)S(1)} fusion(f32[256,256]{1,0:T(8,128)S(1)} %fusion.9, bf16[17,256,256]{2,1,0:T(8,128)(2,1)} %constant_dynamic-update-slice_fusion, s32[]{:T(128)} %bitcast.70, bf16[1,16,256,256]{3,2,1,0:T(8,128)(2,1)S(1)} %copy-done, f32[]{:T(128)} %bitcast.68), kind=kOutput, calls=%fused_computation.11 | convolution fusion | flops 67305472 | bytes 918528 | tf_op jit(solution)/shard_map/pad,pbd->pab/dot_general | solution.py:46
  108.9 2.0 %fusion.7 = f32[256,256]{1,0:T(8,128)S(1)} fusion(f32[256,256]{1,0:T(8,128)S(1)} %fusion.8, bf16[17,256,256]{2,1,0:T(8,128)(2,1)} %constant_dynamic-update-slice_fusion, s32[]{:T(128)} %bitcast.75, bf16[1,16,256,256]{3,2,1,0:T(8,128)(2,1)S(1)} %copy-done, f32[]{:T(128)} %bitcast.73), kind=kOutput, calls=%fused_computation.9 | convolution fusion | flops 67305472 | bytes 918528 | tf_op jit(solution)/shard_map/pad,pbd->pab/dot_general | solution.py:46
  111.0 2.8 %convert_subtract_fusion = (f32[1,256,256]{2,1,0:T(8,128)}, f32[1,256,256]{2,1,0:T(8,128)}) fusion(f32[256]{0:T(256)S(1)} %bitcast.197, f32[256,256]{1,0:T(8,128)S(1)} %fusion.7, bf16[1,16,256,256]{3,2,1,0:T(8,128)(2,1)S(1)} %copy-done, bf16[17,256,256]{2,1,0:T(8,128)(2,1)} %constant_dynamic-update-slice_fusion, s32[]{:T(128)} %bitcast.80, f32[]{:T(128)} %bitcast.78, ...), kind=kOutput, calls=%fused_computation.59 | convolution fusion | flops 67960832 | bytes 1315840 | tf_op jit(solution)/shard_map/pad,pbd->pab/dot_general | solution.py:46
  (49 shorter events, 13.6 us)
Async XLA Ops:
  2.3 44.9 %collective-permute-start = (bf16[1,256,256]{2,1,0:T(8,128)(2,1)S(1)}, bf16[1,256,256]{2,1,0:T(8,128)(2,1)S(1)}, u32[]{:S(2)}, u32[]{:S(2)}) collective-permute-start(bf16[1,256,256]{2,1,0:T(8,128)(2,1)S(1)} %and_select_fusion), channel_id=1, source_target_pairs={{0,8},{1,9},{2,10},{3,11},{4,12},{5,13},{6,14},{7,15},{8,16},{9,17... | collective-permute-start | bytes 393224 | tf_op jit(solution)/shard_map/ppermute | solution.py:12
  5.4 42.6 %collective-permute-start.1 = (bf16[1,256,256]{2,1,0:T(8,128)(2,1)S(1)}, bf16[1,256,256]{2,1,0:T(8,128)(2,1)S(1)}, u32[]{:S(2)}, u32[]{:S(2)}) collective-permute-start(bf16[1,256,256]{2,1,0:T(8,128)(2,1)S(1)} %and_select_fusion), channel_id=1, source_target_pairs={{0,7},{1,8},{2,9},{3,10},{4,11},{5,12},{6,13},{7,14},{8,15},{9,16}... | collective-permute-start | bytes 393224 | tf_op jit(solution)/shard_map/ppermute | solution.py:12
  7.0 43.4 %collective-permute-start.2 = (bf16[1,256,256]{2,1,0:T(8,128)(2,1)S(1)}, bf16[1,256,256]{2,1,0:T(8,128)(2,1)S(1)}, u32[]{:S(2)}, u32[]{:S(2)}) collective-permute-start(bf16[1,256,256]{2,1,0:T(8,128)(2,1)S(1)} %and_select_fusion), channel_id=1, source_target_pairs={{0,6},{1,7},{2,8},{3,9},{4,10},{5,11},{6,12},{7,13},{8,14},{9,15},... | collective-permute-start | bytes 393224 | tf_op jit(solution)/shard_map/ppermute | solution.py:12
  8.5 42.5 %collective-permute-start.3 = (bf16[1,256,256]{2,1,0:T(8,128)(2,1)S(1)}, bf16[1,256,256]{2,1,0:T(8,128)(2,1)S(1)}, u32[]{:S(2)}, u32[]{:S(2)}) collective-permute-start(bf16[1,256,256]{2,1,0:T(8,128)(2,1)S(1)} %and_select_fusion), channel_id=1, source_target_pairs={{0,5},{1,6},{2,7},{3,8},{4,9},{5,10},{6,11},{7,12},{8,13},{9,14},{... | collective-permute-start | bytes 393224 | tf_op jit(solution)/shard_map/ppermute | solution.py:12
  10.4 46.7 %collective-permute-start.4 = (bf16[1,256,256]{2,1,0:T(8,128)(2,1)S(1)}, bf16[1,256,256]{2,1,0:T(8,128)(2,1)S(1)}, u32[]{:S(2)}, u32[]{:S(2)}) collective-permute-start(bf16[1,256,256]{2,1,0:T(8,128)(2,1)S(1)} %and_select_fusion), channel_id=1, source_target_pairs={{0,4},{1,5},{2,6},{3,7},{4,8},{5,9},{6,10},{7,11},{8,12},{9,13},{1... | collective-permute-start | bytes 393224 | tf_op jit(solution)/shard_map/ppermute | solution.py:12
  11.9 3.5 %copy-start.4 = (s32[1,16]{1,0:T(1,128)S(1)}, s32[1,16]{1,0:T(1,128)}, u32[]{:S(2)}) copy-start(s32[1,16]{1,0:T(1,128)} %param.9) | copy-start | bytes 196
  11.9 4.2 %copy-start.2 = (f32[1,16]{1,0:T(1,128)S(1)}, f32[1,16]{1,0:T(1,128)}, u32[]{:S(2)}) copy-start(f32[1,16]{1,0:T(1,128)} %param.11) | copy-start | bytes 196
  15.3 47.5 %copy-start.1 = (bf16[1,256,256]{2,1,0:T(8,128)(2,1)S(1)}, bf16[1,256,256]{2,1,0:T(8,128)(2,1)}, u32[]{:S(2)}) copy-start(bf16[1,256,256]{2,1,0:T(8,128)(2,1)} %param.7) | copy-start | bytes 393220
  47.2 33.5 %copy-start = (bf16[1,16,256,256]{3,2,1,0:T(8,128)(2,1)S(1)}, bf16[1,16,256,256]{3,2,1,0:T(8,128)(2,1)}, u32[]{:S(2)}) copy-start(bf16[1,16,256,256]{3,2,1,0:T(8,128)(2,1)} %param.10) | copy-start | bytes 6291460
  47.2 10.8 %collective-permute-start.5 = (bf16[1,256,256]{2,1,0:T(8,128)(2,1)S(1)}, bf16[1,256,256]{2,1,0:T(8,128)(2,1)S(1)}, u32[]{:S(2)}, u32[]{:S(2)}) collective-permute-start(bf16[1,256,256]{2,1,0:T(8,128)(2,1)S(1)} %and_select_fusion), channel_id=1, source_target_pairs={{0,3},{1,4},{2,5},{3,6},{4,7},{5,8},{6,9},{7,10},{8,11},{9,12},{10... | collective-permute-start | bytes 393224 | tf_op jit(solution)/shard_map/ppermute | solution.py:12
  48.0 12.2 %collective-permute-start.6 = (bf16[1,256,256]{2,1,0:T(8,128)(2,1)S(1)}, bf16[1,256,256]{2,1,0:T(8,128)(2,1)S(1)}, u32[]{:S(2)}, u32[]{:S(2)}) collective-permute-start(bf16[1,256,256]{2,1,0:T(8,128)(2,1)S(1)} %and_select_fusion), channel_id=1, source_target_pairs={{0,2},{1,3},{2,4},{3,5},{4,6},{5,7},{6,8},{7,9},{8,10},{9,11},{10,... | collective-permute-start | bytes 393224 | tf_op jit(solution)/shard_map/ppermute | solution.py:12
  50.4 11.5 %collective-permute-start.7 = (bf16[1,256,256]{2,1,0:T(8,128)(2,1)S(1)}, bf16[1,256,256]{2,1,0:T(8,128)(2,1)S(1)}, u32[]{:S(2)}, u32[]{:S(2)}) collective-permute-start(bf16[1,256,256]{2,1,0:T(8,128)(2,1)S(1)} %and_select_fusion), channel_id=1, source_target_pairs={{0,1},{1,2},{2,3},{3,4},{4,5},{5,6},{6,7},{7,8},{8,9},{9,10},{10,1... | collective-permute-start | bytes 393224 | tf_op jit(solution)/shard_map/ppermute | solution.py:12
  51.1 12.5 %collective-permute-start.8 = (bf16[1,256,256]{2,1,0:T(8,128)(2,1)S(1)}, bf16[1,256,256]{2,1,0:T(8,128)(2,1)S(1)}, u32[]{:S(2)}, u32[]{:S(2)}) collective-permute-start(bf16[1,256,256]{2,1,0:T(8,128)(2,1)S(1)} %and_select_fusion), channel_id=1, source_target_pairs={{0,31},{1,0},{2,1},{3,2},{4,3},{5,4},{6,5},{7,6},{8,7},{9,8},{10,9... | collective-permute-start | bytes 393224 | tf_op jit(solution)/shard_map/ppermute | solution.py:12
  57.1 10.0 %collective-permute-start.9 = (bf16[1,256,256]{2,1,0:T(8,128)(2,1)S(1)}, bf16[1,256,256]{2,1,0:T(8,128)(2,1)S(1)}, u32[]{:S(2)}, u32[]{:S(2)}) collective-permute-start(bf16[1,256,256]{2,1,0:T(8,128)(2,1)S(1)} %and_select_fusion), channel_id=1, source_target_pairs={{0,30},{1,31},{2,0},{3,1},{4,2},{5,3},{6,4},{7,5},{8,6},{9,7},{10,... | collective-permute-start | bytes 393224 | tf_op jit(solution)/shard_map/ppermute | solution.py:12
  58.0 9.7 %collective-permute-start.10 = (bf16[1,256,256]{2,1,0:T(8,128)(2,1)S(1)}, bf16[1,256,256]{2,1,0:T(8,128)(2,1)S(1)}, u32[]{:S(2)}, u32[]{:S(2)}) collective-permute-start(bf16[1,256,256]{2,1,0:T(8,128)(2,1)S(1)} %and_select_fusion), channel_id=1, source_target_pairs={{0,29},{1,30},{2,31},{3,0},{4,1},{5,2},{6,3},{7,4},{8,5},{9,6},{10... | collective-permute-start | bytes 393224 | tf_op jit(solution)/shard_map/ppermute | solution.py:12
  60.1 9.7 %collective-permute-start.11 = (bf16[1,256,256]{2,1,0:T(8,128)(2,1)S(1)}, bf16[1,256,256]{2,1,0:T(8,128)(2,1)S(1)}, u32[]{:S(2)}, u32[]{:S(2)}) collective-permute-start(bf16[1,256,256]{2,1,0:T(8,128)(2,1)S(1)} %and_select_fusion), channel_id=1, source_target_pairs={{0,28},{1,29},{2,30},{3,31},{4,0},{5,1},{6,2},{7,3},{8,4},{9,5},{1... | collective-permute-start | bytes 393224 | tf_op jit(solution)/shard_map/ppermute | solution.py:12
  61.9 11.6 %collective-permute-start.12 = (bf16[1,256,256]{2,1,0:T(8,128)(2,1)S(1)}, bf16[1,256,256]{2,1,0:T(8,128)(2,1)S(1)}, u32[]{:S(2)}, u32[]{:S(2)}) collective-permute-start(bf16[1,256,256]{2,1,0:T(8,128)(2,1)S(1)} %and_select_fusion), channel_id=1, source_target_pairs={{0,27},{1,28},{2,29},{3,30},{4,31},{5,0},{6,1},{7,2},{8,3},{9,4},{... | collective-permute-start | bytes 393224 | tf_op jit(solution)/shard_map/ppermute | solution.py:12
  63.6 10.6 %collective-permute-start.13 = (bf16[1,256,256]{2,1,0:T(8,128)(2,1)S(1)}, bf16[1,256,256]{2,1,0:T(8,128)(2,1)S(1)}, u32[]{:S(2)}, u32[]{:S(2)}) collective-permute-start(bf16[1,256,256]{2,1,0:T(8,128)(2,1)S(1)} %and_select_fusion), channel_id=1, source_target_pairs={{0,26},{1,27},{2,28},{3,29},{4,30},{5,31},{6,0},{7,1},{8,2},{9,3},... | collective-permute-start | bytes 393224 | tf_op jit(solution)/shard_map/ppermute | solution.py:12
  67.1 9.2 %collective-permute-start.14 = (bf16[1,256,256]{2,1,0:T(8,128)(2,1)S(1)}, bf16[1,256,256]{2,1,0:T(8,128)(2,1)S(1)}, u32[]{:S(2)}, u32[]{:S(2)}) collective-permute-start(bf16[1,256,256]{2,1,0:T(8,128)(2,1)S(1)} %and_select_fusion), channel_id=1, source_target_pairs={{0,25},{1,26},{2,27},{3,28},{4,29},{5,30},{6,31},{7,0},{8,1},{9,2}... | collective-permute-start | bytes 393224 | tf_op jit(solution)/shard_map/ppermute | solution.py:12
  67.7 12.4 %collective-permute-start.15 = (bf16[1,256,256]{2,1,0:T(8,128)(2,1)S(1)}, bf16[1,256,256]{2,1,0:T(8,128)(2,1)S(1)}, u32[]{:S(2)}, u32[]{:S(2)}) collective-permute-start(bf16[1,256,256]{2,1,0:T(8,128)(2,1)S(1)} %and_select_fusion), channel_id=1, source_target_pairs={{0,24},{1,25},{2,26},{3,27},{4,28},{5,29},{6,30},{7,31},{8,0},{9,1... | collective-permute-start | bytes 393224 | tf_op jit(solution)/shard_map/ppermute | solution.py:12
  100.8 10.2 %copy-start.3 = (f32[1,256]{1,0:T(1,128)S(1)}, f32[1,256]{1,0:T(1,128)}, u32[]{:S(2)}) copy-start(f32[1,256]{1,0:T(1,128)} %param.12) | copy-start | bytes 3076
where the time goes:
time: 115 us; the launch traced here: 114 us
  matrix products  36.3 us (32%)
  between operations  31.9 us (28%)
  starting transfers between devices  23.9 us (21%)
  local copies, waits for them, and re-layouts  12 us (10%)
  waiting for transfers between devices  7.92 us (7%)
  other arithmetic  1.78 us (2%)
    dot_general x16, matrix products, shards(): jnp.einsum('pad,pbd->pab', half_product, intersection_now, preferred_elem...  32.9 us
    ppermute x16, starting transfers between devices, shifted(): return lax.ppermute(value, axis, pairs)  23.9 us
    unnamed x25, local copies, waits for them, and re-layouts  9.89 us
    ppermute x16, waiting for transfers between devices, shifted(): return lax.ppermute(value, axis, pairs)  7.92 us
    dot_general x1, matrix products, shards(): jnp.einsum('pqa,pqb->pab', factors[:, 0], factors[:, 1], preferred_elemen...  3.43 us
  transfers between devices with their start and end apart: 16, of which 4 were waited for; matrix products, arithmetic and copies ran while one was open for 14% of the time, Pallas kernels for 0%

commit v1 on v0

v1 whole, which is shorter than its diff:
```python
import functools

import jax
import jax.numpy as jnp
from jax import lax
from jax.experimental import pallas as pl
from jax.experimental.pallas import tpu as pltpu
from jax.sharding import PartitionSpec as P

WIN = 8
F32 = jnp.float32


def permuted(value, axis, target):
    count = lax.axis_size(axis)
    return lax.ppermute(value, axis, [(source, target(source)) for source in range(count)])


def swapped(value, axis, bits):
    return permuted(value, axis, lambda source: source ^ bits)


def shifted(value, axis, steps):
    count = lax.axis_size(axis)
    return permuted(value, axis, lambda source: (source + steps) % count)


def top_bit(number):
    return 1 << (number.bit_length() - 1)


def gathered(masked, axis):
    count = lax.axis_size(axis)
    me = lax.axis_index(axis)
    before = shifted(masked, axis, WIN)
    after = shifted(masked, axis, -WIN)
    own = {0: masked}
    for bits in range(2, WIN, 2):
        own[bits] = swapped(masked, axis, bits)
    before, after, own = lax.optimization_barrier((before, after, own))

    def side(bits):
        return jnp.where((me & top_bit(bits)) != 0, before, after)

    far = {bits: swapped(side(bits), axis, bits) for bits in range(2, WIN, 2)}
    for bits in range(1, WIN, 2):
        own[bits] = swapped(own[bits - 1], axis, 1)
    far[1] = swapped(side(1), axis, 1)
    for bits in range(3, WIN, 2):
        far[bits] = swapped(far[bits - 1], axis, 1)
    blocks = [(me ^ bits, own[bits]) for bits in range(WIN)]
    for bits in range(1, WIN):
        other = me ^ bits
        blocks.append((jnp.where(other > me, other - WIN, other + WIN), far[bits]))
    blocks.append((me - WIN, before))
    blocks.append((me + WIN, after))
    return [((source + count) % count, block) for source, block in blocks]


def coupled_kernel(count, slots, sources, neighbours, couplings, *refs):
    blocks, (inter, start, total) = refs[:count], refs[count:]
    sum_now = start[...]
    for position in range(count):
        slot, factor = jnp.int32(0), jnp.float32(0)
        for n in range(slots):
            hit = neighbours[0, n] == sources[position]
            slot = jnp.where(hit, n, slot)
            factor = jnp.where(hit, couplings[0, n], factor)
        inter_now = inter[slot]
        half = jnp.dot(inter_now, blocks[position][...], preferred_element_type=F32).astype(jnp.bfloat16)
        projected = lax.dot_general(
            half, inter_now, (((1,), (1,)), ((), ())), preferred_element_type=F32
        )
        sum_now = sum_now + factor * projected
    total[...] = sum_now


def coupled(blocks, neighbours, couplings, intersections, start):
    count, slots = len(blocks), neighbours.shape[1]
    sources = jnp.stack([source for source, _ in blocks]).astype(jnp.int32)
    arrays = [block[0] for _, block in blocks]
    vmem = pl.BlockSpec(memory_space=pltpu.VMEM)
    smem = pl.BlockSpec(memory_space=pltpu.SMEM)
    width = start.shape[0]
    return pl.pallas_call(
        functools.partial(coupled_kernel, count, slots),
        out_shape=jax.ShapeDtypeStruct(start.shape, F32),
        in_specs=[smem] * 3 + [vmem] * (count + 2),
        out_specs=vmem,
        compiler_params=pltpu.CompilerParams(vmem_limit_bytes=24 << 20),
        cost_estimate=pl.CostEstimate(
            flops=4 * count * width**3, bytes_accessed=2 * (slots + count) * width**2, transcendentals=0
        ),
    )(sources, neighbours, couplings, *arrays, intersections[0], start)


def shards(amplitudes, ranks, neighbours, intersections, couplings, energies, factors):
    pno_width = amplitudes.shape[1]
    aux_count = lax.axis_size("aux")
    row_span = pno_width // aux_count
    first_row = lax.axis_index("aux") * row_span
    positions = jnp.arange(pno_width)
    live_rows = positions[None, :] < ranks[:, None]
    square_mask = live_rows[:, :, None] & live_rows[:, None, :]
    masked = jnp.where(square_mask, amplitudes, jnp.zeros((), jnp.bfloat16))
    blocks = gathered(masked, "pair")
    exchange = jnp.einsum("qa,qb->ab", factors[0, 0], factors[0, 1], preferred_element_type=F32)
    partial_sum = coupled(blocks, neighbours, couplings, intersections, exchange)[None]
    summed = lax.psum_scatter(partial_sum, "aux", scatter_dimension=1, tiled=True)
    row_energy = lax.dynamic_slice_in_dim(energies, first_row, row_span, 1)
    denominator = row_energy[:, :, None] + energies[:, None, :]
    row_amp = lax.dynamic_slice_in_dim(masked, first_row, row_span, 1).astype(F32)
    row_mask = lax.dynamic_slice_in_dim(square_mask, first_row, row_span, 1)
    residual = jnp.where(row_mask, summed + denominator * row_amp, jnp.zeros((), F32))
    return (residual, row_amp - residual / denominator)


def solution(mesh):
    return jax.shard_map(
        shards,
        mesh=mesh,
        in_specs=(
            P("pair", None, None),
            P("pair"),
            P("pair", "aux"),
            P("pair", "aux", None, None),
            P("pair", "aux"),
            P("pair", None),
            P("pair", None, "aux", None),
        ),
        out_specs=(P("pair", "aux", None), P("pair", "aux", None)),
        check_vma=False,
    )
```

time: 115 us -> 38.8 us (0.34)
  matrix products: 36.3 us -> 3.4 us
  between operations: 31.9 us -> 1.77 us
  local copies, waits for them, and re-layouts: 12 us -> 0.12 us
  starting transfers between devices: 23.9 us -> 13.2 us
  waiting for transfers between devices: 7.92 us -> 13.9 us
  Pallas kernels: 0 us -> 2.76 us
  other arithmetic: 1.78 us -> 3.41 us
    dot_general x17 -> x1, matrix products: 36.3 us -> 3.4 us  [shards(): jnp.einsum('qa,qb->ab', factors[0, 0], factors[0, 1], preferred_element_t...]
    ppermute x16, starting transfers between devices: 23.9 us -> 13.2 us  [permuted(): lax.ppermute(value, axis, [(source, target(source)) for source in range(c...]
    unnamed x25 -> x8, local copies, waits for them, and re-layouts: 9.89 us -> 0.03 us
    ppermute x16, waiting for transfers between devices: 7.92 us -> 13.9 us  [permuted(): lax.ppermute(value, axis, [(source, target(source)) for source in range(c...]
    pallas_call x0 -> x1, Pallas kernels: none -> 2.76 us  [coupled(): pl.pallas_call(functools.partial(coupled_kernel, count, slots), out_shape...]
    sub x0 -> x1, other arithmetic: none -> 1.72 us  [shards(): return (residual, row_amp - residual / denominator)]
    slice x2 -> x0, local copies, waits for them, and re-layouts: 1.43 us -> none  [the longest x1 0.72 us: shards(): picked = extended[nearby[:, column]]]
  transfers between devices with their start and end apart: 16 -> 16, of which waited for: 4 -> 7; matrix products, arithmetic and copies ran while one was open for 14% -> 11% of each run, Pallas kernels for 0% -> 0%
where the time goes in v1:
time: 38.8 us; the launch traced here: 38.6 us
  waiting for transfers between devices  13.9 us (36%)
  starting transfers between devices  13.2 us (34%)
  other arithmetic  3.41 us (9%)
  matrix products  3.4 us (9%)
  Pallas kernels  2.76 us (7%)
  between operations  1.77 us (5%)
    ppermute x16, waiting for transfers between devices, permuted(): lax.ppermute(value, axis, [(source, target(source)) for source in range(c...  13.9 us
    ppermute x16, starting transfers between devices, permuted(): lax.ppermute(value, axis, [(source, target(source)) for source in range(c...  13.2 us
    dot_general x1, matrix products, shards(): jnp.einsum('qa,qb->ab', factors[0, 0], factors[0, 1], preferred_element_t...  3.4 us
    pallas_call x1, Pallas kernels, coupled(): pl.pallas_call(functools.partial(coupled_kernel, count, slots), out_shape...  2.76 us
    sub x1, other arithmetic, shards(): return (residual, row_amp - residual / denominator)  1.72 us
    select_n x1, other arithmetic, shards(): masked = jnp.where(square_mask, amplitudes, jnp.zeros((), jnp.bfloat16))  1.01 us
  transfers between devices with their start and end apart: 16, of which 7 were waited for; matrix products, arithmetic and copies ran while one was open for 11% of the time, Pallas kernels for 0%

profile of v1, /device:TPU:0, one launch (start us, length us, event | category | flops | bytes accessed | tf_op | source)
XLA Modules:
  0.0 38.6 jit_solution(9551419433239561334)
XLA Ops:
  1.3 1.0 %and_select_fusion.1 = bf16[1,256,256]{2,1,0:T(8,128)(2,1)S(1)} fusion(bf16[1,256,256]{2,1,0:T(8,128)(2,1)} %param.7, pred[256]{0:T(512)(128)(4,1)S(1)} %iota_compare_fusion), kind=kLoop, calls=%fused_computation.8 | loop fusion | flops 131072 | bytes 262400 | tf_op jit(solution)/shard_map/jit(_where)/select_n | solution.py:105
  2.3 4.0 %collective-permute-start.4 = (bf16[1,256,256]{2,1,0:T(8,128)(2,1)S(1)}, bf16[1,256,256]{2,1,0:T(8,128)(2,1)S(1)}, u32[]{:S(2)}, u32[]{:S(2)}) collective-permute-start(bf16[1,256,256]{2,1,0:T(8,128)(2,1)S(1)} %and_select_fusion.1), channel_id=1, source_target_pairs={{0,6},{1,7},{2,4},{3,5},{4,2},{5,3},{6,0},{7,1},{8,14},{9,15},{10,... | collective-permute-start | bytes 393224 | tf_op jit(solution)/shard_map/ppermute | solution.py:16
  6.3 0.5 %collective-permute-start.3 = (bf16[1,256,256]{2,1,0:T(8,128)(2,1)S(1)}, bf16[1,256,256]{2,1,0:T(8,128)(2,1)S(1)}, u32[]{:S(2)}, u32[]{:S(2)}) collective-permute-start(bf16[1,256,256]{2,1,0:T(8,128)(2,1)S(1)} %and_select_fusion.1), channel_id=1, source_target_pairs={{0,4},{1,5},{2,6},{3,7},{4,0},{5,1},{6,2},{7,3},{8,12},{9,13},{10,... | collective-permute-start | bytes 393224 | tf_op jit(solution)/shard_map/ppermute | solution.py:16
  6.8 0.1 collective-permute-start.2
  6.9 4.0 %collective-permute-start.1 = (bf16[1,256,256]{2,1,0:T(8,128)(2,1)S(1)}, bf16[1,256,256]{2,1,0:T(8,128)(2,1)S(1)}, u32[]{:S(2)}, u32[]{:S(2)}) collective-permute-start(bf16[1,256,256]{2,1,0:T(8,128)(2,1)S(1)} %and_select_fusion.1), channel_id=1, source_target_pairs={{0,24},{1,25},{2,26},{3,27},{4,28},{5,29},{6,30},{7,31},{8,0},{9,1... | collective-permute-start | bytes 393224 | tf_op jit(solution)/shard_map/ppermute | solution.py:16
  10.9 0.0 collective-permute-start
  10.9 0.0 collective-permute-done.4
  10.9 1.7 %collective-permute-done.3 = bf16[1,256,256]{2,1,0:T(8,128)(2,1)S(1)} collective-permute-done((bf16[1,256,256]{2,1,0:T(8,128)(2,1)S(1)}, bf16[1,256,256]{2,1,0:T(8,128)(2,1)S(1)}, u32[]{:S(2)}, u32[]{:S(2)}) %collective-permute-start.3) | collective-permute-done | bytes 131104 | tf_op jit(solution)/shard_map/ppermute | solution.py:16
  12.6 0.2 collective-permute-done.2
  12.8 1.4 %collective-permute-done.1 = bf16[1,256,256]{2,1,0:T(8,128)(2,1)S(1)} collective-permute-done((bf16[1,256,256]{2,1,0:T(8,128)(2,1)S(1)}, bf16[1,256,256]{2,1,0:T(8,128)(2,1)S(1)}, u32[]{:S(2)}, u32[]{:S(2)}) %collective-permute-start.1) | collective-permute-done | bytes 131104 | tf_op jit(solution)/shard_map/ppermute | solution.py:16
  14.2 3.4 %collective-permute-done = bf16[1,256,256]{2,1,0:T(8,128)(2,1)S(1)} collective-permute-done((bf16[1,256,256]{2,1,0:T(8,128)(2,1)S(1)}, bf16[1,256,256]{2,1,0:T(8,128)(2,1)S(1)}, u32[]{:S(2)}, u32[]{:S(2)}) %collective-permute-start) | collective-permute-done | bytes 131104 | tf_op jit(solution)/shard_map/ppermute | solution.py:16
  17.7 0.0 collective-permute-start.5
  17.7 0.5 %collective-permute-start.6 = (bf16[1,256,256]{2,1,0:T(8,128)(2,1)S(1)}, bf16[1,256,256]{2,1,0:T(8,128)(2,1)S(1)}, u32[]{:S(2)}, u32[]{:S(2)}) collective-permute-start(bf16[1,256,256]{2,1,0:T(8,128)(2,1)S(1)} %collective-permute-done.2), channel_id=1, source_target_pairs={{0,1},{1,0},{2,3},{3,2},{4,5},{5,4},{6,7},{7,6},{8,9},{9,8},{10,11... | collective-permute-start | bytes 393224 | tf_op jit(solution)/shard_map/ppermute | solution.py:16
  18.2 0.0 collective-permute-start.7
  18.2 0.7 %broadcast_select_fusion = (bf16[1,256,256]{2,1,0:T(8,128)(2,1)S(1)}, bf16[1,256,256]{2,1,0:T(8,128)(2,1)S(1)}, bf16[1,256,256]{2,1,0:T(8,128)(2,1)}) fusion(bf16[1,256,256]{2,1,0:T(8,128)(2,1)S(1)} %collective-permute-done, bf16[1,256,256]{2,1,0:T(8,128)(2,1)S(1)} %collective-permute-done.1, pred[]{:T(512)S(6)} %ne.99, pred[]{:T(512)S(6)} %ne.98, pred[]{:T(512)S(6)} %ne.97), kind=kLoop, calls=%fused_computation.11 | loop fusion | flops 196608 | bytes 655363 | tf_op jit(solution)/shard_map/jit(_where)/select_n | solution.py:43
  18.9 1.5 %collective-permute-start.10 = (bf16[1,256,256]{2,1,0:T(8,128)(2,1)S(1)}, bf16[1,256,256]{2,1,0:T(8,128)(2,1)}, u32[]{:S(2)}, u32[]{:S(2)}) collective-permute-start(bf16[1,256,256]{2,1,0:T(8,128)(2,1)S(1)} %get-tuple-element.17), channel_id=1, source_target_pairs={{0,2},{1,3},{2,0},{3,1},{4,6},{5,7},{6,4},{7,5},{8,10},{9,11},{10,... | collective-permute-start | bytes 393224 | tf_op jit(solution)/shard_map/ppermute | solution.py:16
  20.4 1.5 %collective-permute-start.14 = (bf16[1,256,256]{2,1,0:T(8,128)(2,1)S(1)}, bf16[1,256,256]{2,1,0:T(8,128)(2,1)}, u32[]{:S(2)}, u32[]{:S(2)}) collective-permute-start(bf16[1,256,256]{2,1,0:T(8,128)(2,1)S(1)} %get-tuple-element.16), channel_id=1, source_target_pairs={{0,6},{1,7},{2,4},{3,5},{4,2},{5,3},{6,0},{7,1},{8,14},{9,15},{10,... | collective-permute-start | bytes 393224 | tf_op jit(solution)/shard_map/ppermute | solution.py:16
  21.9 0.0 collective-permute-done.5
  21.9 0.5 %collective-permute-start.12 = (bf16[1,256,256]{2,1,0:T(8,128)(2,1)S(1)}, bf16[1,256,256]{2,1,0:T(8,128)(2,1)}, u32[]{:S(2)}, u32[]{:S(2)}) collective-permute-start(bf16[1,256,256]{2,1,0:T(8,128)(2,1)S(1)} %get-tuple-element.16), channel_id=1, source_target_pairs={{0,4},{1,5},{2,6},{3,7},{4,0},{5,1},{6,2},{7,3},{8,12},{9,13},{10,... | collective-permute-start | bytes 393224 | tf_op jit(solution)/shard_map/ppermute | solution.py:16
  22.4 0.0 copy-start
  22.4 0.0 copy-start.1
  22.4 0.0 copy-start.2
  22.4 0.5 %collective-permute-start.9 = (bf16[1,256,256]{2,1,0:T(8,128)(2,1)}, bf16[1,256,256]{2,1,0:T(8,128)(2,1)}, u32[]{:S(2)}, u32[]{:S(2)}) collective-permute-start(bf16[1,256,256]{2,1,0:T(8,128)(2,1)} %get-tuple-element.18), channel_id=1, source_target_pairs={{0,1},{1,0},{2,3},{3,2},{4,5},{5,4},{6,7},{7,6},{8,9},{9,8},{10,11... | collective-permute-start | bytes 393224 | tf_op jit(solution)/shard_map/ppermute | solution.py:16
  23.0 2.3 %collective-permute-done.10 = bf16[1,256,256]{2,1,0:T(8,128)(2,1)} collective-permute-done((bf16[1,256,256]{2,1,0:T(8,128)(2,1)S(1)}, bf16[1,256,256]{2,1,0:T(8,128)(2,1)}, u32[]{:S(2)}, u32[]{:S(2)}) %collective-permute-start.10) | collective-permute-done | bytes 131104 | tf_op jit(solution)/shard_map/ppermute | solution.py:16
  25.3 0.0 collective-permute-start.11
  25.3 3.5 %collective-permute-done.14 = bf16[1,256,256]{2,1,0:T(8,128)(2,1)} collective-permute-done((bf16[1,256,256]{2,1,0:T(8,128)(2,1)S(1)}, bf16[1,256,256]{2,1,0:T(8,128)(2,1)}, u32[]{:S(2)}, u32[]{:S(2)}) %collective-permute-start.14) | collective-permute-done | bytes 131104 | tf_op jit(solution)/shard_map/ppermute | solution.py:16
  28.8 1.4 %collective-permute-done.12 = bf16[1,256,256]{2,1,0:T(8,128)(2,1)} collective-permute-done((bf16[1,256,256]{2,1,0:T(8,128)(2,1)S(1)}, bf16[1,256,256]{2,1,0:T(8,128)(2,1)}, u32[]{:S(2)}, u32[]{:S(2)}) %collective-permute-start.12) | collective-permute-done | bytes 131104 | tf_op jit(solution)/shard_map/ppermute | solution.py:16
  30.1 3.4 %fusion.refs_18_ = f32[256,256]{1,0:T(8,128)S(1)} fusion(bf16[1,2,5120,256]{3,2,1,0:T(8,128)(2,1)} %param.13), kind=kOutput, calls=%fused_computation | convolution fusion | flops 671088640 | bytes 5505024 | tf_op jit(solution)/shard_map/qa,qb->ab/dot_general | solution.py:107
  33.9 0.1 stack.71.sources
  34.0 0.0 copy-start.3
  34.1 2.8 %shard_map.89 = f32[256,256]{1,0:T(8,128)S(1)} custom-call(s32[17]{0:T(128)S(1)} %stack.71.sources, s32[1,16]{1,0:T(1,128)S(1)} %copy-done.1, f32[1,16]{1,0:T(1,128)S(1)} %copy-done.2, bf16[256,256]{1,0:T(8,128)(2,1)S(1)} %bitcast.48, bf16[256,256]{1,0:T(8,128)(2,1)S(1)} %bitcast.54, bf16[256,256]{1,0:T(8,128)(2,1)S(1)} %bitcast.53, ...), custom_call_target="tpu_custom_call" | custom-call | flops 1140850688 | bytes 4325376 | tf_op jit(solution)/shard_map/pallas_call | solution.py:85
  36.9 1.7 %convert_subtract_fusion = (f32[1,256,256]{2,1,0:T(8,128)}, f32[1,256,256]{2,1,0:T(8,128)}) fusion(f32[256]{0:T(256)} %bitcast.57, f32[256,256]{1,0:T(8,128)S(1)} %shard_map.89, pred[256]{0:T(512)(128)(4,1)S(1)} %iota_compare_fusion, bf16[1,256,256]{2,1,0:T(8,128)(2,1)S(1)} %copy-done.3), kind=kLoop, calls=%fused_computation.9 | loop fusion | flops 589824 | bytes 918784 | tf_op jit(solution)/shard_map/sub | solution.py:115
  (15 shorter events, 0.0 us)
Async XLA Ops:
  2.3 8.6 %collective-permute-start.4 = (bf16[1,256,256]{2,1,0:T(8,128)(2,1)S(1)}, bf16[1,256,256]{2,1,0:T(8,128)(2,1)S(1)}, u32[]{:S(2)}, u32[]{:S(2)}) collective-permute-start(bf16[1,256,256]{2,1,0:T(8,128)(2,1)S(1)} %and_select_fusion.1), channel_id=1, source_target_pairs={{0,6},{1,7},{2,4},{3,5},{4,2},{5,3},{6,0},{7,1},{8,14},{9,15},{10,... | collective-permute-start | bytes 393224 | tf_op jit(solution)/shard_map/ppermute | solution.py:16
  6.3 6.3 %collective-permute-start.3 = (bf16[1,256,256]{2,1,0:T(8,128)(2,1)S(1)}, bf16[1,256,256]{2,1,0:T(8,128)(2,1)S(1)}, u32[]{:S(2)}, u32[]{:S(2)}) collective-permute-start(bf16[1,256,256]{2,1,0:T(8,128)(2,1)S(1)} %and_select_fusion.1), channel_id=1, source_target_pairs={{0,4},{1,5},{2,6},{3,7},{4,0},{5,1},{6,2},{7,3},{8,12},{9,13},{10,... | collective-permute-start | bytes 393224 | tf_op jit(solution)/shard_map/ppermute | solution.py:16
  6.8 6.0 %collective-permute-start.2 = (bf16[1,256,256]{2,1,0:T(8,128)(2,1)S(1)}, bf16[1,256,256]{2,1,0:T(8,128)(2,1)S(1)}, u32[]{:S(2)}, u32[]{:S(2)}) collective-permute-start(bf16[1,256,256]{2,1,0:T(8,128)(2,1)S(1)} %and_select_fusion.1), channel_id=1, source_target_pairs={{0,2},{1,3},{2,0},{3,1},{4,6},{5,7},{6,4},{7,5},{8,10},{9,11},{10,... | collective-permute-start | bytes 393224 | tf_op jit(solution)/shard_map/ppermute | solution.py:16
  6.9 7.3 %collective-permute-start.1 = (bf16[1,256,256]{2,1,0:T(8,128)(2,1)S(1)}, bf16[1,256,256]{2,1,0:T(8,128)(2,1)S(1)}, u32[]{:S(2)}, u32[]{:S(2)}) collective-permute-start(bf16[1,256,256]{2,1,0:T(8,128)(2,1)S(1)} %and_select_fusion.1), channel_id=1, source_target_pairs={{0,24},{1,25},{2,26},{3,27},{4,28},{5,29},{6,30},{7,31},{8,0},{9,1... | collective-permute-start | bytes 393224 | tf_op jit(solution)/shard_map/ppermute | solution.py:16
  10.9 6.8 %collective-permute-start = (bf16[1,256,256]{2,1,0:T(8,128)(2,1)S(1)}, bf16[1,256,256]{2,1,0:T(8,128)(2,1)S(1)}, u32[]{:S(2)}, u32[]{:S(2)}) collective-permute-start(bf16[1,256,256]{2,1,0:T(8,128)(2,1)S(1)} %and_select_fusion.1), channel_id=1, source_target_pairs={{0,8},{1,9},{2,10},{3,11},{4,12},{5,13},{6,14},{7,15},{8,16},{9,17... | collective-permute-start | bytes 393224 | tf_op jit(solution)/shard_map/ppermute | solution.py:16
  17.7 4.2 %collective-permute-start.5 = (bf16[1,256,256]{2,1,0:T(8,128)(2,1)S(1)}, bf16[1,256,256]{2,1,0:T(8,128)(2,1)S(1)}, u32[]{:S(2)}, u32[]{:S(2)}) collective-permute-start(bf16[1,256,256]{2,1,0:T(8,128)(2,1)S(1)} %and_select_fusion.1), channel_id=1, source_target_pairs={{0,1},{1,0},{2,3},{3,2},{4,5},{5,4},{6,7},{7,6},{8,9},{9,8},{10,11... | collective-permute-start | bytes 393224 | tf_op jit(solution)/shard_map/ppermute | solution.py:16
  17.7 4.7 %collective-permute-start.6 = (bf16[1,256,256]{2,1,0:T(8,128)(2,1)S(1)}, bf16[1,256,256]{2,1,0:T(8,128)(2,1)S(1)}, u32[]{:S(2)}, u32[]{:S(2)}) collective-permute-start(bf16[1,256,256]{2,1,0:T(8,128)(2,1)S(1)} %collective-permute-done.2), channel_id=1, source_target_pairs={{0,1},{1,0},{2,3},{3,2},{4,5},{5,4},{6,7},{7,6},{8,9},{9,8},{10,11... | collective-permute-start | bytes 393224 | tf_op jit(solution)/shard_map/ppermute | solution.py:16
  18.2 4.2 %collective-permute-start.7 = (bf16[1,256,256]{2,1,0:T(8,128)(2,1)S(1)}, bf16[1,256,256]{2,1,0:T(8,128)(2,1)S(1)}, u32[]{:S(2)}, u32[]{:S(2)}) collective-permute-start(bf16[1,256,256]{2,1,0:T(8,128)(2,1)S(1)} %collective-permute-done.3), channel_id=1, source_target_pairs={{0,1},{1,0},{2,3},{3,2},{4,5},{5,4},{6,7},{7,6},{8,9},{9,8},{10,11... | collective-permute-start | bytes 393224 | tf_op jit(solution)/shard_map/ppermute | solution.py:16
  18.9 6.4 %collective-permute-start.10 = (bf16[1,256,256]{2,1,0:T(8,128)(2,1)S(1)}, bf16[1,256,256]{2,1,0:T(8,128)(2,1)}, u32[]{:S(2)}, u32[]{:S(2)}) collective-permute-start(bf16[1,256,256]{2,1,0:T(8,128)(2,1)S(1)} %get-tuple-element.17), channel_id=1, source_target_pairs={{0,2},{1,3},{2,0},{3,1},{4,6},{5,7},{6,4},{7,5},{8,10},{9,11},{10,... | collective-permute-start | bytes 393224 | tf_op jit(solution)/shard_map/ppermute | solution.py:16
  20.4 8.4 %collective-permute-start.14 = (bf16[1,256,256]{2,1,0:T(8,128)(2,1)S(1)}, bf16[1,256,256]{2,1,0:T(8,128)(2,1)}, u32[]{:S(2)}, u32[]{:S(2)}) collective-permute-start(bf16[1,256,256]{2,1,0:T(8,128)(2,1)S(1)} %get-tuple-element.16), channel_id=1, source_target_pairs={{0,6},{1,7},{2,4},{3,5},{4,2},{5,3},{6,0},{7,1},{8,14},{9,15},{10,... | collective-permute-start | bytes 393224 | tf_op jit(solution)/shard_map/ppermute | solution.py:16
  21.9 8.3 %collective-permute-start.12 = (bf16[1,256,256]{2,1,0:T(8,128)(2,1)S(1)}, bf16[1,256,256]{2,1,0:T(8,128)(2,1)}, u32[]{:S(2)}, u32[]{:S(2)}) collective-permute-start(bf16[1,256,256]{2,1,0:T(8,128)(2,1)S(1)} %get-tuple-element.16), channel_id=1, source_target_pairs={{0,4},{1,5},{2,6},{3,7},{4,0},{5,1},{6,2},{7,3},{8,12},{9,13},{10,... | collective-permute-start | bytes 393224 | tf_op jit(solution)/shard_map/ppermute | solution.py:16
  22.4 11.6 %collective-permute-start.8 = (bf16[1,256,256]{2,1,0:T(8,128)(2,1)S(1)}, bf16[1,256,256]{2,1,0:T(8,128)(2,1)}, u32[]{:S(2)}, u32[]{:S(2)}) collective-permute-start(bf16[1,256,256]{2,1,0:T(8,128)(2,1)S(1)} %collective-permute-done.4), channel_id=1, source_target_pairs={{0,1},{1,0},{2,3},{3,2},{4,5},{5,4},{6,7},{7,6},{8,9},{9,8},{10,11... | collective-permute-start | bytes 393224 | tf_op jit(solution)/shard_map/ppermute | solution.py:16
  22.4 11.7 %copy-start = (bf16[1,16,256,256]{3,2,1,0:T(8,128)(2,1)S(1)}, bf16[1,16,256,256]{3,2,1,0:T(8,128)(2,1)}, u32[]{:S(2)}) copy-start(bf16[1,16,256,256]{3,2,1,0:T(8,128)(2,1)} %param.10) | copy-start | bytes 6291460
  22.4 11.7 %copy-start.1 = (s32[1,16]{1,0:T(1,128)S(1)}, s32[1,16]{1,0:T(1,128)}, u32[]{:S(2)}) copy-start(s32[1,16]{1,0:T(1,128)} %neighbours.1) | copy-start | bytes 196
  22.4 11.7 %copy-start.2 = (f32[1,16]{1,0:T(1,128)S(1)}, f32[1,16]{1,0:T(1,128)}, u32[]{:S(2)}) copy-start(f32[1,16]{1,0:T(1,128)} %couplings.1) | copy-start | bytes 196
  22.4 11.6 %collective-permute-start.9 = (bf16[1,256,256]{2,1,0:T(8,128)(2,1)}, bf16[1,256,256]{2,1,0:T(8,128)(2,1)}, u32[]{:S(2)}, u32[]{:S(2)}) collective-permute-start(bf16[1,256,256]{2,1,0:T(8,128)(2,1)} %get-tuple-element.18), channel_id=1, source_target_pairs={{0,1},{1,0},{2,3},{3,2},{4,5},{5,4},{6,7},{7,6},{8,9},{9,8},{10,11... | collective-permute-start | bytes 393224 | tf_op jit(solution)/shard_map/ppermute | solution.py:16
  25.3 8.7 %collective-permute-start.11 = (bf16[1,256,256]{2,1,0:T(8,128)(2,1)}, bf16[1,256,256]{2,1,0:T(8,128)(2,1)}, u32[]{:S(2)}, u32[]{:S(2)}) collective-permute-start(bf16[1,256,256]{2,1,0:T(8,128)(2,1)} %collective-permute-done.10), channel_id=1, source_target_pairs={{0,1},{1,0},{2,3},{3,2},{4,5},{5,4},{6,7},{7,6},{8,9},{9,8},{10,11... | collective-permute-start | bytes 393224 | tf_op jit(solution)/shard_map/ppermute | solution.py:16
  28.8 5.3 %collective-permute-start.15 = (bf16[1,256,256]{2,1,0:T(8,128)(2,1)}, bf16[1,256,256]{2,1,0:T(8,128)(2,1)}, u32[]{:S(2)}, u32[]{:S(2)}) collective-permute-start(bf16[1,256,256]{2,1,0:T(8,128)(2,1)} %collective-permute-done.14), channel_id=1, source_target_pairs={{0,1},{1,0},{2,3},{3,2},{4,5},{5,4},{6,7},{7,6},{8,9},{9,8},{10,11... | collective-permute-start | bytes 393224 | tf_op jit(solution)/shard_map/ppermute | solution.py:16
  30.1 3.9 %collective-permute-start.13 = (bf16[1,256,256]{2,1,0:T(8,128)(2,1)}, bf16[1,256,256]{2,1,0:T(8,128)(2,1)}, u32[]{:S(2)}, u32[]{:S(2)}) collective-permute-start(bf16[1,256,256]{2,1,0:T(8,128)(2,1)} %collective-permute-done.12), channel_id=1, source_target_pairs={{0,1},{1,0},{2,3},{3,2},{4,5},{5,4},{6,7},{7,6},{8,9},{9,8},{10,11... | collective-permute-start | bytes 393224 | tf_op jit(solution)/shard_map/ppermute | solution.py:16
  34.0 2.9 %copy-start.3 = (bf16[1,256,256]{2,1,0:T(8,128)(2,1)S(1)}, bf16[1,256,256]{2,1,0:T(8,128)(2,1)}, u32[]{:S(2)}) copy-start(bf16[1,256,256]{2,1,0:T(8,128)(2,1)} %param.7) | copy-start | bytes 393220

commit v2 on v1

v2 whole, which is shorter than its diff:
```python
import functools

import jax
import jax.numpy as jnp
from jax import lax
from jax.experimental import pallas as pl
from jax.experimental.pallas import tpu as pltpu
from jax.sharding import PartitionSpec as P

WIN = 8
F32 = jnp.float32
BF16 = jnp.bfloat16
VMEM = pl.BlockSpec(memory_space=pltpu.VMEM)
SMEM = pl.BlockSpec(memory_space=pltpu.SMEM)


def permuted(value, axis, target):
    count = lax.axis_size(axis)
    return lax.ppermute(value, axis, [(source, target(source)) for source in range(count)])


def swapped(value, axis, bits):
    return permuted(value, axis, lambda source: source ^ bits)


def shifted(value, axis, steps):
    count = lax.axis_size(axis)
    return permuted(value, axis, lambda source: (source + steps) % count)


def top_bit(number):
    return 1 << (number.bit_length() - 1)


def held(*arrays):
    return [pltpu.with_memory_space_constraint(array, pltpu.VMEM) for array in arrays]


def live_square(rank, shape):
    rows = lax.broadcasted_iota(jnp.int32, shape, 0)
    columns = lax.broadcasted_iota(jnp.int32, shape, 1)
    return jnp.maximum(rows, columns) < rank


def mask_kernel(rank, amplitude, masked):
    square = live_square(rank[0], amplitude.shape)
    masked[...] = jnp.where(square, amplitude[...].astype(F32), 0.0).astype(BF16)


def mask(ranks, amplitude):
    return pl.pallas_call(
        mask_kernel,
        out_shape=jax.ShapeDtypeStruct(amplitude.shape, BF16),
        in_specs=[SMEM, VMEM],
        out_specs=VMEM,
    )(ranks, amplitude)


def coupled_sum(sources, neighbours, couplings, inter, blocks, sum_now):
    for position, block in enumerate(blocks):
        slot, factor = jnp.int32(0), jnp.float32(0)
        for n in range(neighbours.shape[1]):
            hit = neighbours[0, n] == sources[position]
            slot = jnp.where(hit, n, slot)
            factor = jnp.where(hit, couplings[0, n], factor)
        inter_now = inter[slot]
        half = jnp.dot(inter_now, block[...], preferred_element_type=F32).astype(BF16)
        projected = lax.dot_general(
            half, inter_now, (((1,), (1,)), ((), ())), preferred_element_type=F32
        )
        sum_now = sum_now + factor * projected
    return sum_now


def coupled_kernel(count, sources, neighbours, couplings, *refs):
    blocks, (inter, start, total) = refs[:count], refs[count:]
    total[...] = coupled_sum(sources, neighbours, couplings, inter, blocks, start[...])


def last_kernel(count, sources, neighbours, couplings, *refs):
    blocks, (inter, start, rank, energy, masked, residual, updated) = refs[:count], refs[count:]
    total = coupled_sum(sources, neighbours, couplings, inter, blocks, start[...])
    along = jnp.broadcast_to(energy[...], total.shape)
    denominator = along + along.T
    own = masked[...].astype(F32)
    square = live_square(rank[0], total.shape)
    residual_now = jnp.where(square, total + denominator * own, 0.0)
    residual[...] = residual_now
    updated[...] = own - residual_now / denominator


def coupled(blocks, neighbours, couplings, inter, start, ending=None):
    count, slots, width = len(blocks), neighbours.shape[1], start.shape[0]
    sources = jnp.stack([source for source, _ in blocks]).astype(jnp.int32)
    arrays = held(*[block for _, block in blocks], inter, start)
    shape = jax.ShapeDtypeStruct(start.shape, F32)
    cost = pl.CostEstimate(
        flops=4 * count * width**3, bytes_accessed=2 * (slots + count) * width**2, transcendentals=0
    )
    params = pltpu.CompilerParams(vmem_limit_bytes=4 << 20)
    in_specs = [SMEM] * 3 + [VMEM] * (count + 2)
    if ending is None:
        return pl.pallas_call(
            functools.partial(coupled_kernel, count),
            out_shape=shape,
            in_specs=in_specs,
            out_specs=VMEM,
            compiler_params=params,
            cost_estimate=cost,
        )(sources, neighbours, couplings, *arrays)
    ranks, energies, masked = ending
    return pl.pallas_call(
        functools.partial(last_kernel, count),
        out_shape=(shape, shape),
        in_specs=in_specs + [SMEM, VMEM, VMEM],
        out_specs=(VMEM, VMEM),
        compiler_params=params,
        cost_estimate=cost,
    )(sources, neighbours, couplings, *arrays, ranks, energies, *held(masked))


def shards(amplitudes, ranks, neighbours, intersections, couplings, energies, factors):
    pno_width = amplitudes.shape[1]
    aux_count = lax.axis_size("aux")
    axis = "pair"
    count = lax.axis_size(axis)
    me = lax.axis_index(axis)
    masked = mask(ranks, amplitudes[0])
    inter = intersections[0]

    own = {0: masked}
    for bits in reversed(range(2, WIN, 2)):
        own[bits] = swapped(masked, axis, bits)
    after = shifted(masked, axis, -WIN)
    before = shifted(masked, axis, WIN)
    own[2], own[4], after, before = lax.optimization_barrier((own[2], own[4], after, before))

    def side(bits):
        return jnp.where((me & top_bit(bits)) != 0, before, after)

    far = {bits: swapped(side(bits), axis, bits) for bits in range(2, WIN, 2)}
    for bits in range(1, WIN, 2):
        own[bits] = swapped(own[bits - 1], axis, 1)
    far[1] = swapped(side(1), axis, 1)
    own[3], factors = lax.optimization_barrier((own[3], factors))
    exchange = jnp.einsum("qa,qb->ab", factors[0, 0], factors[0, 1], preferred_element_type=F32)
    near_blocks = [(me ^ bits, own[bits]) for bits in range(WIN)]
    partial_sum = coupled(near_blocks, neighbours, couplings, inter, exchange)
    far, partial_sum = lax.optimization_barrier((far, partial_sum))

    def far_source(bits):
        other = me ^ bits
        return jnp.where(other > me, other - WIN + count, other + WIN) % count

    for bits in range(3, WIN, 2):
        far[bits] = swapped(far[bits - 1], axis, 1)
    far_blocks = [((me - WIN + count) % count, before), ((me + WIN) % count, after)]
    far_blocks += [(far_source(bits), far[bits]) for bits in (1, *range(2, WIN, 2))]
    partial_sum = coupled(far_blocks, neighbours, couplings, inter, partial_sum)
    far_blocks = [(far_source(bits), far[bits]) for bits in range(3, WIN, 2)]
    if aux_count == 1:
        residual, updated = coupled(
            far_blocks, neighbours, couplings, inter, partial_sum, (ranks, energies, masked)
        )
        return residual[None], updated[None]

    partial_sum = coupled(far_blocks, neighbours, couplings, inter, partial_sum)[None]
    row_span = pno_width // aux_count
    first_row = lax.axis_index("aux") * row_span
    live_rows = jnp.arange(pno_width)[None, :] < ranks[:, None]
    square_mask = live_rows[:, :, None] & live_rows[:, None, :]
    summed = lax.psum_scatter(partial_sum, "aux", scatter_dimension=1, tiled=True)
    row_energy = lax.dynamic_slice_in_dim(energies, first_row, row_span, 1)
    denominator = row_energy[:, :, None] + energies[:, None, :]
    row_amp = lax.dynamic_slice_in_dim(masked[None], first_row, row_span, 1).astype(F32)
    row_mask = lax.dynamic_slice_in_dim(square_mask, first_row, row_span, 1)
    residual = jnp.where(row_mask, summed + denominator * row_amp, jnp.zeros((), F32))
    return (residual, row_amp - residual / denominator)


def solution(mesh):
    return jax.shard_map(
        shards,
        mesh=mesh,
        in_specs=(
            P("pair", None, None),
            P("pair"),
            P("pair", "aux"),
            P("pair", "aux", None, None),
            P("pair", "aux"),
            P("pair", None),
            P("pair", None, "aux", None),
        ),
        out_specs=(P("pair", "aux", None), P("pair", "aux", None)),
        check_vma=False,
    )
```

time: 38.8 us -> 31 us (0.80)
  waiting for transfers between devices: 13.9 us -> 6.62 us
  other arithmetic: 3.41 us -> 0.11 us
  Pallas kernels: 2.76 us -> 6.06 us
    ppermute x16, waiting for transfers between devices: 13.9 us -> 6.62 us  [permuted(): lax.ppermute(value, axis, [(source, target(source)) for source in range(c...]
    pallas_call x1 -> x4, Pallas kernels: 2.76 us -> 6.06 us  [the longest x2 2.61 us: coupled(): pl.pallas_call(functools.partial(coupled_kernel, count), out_shape=shape,...]
    sub x1 -> x0, other arithmetic: 1.72 us -> none  [shards(): return (residual, row_amp - residual / denominator)]
    select_n x1 -> x0, other arithmetic: 1.01 us -> none  [shards(): masked = jnp.where(square_mask, amplitudes, jnp.zeros((), jnp.bfloat16))]
    select_n x1, other arithmetic: 0.68 us -> 0.03 us  [side(): return jnp.where(me & top_bit(bits) != 0, before, after)]
  transfers between devices with their start and end apart: 16 -> 16, of which waited for: 7 -> 6; matrix products, arithmetic and copies ran while one was open for 11% -> 12% of each run, Pallas kernels for 0% -> 8%
where the time goes in v2:
time: 31 us; the launch traced here: 30.9 us
  starting transfers between devices  12.9 us (42%)
  waiting for transfers between devices  6.62 us (21%)
  Pallas kernels  6.06 us (20%)
  matrix products  3.52 us (11%)
  between operations  1.42 us (5%)
    ppermute x16, starting transfers between devices, permuted(): lax.ppermute(value, axis, [(source, target(source)) for source in range(c...  12.9 us
    ppermute x16, waiting for transfers between devices, permuted(): lax.ppermute(value, axis, [(source, target(source)) for source in range(c...  6.62 us
    dot_general x1, matrix products, shards(): jnp.einsum('qa,qb->ab', factors[0, 0], factors[0, 1], preferred_element_t...  3.52 us
    pallas_call x2, Pallas kernels, coupled(): pl.pallas_call(functools.partial(coupled_kernel, count), out_shape=shape,...  2.61 us
    pallas_call x1, Pallas kernels, coupled(): pl.pallas_call(functools.partial(last_kernel, count), out_shape=(shape, s...  1.85 us
    pallas_call x1, Pallas kernels, mask(): pl.pallas_call(mask_kernel, out_shape=jax.ShapeDtypeStruct(amplitude.shap...  1.6 us
  transfers between devices with their start and end apart: 16, of which 6 were waited for; matrix products, arithmetic and copies ran while one was open for 12% of the time, Pallas kernels for 8%

profile of v2, /device:TPU:0, one launch (start us, length us, event | category | flops | bytes accessed | tf_op | source)
XLA Modules:
  0.0 30.9 jit_solution(18254291973245231877)
XLA Ops:
  1.3 1.6 %shard_map.86.refs_0_.refs_7_ = bf16[256,256]{1,0:T(8,128)(2,1)} custom-call(s32[1]{0:T(128)S(6)} %copy.9.rank.refs_5_, bf16[256,256]{1,0:T(8,128)(2,1)} %bitcast.30), custom_call_target="tpu_custom_call" | custom-call | tf_op jit(solution)/shard_map/pallas_call | solution.py:51
  2.9 3.0 %collective-permute-start.3 = (bf16[256,256]{1,0:T(8,128)(2,1)}, bf16[256,256]{1,0:T(8,128)(2,1)S(1)}, u32[]{:S(2)}, u32[]{:S(2)}) collective-permute-start(bf16[256,256]{1,0:T(8,128)(2,1)} %shard_map.86.refs_0_.refs_7_), channel_id=1, source_target_pairs={{0,8},{1,9},{2,10},{3,11},{4,12},{5,13},{6,14},{7,15},{8,16},{9,17... | collective-permute-start | bytes 393224 | tf_op jit(solution)/shard_map/ppermute | solution.py:19
  5.9 2.0 %collective-permute-start.2 = (bf16[256,256]{1,0:T(8,128)(2,1)}, bf16[256,256]{1,0:T(8,128)(2,1)S(1)}, u32[]{:S(2)}, u32[]{:S(2)}) collective-permute-start(bf16[256,256]{1,0:T(8,128)(2,1)} %shard_map.86.refs_0_.refs_7_), channel_id=1, source_target_pairs={{0,24},{1,25},{2,26},{3,27},{4,28},{5,29},{6,30},{7,31},{8,0},{9,1... | collective-permute-start | bytes 393224 | tf_op jit(solution)/shard_map/ppermute | solution.py:19
  7.9 1.7 %collective-permute-start.1 = (bf16[256,256]{1,0:T(8,128)(2,1)}, bf16[256,256]{1,0:T(8,128)(2,1)S(1)}, u32[]{:S(2)}, u32[]{:S(2)}) collective-permute-start(bf16[256,256]{1,0:T(8,128)(2,1)} %shard_map.86.refs_0_.refs_7_), channel_id=1, source_target_pairs={{0,4},{1,5},{2,6},{3,7},{4,0},{5,1},{6,2},{7,3},{8,12},{9,13},{10,... | collective-permute-start | bytes 393224 | tf_op jit(solution)/shard_map/ppermute | solution.py:19
  9.7 1.5 %collective-permute-start = (bf16[256,256]{1,0:T(8,128)(2,1)}, bf16[256,256]{1,0:T(8,128)(2,1)S(1)}, u32[]{:S(2)}, u32[]{:S(2)}) collective-permute-start(bf16[256,256]{1,0:T(8,128)(2,1)} %shard_map.86.refs_0_.refs_7_), channel_id=1, source_target_pairs={{0,2},{1,3},{2,0},{3,1},{4,6},{5,7},{6,4},{7,5},{8,10},{9,11},{10,... | collective-permute-start | bytes 393224 | tf_op jit(solution)/shard_map/ppermute | solution.py:19
  11.2 0.3 collective-permute-start.11
  11.4 0.1 stack.79.sources
  11.5 0.1 stack.72.sources
  11.6 0.9 %collective-permute-done.3.refs_0_ = bf16[256,256]{1,0:T(8,128)(2,1)S(1)} collective-permute-done((bf16[256,256]{1,0:T(8,128)(2,1)}, bf16[256,256]{1,0:T(8,128)(2,1)S(1)}, u32[]{:S(2)}, u32[]{:S(2)}) %collective-permute-start.3) | collective-permute-done | bytes 131104 | tf_op jit(solution)/shard_map/ppermute | solution.py:19
  12.5 0.0 collective-permute-start.8
  12.5 1.4 %collective-permute-done.2.refs_1_ = bf16[256,256]{1,0:T(8,128)(2,1)S(1)} collective-permute-done((bf16[256,256]{1,0:T(8,128)(2,1)}, bf16[256,256]{1,0:T(8,128)(2,1)S(1)}, u32[]{:S(2)}, u32[]{:S(2)}) %collective-permute-start.2) | collective-permute-done | bytes 131104 | tf_op jit(solution)/shard_map/ppermute | solution.py:19
  13.9 0.0 collective-permute-done.1.refs_4_
  13.9 1.9 %collective-permute-done.refs_2_ = bf16[256,256]{1,0:T(8,128)(2,1)S(1)} collective-permute-done((bf16[256,256]{1,0:T(8,128)(2,1)}, bf16[256,256]{1,0:T(8,128)(2,1)S(1)}, u32[]{:S(2)}, u32[]{:S(2)}) %collective-permute-start) | collective-permute-done | bytes 131104 | tf_op jit(solution)/shard_map/ppermute | solution.py:19
  15.7 1.6 %collective-permute-done.11.refs_6_ = bf16[256,256]{1,0:T(8,128)(2,1)S(1)} collective-permute-done((bf16[256,256]{1,0:T(8,128)(2,1)}, bf16[256,256]{1,0:T(8,128)(2,1)S(1)}, u32[]{:S(2)}, u32[]{:S(2)}) %collective-permute-start.11) | collective-permute-done | bytes 131104 | tf_op jit(solution)/shard_map/ppermute | solution.py:19
  17.4 2.2 %collective-permute-start.7 = (bf16[256,256]{1,0:T(8,128)(2,1)S(1)}, bf16[256,256]{1,0:T(8,128)(2,1)S(1)}, u32[]{:S(2)}, u32[]{:S(2)}) collective-permute-start(bf16[256,256]{1,0:T(8,128)(2,1)S(1)} %get-tuple-element.28), channel_id=1, source_target_pairs={{0,6},{1,7},{2,4},{3,5},{4,2},{5,3},{6,0},{7,1},{8,14},{9,15},{10,... | collective-permute-start | bytes 393224 | tf_op jit(solution)/shard_map/ppermute | solution.py:19
  19.6 0.5 %collective-permute-start.6 = (bf16[256,256]{1,0:T(8,128)(2,1)S(1)}, bf16[256,256]{1,0:T(8,128)(2,1)S(1)}, u32[]{:S(2)}, u32[]{:S(2)}) collective-permute-start(bf16[256,256]{1,0:T(8,128)(2,1)S(1)} %get-tuple-element.28), channel_id=1, source_target_pairs={{0,4},{1,5},{2,6},{3,7},{4,0},{5,1},{6,2},{7,3},{8,12},{9,13},{10,... | collective-permute-start | bytes 393224 | tf_op jit(solution)/shard_map/ppermute | solution.py:19
  20.2 0.9 %collective-permute-start.5 = (bf16[256,256]{1,0:T(8,128)(2,1)S(1)}, bf16[256,256]{1,0:T(8,128)(2,1)S(1)}, u32[]{:S(2)}, u32[]{:S(2)}) collective-permute-start(bf16[256,256]{1,0:T(8,128)(2,1)S(1)} %get-tuple-element.29), channel_id=1, source_target_pairs={{0,2},{1,3},{2,0},{3,1},{4,6},{5,7},{6,4},{7,5},{8,10},{9,11},{10,... | collective-permute-start | bytes 393224 | tf_op jit(solution)/shard_map/ppermute | solution.py:19
  21.1 0.0 collective-permute-done.12.refs_7_
  21.1 0.0 copy-start.3
  21.1 0.2 collective-permute-start.4
  21.3 3.5 %fusion.refs_9_ = f32[256,256]{1,0:T(8,128)S(1)} fusion(bf16[1,2,5120,256]{3,2,1,0:T(8,128)(2,1)} %param.13), kind=kOutput, calls=%fused_computation | convolution fusion | flops 671088640 | bytes 5505024 | tf_op jit(solution)/shard_map/qa,qb->ab/dot_general | solution.py:146
  24.8 0.0 collective-permute-done.10.refs_5_
  24.9 1.4 %shard_map.87.refs_7_ = f32[256,256]{1,0:T(8,128)S(1)} custom-call(s32[8]{0:T(128)S(1)} %stack.72.sources, s32[1,16]{1,0:T(1,128)S(1)} %copy-done.2, f32[1,16]{1,0:T(1,128)S(1)} %copy-done.3, bf16[256,256]{1,0:T(8,128)(2,1)S(1)} %copy-done.1, bf16[256,256]{1,0:T(8,128)(2,1)S(1)} %collective-permute-done.8.refs_1_, ...), custom_call_target="tpu_custom_call" | custom-call | flops 536870912 | bytes 3145728 | tf_op jit(solution)/shard_map/pallas_call | solution.py:103
  26.3 0.0 copy-start.4
  26.3 0.6 %collective-permute-done.5.refs_3_ = bf16[256,256]{1,0:T(8,128)(2,1)S(1)} collective-permute-done((bf16[256,256]{1,0:T(8,128)(2,1)S(1)}, bf16[256,256]{1,0:T(8,128)(2,1)S(1)}, u32[]{:S(2)}, u32[]{:S(2)}) %collective-permute-start.5) | collective-permute-done | bytes 131104 | tf_op jit(solution)/shard_map/ppermute | solution.py:19
  26.9 0.2 collective-permute-done.6.refs_4_
  27.1 0.0 collective-permute-start.13
  27.1 0.5 %collective-permute-start.14 = (bf16[256,256]{1,0:T(8,128)(2,1)S(1)}, bf16[256,256]{1,0:T(8,128)(2,1)S(1)}, u32[]{:S(2)}, u32[]{:S(2)}) collective-permute-start(bf16[256,256]{1,0:T(8,128)(2,1)S(1)} %collective-permute-done.6.refs_4_), channel_id=1, source_target_pairs={{0,1},{1,0},{2,3},{3,2},{4,5},{5,4},{6,7},{7,6},{8,9},{9,8},{10,11... | collective-permute-start | bytes 393224 | tf_op jit(solution)/shard_map/ppermute | solution.py:19
  27.6 0.0 collective-permute-start.15
  27.7 0.1 pad_add_fusion.sources
  27.7 1.2 %shard_map.88.refs_4_ = f32[256,256]{1,0:T(8,128)S(1)} custom-call(s32[6]{0:T(128)S(1)} %stack.79.sources, s32[1,16]{1,0:T(1,128)S(1)} %copy-done.2, f32[1,16]{1,0:T(1,128)S(1)} %copy-done.3, bf16[256,256]{1,0:T(8,128)(2,1)S(1)} %collective-permute-done.3.refs_0_, bf16[256,256]{1,0:T(8,128)(2,1)S(1)} %collective-permute-done.2.refs_1_, ...), custom_call_target="tpu_custom_call" | custom-call | flops 402653184 | bytes 2883584 | tf_op jit(solution)/shard_map/pallas_call | solution.py:103
  29.0 1.8 %shard_map.89 = (f32[256,256]{1,0:T(8,128)}, f32[256,256]{1,0:T(8,128)}) custom-call(s32[3]{0:T(128)S(1)} %pad_add_fusion.sources, s32[1,16]{1,0:T(1,128)S(1)} %copy-done.2, f32[1,16]{1,0:T(1,128)S(1)} %copy-done.3, bf16[256,256]{1,0:T(8,128)(2,1)S(1)} %collective-permute-done.13.refs_0_, bf16[256,256]{1,0:T(8,128)(2,1)S(1)} %collective-permute-done.14.refs_1_, ...), custom_call_target="tpu_custom_call" | custom-call | flops 201326592 | bytes 2490368 | tf_op jit(solution)/shard_map/pallas_call | solution.py:112
  (19 shorter events, 0.1 us)
Async XLA Ops:
  2.9 9.6 %collective-permute-start.3 = (bf16[256,256]{1,0:T(8,128)(2,1)}, bf16[256,256]{1,0:T(8,128)(2,1)S(1)}, u32[]{:S(2)}, u32[]{:S(2)}) collective-permute-start(bf16[256,256]{1,0:T(8,128)(2,1)} %shard_map.86.refs_0_.refs_7_), channel_id=1, source_target_pairs={{0,8},{1,9},{2,10},{3,11},{4,12},{5,13},{6,14},{7,15},{8,16},{9,17... | collective-permute-start | bytes 393224 | tf_op jit(solution)/shard_map/ppermute | solution.py:19
  5.9 8.0 %collective-permute-start.2 = (bf16[256,256]{1,0:T(8,128)(2,1)}, bf16[256,256]{1,0:T(8,128)(2,1)S(1)}, u32[]{:S(2)}, u32[]{:S(2)}) collective-permute-start(bf16[256,256]{1,0:T(8,128)(2,1)} %shard_map.86.refs_0_.refs_7_), channel_id=1, source_target_pairs={{0,24},{1,25},{2,26},{3,27},{4,28},{5,29},{6,30},{7,31},{8,0},{9,1... | collective-permute-start | bytes 393224 | tf_op jit(solution)/shard_map/ppermute | solution.py:19
  7.9 6.0 %collective-permute-start.1 = (bf16[256,256]{1,0:T(8,128)(2,1)}, bf16[256,256]{1,0:T(8,128)(2,1)S(1)}, u32[]{:S(2)}, u32[]{:S(2)}) collective-permute-start(bf16[256,256]{1,0:T(8,128)(2,1)} %shard_map.86.refs_0_.refs_7_), channel_id=1, source_target_pairs={{0,4},{1,5},{2,6},{3,7},{4,0},{5,1},{6,2},{7,3},{8,12},{9,13},{10,... | collective-permute-start | bytes 393224 | tf_op jit(solution)/shard_map/ppermute | solution.py:19
  9.7 6.1 %collective-permute-start = (bf16[256,256]{1,0:T(8,128)(2,1)}, bf16[256,256]{1,0:T(8,128)(2,1)S(1)}, u32[]{:S(2)}, u32[]{:S(2)}) collective-permute-start(bf16[256,256]{1,0:T(8,128)(2,1)} %shard_map.86.refs_0_.refs_7_), channel_id=1, source_target_pairs={{0,2},{1,3},{2,0},{3,1},{4,6},{5,7},{6,4},{7,5},{8,10},{9,11},{10,... | collective-permute-start | bytes 393224 | tf_op jit(solution)/shard_map/ppermute | solution.py:19
  11.2 6.2 %collective-permute-start.11 = (bf16[256,256]{1,0:T(8,128)(2,1)}, bf16[256,256]{1,0:T(8,128)(2,1)S(1)}, u32[]{:S(2)}, u32[]{:S(2)}) collective-permute-start(bf16[256,256]{1,0:T(8,128)(2,1)} %shard_map.86.refs_0_.refs_7_), channel_id=1, source_target_pairs={{0,6},{1,7},{2,4},{3,5},{4,2},{5,3},{6,0},{7,1},{8,14},{9,15},{10,... | collective-permute-start | bytes 393224 | tf_op jit(solution)/shard_map/ppermute | solution.py:19
  12.5 7.7 %collective-permute-start.8 = (bf16[256,256]{1,0:T(8,128)(2,1)}, bf16[256,256]{1,0:T(8,128)(2,1)S(1)}, u32[]{:S(2)}, u32[]{:S(2)}) collective-permute-start(bf16[256,256]{1,0:T(8,128)(2,1)} %shard_map.86.refs_0_.refs_7_), channel_id=1, source_target_pairs={{0,1},{1,0},{2,3},{3,2},{4,5},{5,4},{6,7},{7,6},{8,9},{9,8},{10,11... | collective-permute-start | bytes 393224 | tf_op jit(solution)/shard_map/ppermute | solution.py:19
  15.7 4.4 %collective-permute-start.9 = (bf16[256,256]{1,0:T(8,128)(2,1)S(1)}, bf16[256,256]{1,0:T(8,128)(2,1)S(1)}, u32[]{:S(2)}, u32[]{:S(2)}) collective-permute-start(bf16[256,256]{1,0:T(8,128)(2,1)S(1)} %collective-permute-done.refs_2_), channel_id=1, source_target_pairs={{0,1},{1,0},{2,3},{3,2},{4,5},{5,4},{6,7},{7,6},{8,9},{9,8},{10,11... | collective-permute-start | bytes 393224 | tf_op jit(solution)/shard_map/ppermute | solution.py:19
  17.4 3.7 %collective-permute-start.12 = (bf16[256,256]{1,0:T(8,128)(2,1)S(1)}, bf16[256,256]{1,0:T(8,128)(2,1)S(1)}, u32[]{:S(2)}, u32[]{:S(2)}) collective-permute-start(bf16[256,256]{1,0:T(8,128)(2,1)S(1)} %collective-permute-done.11.refs_6_), channel_id=1, source_target_pairs={{0,1},{1,0},{2,3},{3,2},{4,5},{5,4},{6,7},{7,6},{8,9},{9,8},{10,11... | collective-permute-start | bytes 393224 | tf_op jit(solution)/shard_map/ppermute | solution.py:19
  17.4 9.5 %collective-permute-start.7 = (bf16[256,256]{1,0:T(8,128)(2,1)S(1)}, bf16[256,256]{1,0:T(8,128)(2,1)S(1)}, u32[]{:S(2)}, u32[]{:S(2)}) collective-permute-start(bf16[256,256]{1,0:T(8,128)(2,1)S(1)} %get-tuple-element.28), channel_id=1, source_target_pairs={{0,6},{1,7},{2,4},{3,5},{4,2},{5,3},{6,0},{7,1},{8,14},{9,15},{10,... | collective-permute-start | bytes 393224 | tf_op jit(solution)/shard_map/ppermute | solution.py:19
  19.6 7.5 %collective-permute-start.6 = (bf16[256,256]{1,0:T(8,128)(2,1)S(1)}, bf16[256,256]{1,0:T(8,128)(2,1)S(1)}, u32[]{:S(2)}, u32[]{:S(2)}) collective-permute-start(bf16[256,256]{1,0:T(8,128)(2,1)S(1)} %get-tuple-element.28), channel_id=1, source_target_pairs={{0,4},{1,5},{2,6},{3,7},{4,0},{5,1},{6,2},{7,3},{8,12},{9,13},{10,... | collective-permute-start | bytes 393224 | tf_op jit(solution)/shard_map/ppermute | solution.py:19
  20.2 4.7 %collective-permute-start.10 = (bf16[256,256]{1,0:T(8,128)(2,1)S(1)}, bf16[256,256]{1,0:T(8,128)(2,1)S(1)}, u32[]{:S(2)}, u32[]{:S(2)}) collective-permute-start(bf16[256,256]{1,0:T(8,128)(2,1)S(1)} %collective-permute-done.1.refs_4_), channel_id=1, source_target_pairs={{0,1},{1,0},{2,3},{3,2},{4,5},{5,4},{6,7},{7,6},{8,9},{9,8},{10,11... | collective-permute-start | bytes 393224 | tf_op jit(solution)/shard_map/ppermute | solution.py:19
  20.2 6.8 %collective-permute-start.5 = (bf16[256,256]{1,0:T(8,128)(2,1)S(1)}, bf16[256,256]{1,0:T(8,128)(2,1)S(1)}, u32[]{:S(2)}, u32[]{:S(2)}) collective-permute-start(bf16[256,256]{1,0:T(8,128)(2,1)S(1)} %get-tuple-element.29), channel_id=1, source_target_pairs={{0,2},{1,3},{2,0},{3,1},{4,6},{5,7},{6,4},{7,5},{8,10},{9,11},{10,... | collective-permute-start | bytes 393224 | tf_op jit(solution)/shard_map/ppermute | solution.py:19
  21.1 3.8 %copy-start = (bf16[1,16,256,256]{3,2,1,0:T(8,128)(2,1)S(1)}, bf16[1,16,256,256]{3,2,1,0:T(8,128)(2,1)}, u32[]{:S(2)}) copy-start(bf16[1,16,256,256]{3,2,1,0:T(8,128)(2,1)} %param.10) | copy-start | bytes 6291460
  21.1 3.8 %copy-start.1 = (bf16[256,256]{1,0:T(8,128)(2,1)S(1)}, bf16[256,256]{1,0:T(8,128)(2,1)}, u32[]{:S(2)}) copy-start(bf16[256,256]{1,0:T(8,128)(2,1)} %shard_map.86.refs_0_.refs_7_) | copy-start | bytes 393220
  21.1 3.8 %copy-start.2 = (s32[1,16]{1,0:T(1,128)S(1)}, s32[1,16]{1,0:T(1,128)}, u32[]{:S(2)}) copy-start(s32[1,16]{1,0:T(1,128)} %neighbours.5) | copy-start | bytes 196
  21.1 3.8 %copy-start.3 = (f32[1,16]{1,0:T(1,128)S(1)}, f32[1,16]{1,0:T(1,128)}, u32[]{:S(2)}) copy-start(f32[1,16]{1,0:T(1,128)} %couplings.5) | copy-start | bytes 196
  21.1 5.8 %collective-permute-start.4 = (bf16[256,256]{1,0:T(8,128)(2,1)S(1)}, bf16[256,256]{1,0:T(8,128)(2,1)S(1)}, u32[]{:S(2)}, u32[]{:S(2)}) collective-permute-start(bf16[256,256]{1,0:T(8,128)(2,1)S(1)} %get-tuple-element.30), channel_id=1, source_target_pairs={{0,1},{1,0},{2,3},{3,2},{4,5},{5,4},{6,7},{7,6},{8,9},{9,8},{10,11... | collective-permute-start | bytes 393224 | tf_op jit(solution)/shard_map/ppermute | solution.py:19
  26.3 2.7 %copy-start.4 = (f32[1,256]{1,0:T(1,128)S(1)}, f32[1,256]{1,0:T(1,128)}, u32[]{:S(2)}) copy-start(f32[1,256]{1,0:T(1,128)} %refs_6_.1) | copy-start | bytes 3076
  27.1 1.9 %collective-permute-start.13 = (bf16[256,256]{1,0:T(8,128)(2,1)S(1)}, bf16[256,256]{1,0:T(8,128)(2,1)S(1)}, u32[]{:S(2)}, u32[]{:S(2)}) collective-permute-start(bf16[256,256]{1,0:T(8,128)(2,1)S(1)} %collective-permute-done.5.refs_3_), channel_id=1, source_target_pairs={{0,1},{1,0},{2,3},{3,2},{4,5},{5,4},{6,7},{7,6},{8,9},{9,8},{10,11... | collective-permute-start | bytes 393224 | tf_op jit(solution)/shard_map/ppermute | solution.py:19
  27.1 1.8 %collective-permute-start.14 = (bf16[256,256]{1,0:T(8,128)(2,1)S(1)}, bf16[256,256]{1,0:T(8,128)(2,1)S(1)}, u32[]{:S(2)}, u32[]{:S(2)}) collective-permute-start(bf16[256,256]{1,0:T(8,128)(2,1)S(1)} %collective-permute-done.6.refs_4_), channel_id=1, source_target_pairs={{0,1},{1,0},{2,3},{3,2},{4,5},{5,4},{6,7},{7,6},{8,9},{9,8},{10,11... | collective-permute-start | bytes 393224 | tf_op jit(solution)/shard_map/ppermute | solution.py:19
  27.6 1.4 %collective-permute-start.15 = (bf16[256,256]{1,0:T(8,128)(2,1)S(1)}, bf16[256,256]{1,0:T(8,128)(2,1)S(1)}, u32[]{:S(2)}, u32[]{:S(2)}) collective-permute-start(bf16[256,256]{1,0:T(8,128)(2,1)S(1)} %collective-permute-done.7.refs_5_), channel_id=1, source_target_pairs={{0,1},{1,0},{2,3},{3,2},{4,5},{5,4},{6,7},{7,6},{8,9},{9,8},{10,11... | collective-permute-start | bytes 393224 | tf_op jit(solution)/shard_map/ppermute | solution.py:19

commit v3 on v2

v3 whole, which is shorter than its diff:
```python
import functools

import jax
import jax.numpy as jnp
from jax import lax
from jax.experimental import pallas as pl
from jax.experimental.pallas import tpu as pltpu
from jax.sharding import PartitionSpec as P

WIN = 8
F32 = jnp.float32
BF16 = jnp.bfloat16
VMEM = pl.BlockSpec(memory_space=pltpu.VMEM)
SMEM = pl.BlockSpec(memory_space=pltpu.SMEM)
PARAMS = pltpu.CompilerParams(vmem_limit_bytes=4 << 20)


def permuted(value, axis, target):
    count = lax.axis_size(axis)
    return lax.ppermute(value, axis, [(source, target(source)) for source in range(count)])


def swapped(value, axis, bits):
    return permuted(value, axis, lambda source: source ^ bits)


def shifted(value, axis, steps):
    count = lax.axis_size(axis)
    return permuted(value, axis, lambda source: (source + steps) % count)


def top_bit(number):
    return 1 << (number.bit_length() - 1)


def held(*arrays):
    return [pltpu.with_memory_space_constraint(array, pltpu.VMEM) for array in arrays]


def live_square(rank, shape):
    rows = lax.broadcasted_iota(jnp.int32, shape, 0)
    columns = lax.broadcasted_iota(jnp.int32, shape, 1)
    return jnp.maximum(rows, columns) < rank


def cost(count, width):
    return pl.CostEstimate(
        flops=4 * count * width**3, bytes_accessed=4 * count * width**2, transcendentals=0
    )


def mask_kernel(rank, amplitude, masked):
    square = live_square(rank[...], amplitude.shape)
    masked[...] = jnp.where(square, amplitude[...].astype(F32), 0.0).astype(BF16)


def mask(ranks, amplitude):
    return pl.pallas_call(
        mask_kernel,
        out_shape=pltpu.VMEM(amplitude.shape, BF16),
        in_specs=[VMEM, VMEM],
        out_specs=VMEM,
    )(ranks[None], amplitude)


def pack_kernel(axis, *refs):
    (before, after), own = refs[:2], refs[2 : 2 + WIN // 2]
    packed, *sides = refs[2 + WIN // 2 :]
    me = lax.axis_index(axis)
    for position, block in enumerate(own):
        packed[position] = block[...]
    for bits, side in zip((1, 2, 4), (packed.at[len(own)], *sides)):
        side[...] = jnp.where((me & bits) != 0, before[...], after[...])


def pack(axis, before, after, own):
    shape = pltpu.VMEM(before.shape, BF16)
    arrays = held(before, after, *own)
    return pl.pallas_call(
        functools.partial(pack_kernel, axis),
        out_shape=(pltpu.VMEM((len(own) + 1, *before.shape), BF16), shape, shape),
        in_specs=[VMEM] * len(arrays),
        out_specs=(VMEM,) * 3,
        compiler_params=PARAMS,
    )(*arrays)


def one_term(inter, block, factor):
    half = jnp.dot(inter, block, preferred_element_type=F32).astype(BF16)
    projected = lax.dot_general(
        half, inter, (((1,), (1,)), ((), ())), preferred_element_type=F32
    )
    return factor * projected


def find(position, sources, neighbours, couplings):
    slot, factor = jnp.int32(0), jnp.float32(0)
    for n in range(neighbours.shape[1]):
        hit = neighbours[0, n] == sources[position]
        slot = jnp.where(hit, n, slot)
        factor = jnp.where(hit, couplings[0, n], factor)
    return slot, factor


def near_kernel(
    whole, sources, neighbours, couplings, rank, energy, inter, start, mine, theirs,
    total, scale, far_inter, far_factor, near_inter, sems,
):
    near = [ref.at[k] for ref in (mine, theirs) for k in range(WIN // 2)]
    copies, factors = [], []
    for position in range(sources.shape[0]):
        slot, factor = find(position, sources, neighbours, couplings)
        far = position - len(near)
        target = near_inter.at[position] if far < 0 else far_inter.at[far]
        copy = pltpu.make_async_copy(inter.at[slot], target, sems.at[position])
        copy.start()
        copies.append(copy)
        factors.append(factor)
    along = jnp.broadcast_to(energy[...], total.shape)
    denominator = along + along.T
    sum_now = start[...]
    if whole:
        sum_now = sum_now + denominator * mine[0].astype(F32)
    scale[...] = jnp.where(live_square(rank[...], total.shape), 1.0 / denominator, 0.0)
    for far in range(far_inter.shape[0]):
        far_factor[far] = jnp.full(far_factor.shape[1:], factors[len(near) + far], F32)
    for position, block in enumerate(near):
        copies[position].wait()
        sum_now = sum_now + one_term(near_inter[position], block[...], factors[position])
    total[...] = sum_now
    for copy in copies[len(near):]:
        copy.wait()


def near_sum(whole, sources, neighbours, couplings, ranks, energies, inter, start, mine, theirs):
    far = sources.shape[0] - WIN
    width = start.shape[0]
    inter = pltpu.with_memory_space_constraint(inter, pltpu.HBM)
    return pl.pallas_call(
        functools.partial(near_kernel, whole),
        out_shape=(
            pltpu.VMEM(start.shape, F32),
            pltpu.VMEM(start.shape, F32),
            pltpu.VMEM((far, width, width), BF16),
            pltpu.VMEM((far, 1, width), F32),
        ),
        in_specs=[SMEM] * 3 + [VMEM] * 2 + [pl.BlockSpec(memory_space=pl.ANY)] + [VMEM] * 3,
        out_specs=(VMEM,) * 4,
        scratch_shapes=[
            pltpu.VMEM((WIN, width, width), BF16),
            pltpu.SemaphoreType.DMA((sources.shape[0],)),
        ],
        compiler_params=PARAMS,
        cost_estimate=cost(WIN, width),
    )(sources, neighbours, couplings, ranks[None], energies, inter, *held(start, mine, theirs))


def far_kernel(first, count, far_inter, far_factor, start, *refs):
    sum_now = start[...]
    for position in range(count):
        block = refs[position]
        block = block[...] if len(block.shape) == 2 else block[block.shape[0] - 1]
        sum_now = sum_now + one_term(
            far_inter[first + position], block, far_factor[first + position]
        )
    if len(refs) == count + 1:
        refs[count][...] = sum_now
    else:
        scale, masked, residual, updated = refs[count:]
        residual[...] = jnp.where(scale[...] > 0, sum_now, 0.0)
        updated[...] = masked[...].astype(F32) - sum_now * scale[...]


def far_sum(first, far_inter, far_factor, start, blocks, ending=()):
    out_shape = pltpu.VMEM(start.shape, F32)
    if ending:
        out_shape = (jax.ShapeDtypeStruct(start.shape, F32),) * 2
    arrays = held(far_inter, far_factor, start, *blocks, *ending)
    return pl.pallas_call(
        functools.partial(far_kernel, first, len(blocks)),
        out_shape=out_shape,
        in_specs=[VMEM] * len(arrays),
        out_specs=(VMEM, VMEM) if ending else VMEM,
        compiler_params=PARAMS,
        cost_estimate=cost(len(blocks), start.shape[0]),
    )(*arrays)


def shards(amplitudes, ranks, neighbours, intersections, couplings, energies, factors):
    aux_count = lax.axis_size("aux")
    axis = "pair"
    count = lax.axis_size(axis)
    me = lax.axis_index(axis)
    masked = mask(ranks, amplitudes[0])
    cross = range(2, WIN, 2)

    own = {0: masked}
    for bits in reversed(cross):
        own[bits] = swapped(masked, axis, bits)
    after = shifted(masked, axis, -WIN)
    before = shifted(masked, axis, WIN)
    exchange = jnp.einsum("qa,qb->ab", factors[0, 0], factors[0, 1], preferred_element_type=F32)
    own[2], own[4], after, before, exchange = lax.optimization_barrier(
        (own[2], own[4], after, before, exchange)
    )
    mine, side2, side4 = pack(axis, before, after, [own[bits] for bits in (0, *cross)])
    far = {2: swapped(side2, axis, 2), 4: swapped(side4, axis, 4)}
    far[6] = permuted(
        own[6], axis, lambda source: (source + (-WIN if source & top_bit(6) else WIN)) % count
    )
    theirs = swapped(mine, axis, 1)

    def far_source(bits):
        other = me ^ bits
        return jnp.where(other > me, other - WIN + count, other + WIN) % count

    sources = [me ^ bits for bits in (*range(0, WIN, 2), *range(1, WIN, 2))]
    sources += [(me - WIN + count) % count, (me + WIN) % count]
    sources += [far_source(bits) for bits in (1, *cross, *range(3, WIN, 2))]
    sources = jnp.stack(sources).astype(jnp.int32)
    total, scale, far_inter, far_factor = near_sum(
        aux_count == 1, sources, neighbours, couplings, ranks, energies, intersections[0], exchange, mine, theirs
    )
    far, total, scale, far_inter, far_factor = lax.optimization_barrier(
        (far, total, scale, far_inter, far_factor)
    )
    early = [before, after, theirs, *(far[bits] for bits in cross)]
    late = [swapped(far[bits], axis, 1) for bits in cross]
    total = far_sum(0, far_inter, far_factor, total, early)
    if aux_count == 1:
        residual, updated = far_sum(len(early), far_inter, far_factor, total, late, (scale, masked))
        return residual[None], updated[None]

    partial_sum = far_sum(len(early), far_inter, far_factor, total, late)[None]
    pno_width = amplitudes.shape[1]
    row_span = pno_width // aux_count
    first_row = lax.axis_index("aux") * row_span
    live_rows = jnp.arange(pno_width)[None, :] < ranks[:, None]
    square_mask = live_rows[:, :, None] & live_rows[:, None, :]
    summed = lax.psum_scatter(partial_sum, "aux", scatter_dimension=1, tiled=True)
    row_energy = lax.dynamic_slice_in_dim(energies, first_row, row_span, 1)
    denominator = row_energy[:, :, None] + energies[:, None, :]
    row_amp = lax.dynamic_slice_in_dim(masked[None], first_row, row_span, 1).astype(F32)
    row_mask = lax.dynamic_slice_in_dim(square_mask, first_row, row_span, 1)
    residual = jnp.where(row_mask, summed + denominator * row_amp, jnp.zeros((), F32))
    return (residual, row_amp - residual / denominator)


def solution(mesh):
    return jax.shard_map(
        shards,
        mesh=mesh,
        in_specs=(
            P("pair", None, None),
            P("pair"),
            P("pair", "aux"),
            P("pair", "aux", None, None),
            P("pair", "aux"),
            P("pair", None),
            P("pair", None, "aux", None),
        ),
        out_specs=(P("pair", "aux", None), P("pair", "aux", None)),
        check_vma=False,
    )
```

time: 31 us -> 27.6 us (0.89)
  waiting for transfers between devices: 6.62 us -> 1.82 us
  Pallas kernels: 6.06 us -> 7.41 us
    ppermute x16 -> x12, waiting for transfers between devices: 6.62 us -> 1.82 us  [permuted(): lax.ppermute(value, axis, [(source, target(source)) for source in range(c...]
    pallas_call x4 -> x5, Pallas kernels: 6.06 us -> 7.41 us  [the longest x1 4.38 us: near_sum(): pl.pallas_call(functools.partial(near_kernel, whole), out_shape=(pltpu.VM...]
    ppermute x16 -> x12, starting transfers between devices: 12.9 us -> 13.2 us  [permuted(): lax.ppermute(value, axis, [(source, target(source)) for source in range(c...]
  transfers between devices with their start and end apart: 16 -> 12, of which waited for: 6 -> 6; matrix products, arithmetic and copies ran while one was open for 12% -> 13% of each run, Pallas kernels for 8% -> 18%
where the time goes in v3:
time: 27.6 us; the launch traced here: 27.4 us
  starting transfers between devices  13.2 us (48%)
  Pallas kernels  7.41 us (27%)
  matrix products  3.4 us (12%)
  waiting for transfers between devices  1.82 us (7%)
  between operations  1.42 us (5%)
    ppermute x12, starting transfers between devices, permuted(): lax.ppermute(value, axis, [(source, target(source)) for source in range(c...  13.2 us
    pallas_call x1, Pallas kernels, near_sum(): pl.pallas_call(functools.partial(near_kernel, whole), out_shape=(pltpu.VM...  4.38 us
    dot_general x1, matrix products, shards(): jnp.einsum('qa,qb->ab', factors[0, 0], factors[0, 1], preferred_element_t...  3.4 us
    pallas_call x2, Pallas kernels, far_sum(): pl.pallas_call(functools.partial(far_kernel, first, len(blocks)), out_sha...  1.96 us
    ppermute x12, waiting for transfers between devices, permuted(): lax.ppermute(value, axis, [(source, target(source)) for source in range(c...  1.82 us
    pallas_call x1, Pallas kernels, mask(): pl.pallas_call(mask_kernel, out_shape=pltpu.VMEM(amplitude.shape, BF16),...  1.01 us
  transfers between devices with their start and end apart: 12, of which 6 were waited for; matrix products, arithmetic and copies ran while one was open for 13% of the time, Pallas kernels for 18%

profile of v3, /device:TPU:0, one launch (start us, length us, event | category | flops | bytes accessed | tf_op | source)
XLA Modules:
  0.0 27.4 jit_solution(93865786683108332)
XLA Ops:
  1.3 1.0 %shard_map.86.refs_2_.refs_4_ = bf16[256,256]{1,0:T(8,128)(2,1)S(1)} custom-call(s32[1,1]{1,0:T(1,128)} %bitcast.28.rank, bf16[256,256]{1,0:T(8,128)(2,1)} %bitcast.31), custom_call_target="tpu_custom_call" | custom-call | tf_op jit(solution)/shard_map/pallas_call | solution.py:58
  2.3 0.0 copy-start
  2.3 0.0 copy-start.1
  2.3 0.0 copy-start.2
  2.3 4.0 %collective-permute-start.4 = (bf16[256,256]{1,0:T(8,128)(2,1)S(1)}, bf16[256,256]{1,0:T(8,128)(2,1)S(1)}, u32[]{:S(2)}, u32[]{:S(2)}) collective-permute-start(bf16[256,256]{1,0:T(8,128)(2,1)S(1)} %shard_map.86.refs_2_.refs_4_), channel_id=1, source_target_pairs={{0,6},{1,7},{2,4},{3,5},{4,2},{5,3},{6,0},{7,1},{8,14},{9,15},{10,... | collective-permute-start | bytes 393224 | tf_op jit(solution)/shard_map/ppermute | solution.py:20
  6.3 1.6 %collective-permute-start.3 = (bf16[256,256]{1,0:T(8,128)(2,1)S(1)}, bf16[256,256]{1,0:T(8,128)(2,1)S(1)}, u32[]{:S(2)}, u32[]{:S(2)}) collective-permute-start(bf16[256,256]{1,0:T(8,128)(2,1)S(1)} %shard_map.86.refs_2_.refs_4_), channel_id=1, source_target_pairs={{0,8},{1,9},{2,10},{3,11},{4,12},{5,13},{6,14},{7,15},{8,16},{9,17... | collective-permute-start | bytes 393224 | tf_op jit(solution)/shard_map/ppermute | solution.py:20
  7.9 2.2 %collective-permute-start.2 = (bf16[256,256]{1,0:T(8,128)(2,1)S(1)}, bf16[256,256]{1,0:T(8,128)(2,1)S(1)}, u32[]{:S(2)}, u32[]{:S(2)}) collective-permute-start(bf16[256,256]{1,0:T(8,128)(2,1)S(1)} %shard_map.86.refs_2_.refs_4_), channel_id=1, source_target_pairs={{0,24},{1,25},{2,26},{3,27},{4,28},{5,29},{6,30},{7,31},{8,0},{9,1... | collective-permute-start | bytes 393224 | tf_op jit(solution)/shard_map/ppermute | solution.py:20
  10.1 0.5 %collective-permute-start.1 = (bf16[256,256]{1,0:T(8,128)(2,1)S(1)}, bf16[256,256]{1,0:T(8,128)(2,1)S(1)}, u32[]{:S(2)}, u32[]{:S(2)}) collective-permute-start(bf16[256,256]{1,0:T(8,128)(2,1)S(1)} %shard_map.86.refs_2_.refs_4_), channel_id=1, source_target_pairs={{0,4},{1,5},{2,6},{3,7},{4,0},{5,1},{6,2},{7,3},{8,12},{9,13},{10,... | collective-permute-start | bytes 393224 | tf_op jit(solution)/shard_map/ppermute | solution.py:20
  10.6 0.3 %collective-permute-start = (bf16[256,256]{1,0:T(8,128)(2,1)S(1)}, bf16[256,256]{1,0:T(8,128)(2,1)S(1)}, u32[]{:S(2)}, u32[]{:S(2)}) collective-permute-start(bf16[256,256]{1,0:T(8,128)(2,1)S(1)} %shard_map.86.refs_2_.refs_4_), channel_id=1, source_target_pairs={{0,2},{1,3},{2,0},{3,1},{4,6},{5,7},{6,4},{7,5},{8,10},{9,11},{10,... | collective-permute-start | bytes 393224 | tf_op jit(solution)/shard_map/ppermute | solution.py:20
  10.9 3.4 %fusion.start = f32[256,256]{1,0:T(8,128)S(1)} fusion(bf16[1,2,5120,256]{3,2,1,0:T(8,128)(2,1)} %param.13), kind=kOutput, calls=%fused_computation | convolution fusion | flops 671088640 | bytes 5505024 | tf_op jit(solution)/shard_map/qa,qb->ab/dot_general | solution.py:202
  14.3 0.1 collective-permute-done.3.refs_0_
  14.5 0.9 %collective-permute-done.2.refs_1_ = bf16[256,256]{1,0:T(8,128)(2,1)S(1)} collective-permute-done((bf16[256,256]{1,0:T(8,128)(2,1)S(1)}, bf16[256,256]{1,0:T(8,128)(2,1)S(1)}, u32[]{:S(2)}, u32[]{:S(2)}) %collective-permute-start.2) | collective-permute-done | bytes 131104 | tf_op jit(solution)/shard_map/ppermute | solution.py:20
  15.4 0.0 collective-permute-done.1.refs_4_
  15.4 0.2 collective-permute-done.refs_3_
  15.6 0.1 shard_map.87
  15.7 0.1 collective-permute-start.8
  15.7 0.6 %collective-permute-start.5 = (bf16[256,256]{1,0:T(8,128)(2,1)S(1)}, bf16[256,256]{1,0:T(8,128)(2,1)S(1)}, u32[]{:S(2)}, u32[]{:S(2)}) collective-permute-start(bf16[256,256]{1,0:T(8,128)(2,1)S(1)} %get-tuple-element.27), channel_id=1, source_target_pairs={{0,2},{1,3},{2,0},{3,1},{4,6},{5,7},{6,4},{7,5},{8,10},{9,11},{10,... | collective-permute-start | bytes 393224 | tf_op jit(solution)/shard_map/ppermute | solution.py:20
  16.3 0.9 %collective-permute-start.7 = (bf16[256,256]{1,0:T(8,128)(2,1)S(1)}, bf16[256,256]{1,0:T(8,128)(2,1)S(1)}, u32[]{:S(2)}, u32[]{:S(2)}) collective-permute-start(bf16[256,256]{1,0:T(8,128)(2,1)S(1)} %collective-permute-done.4.refs_5_), channel_id=1, source_target_pairs={{0,8},{1,9},{2,10},{3,11},{4,28},{5,29},{6,30},{7,31},{8,16},{9,17... | collective-permute-start | bytes 393224 | tf_op jit(solution)/shard_map/ppermute | solution.py:20
  17.2 2.4 %collective-permute-start.6 = (bf16[256,256]{1,0:T(8,128)(2,1)S(1)}, bf16[256,256]{1,0:T(8,128)(2,1)S(1)}, u32[]{:S(2)}, u32[]{:S(2)}) collective-permute-start(bf16[256,256]{1,0:T(8,128)(2,1)S(1)} %get-tuple-element.28), channel_id=1, source_target_pairs={{0,4},{1,5},{2,6},{3,7},{4,0},{5,1},{6,2},{7,3},{8,12},{9,13},{10,... | collective-permute-start | bytes 393224 | tf_op jit(solution)/shard_map/ppermute | solution.py:20
  19.7 0.1 stack.71.sources
  19.8 0.0 collective-permute-done.8.theirs.refs_2_
  19.8 4.4 %shard_map.88 = (f32[256,256]{1,0:T(8,128)S(1)}, f32[256,256]{1,0:T(8,128)S(1)}, bf16[9,256,256]{2,1,0:T(8,128)(2,1)S(1)}, f32[9,1,256]{2,1,0:T(1,128)S(1)}) custom-call(s32[17]{0:T(128)S(1)} %stack.71.sources, s32[1,16]{1,0:T(1,128)S(1)} %copy-done.1, f32[1,16]{1,0:T(1,128)S(1)} %copy-done.2, s32[1,1]{1,0:T(1,128)} %bitcast.29.rank, f32[1,256]{1,0:T(1,128)S(1)} %copy-done, ...), custom_call_target="tpu_custom_call" | custom-call | flops 536870912 | bytes 2097152 | tf_op jit(solution)/shard_map/pallas_call | solution.py:139
  24.2 0.0 collective-permute-done.5.refs_3_
  24.2 0.0 collective-permute-done.6.refs_4_
  24.2 0.1 collective-permute-start.9
  24.3 0.5 %collective-permute-start.10 = (bf16[256,256]{1,0:T(8,128)(2,1)S(1)}, bf16[256,256]{1,0:T(8,128)(2,1)S(1)}, u32[]{:S(2)}, u32[]{:S(2)}) collective-permute-start(bf16[256,256]{1,0:T(8,128)(2,1)S(1)} %collective-permute-done.6.refs_4_), channel_id=1, source_target_pairs={{0,1},{1,0},{2,3},{3,2},{4,5},{5,4},{6,7},{7,6},{8,9},{9,8},{10,11... | collective-permute-start | bytes 393224 | tf_op jit(solution)/shard_map/ppermute | solution.py:20
  24.8 0.1 collective-permute-start.11
  24.9 0.7 %shard_map.89.start = f32[256,256]{1,0:T(8,128)S(1)} custom-call(bf16[9,256,256]{2,1,0:T(8,128)(2,1)S(1)} %get-tuple-element.35.far_inter, f32[9,1,256]{2,1,0:T(1,128)S(1)} %get-tuple-element.36.far_factor, f32[256,256]{1,0:T(8,128)S(1)} %get-tuple-element.37.start, bf16[256,256]{1,0:T(8,128)(2,1)S(1)} %collective-permute-done.3.refs_0_, ...), custom_call_target="tpu_custom_call" | custom-call | flops 402653184 | bytes 1572864 | tf_op jit(solution)/shard_map/pallas_call | solution.py:179
  25.6 0.1 collective-permute-done.9.refs_0_
  25.6 0.2 collective-permute-done.10.refs_1_
  25.8 0.3 %collective-permute-done.11.refs_2_ = bf16[256,256]{1,0:T(8,128)(2,1)S(1)} collective-permute-done((bf16[256,256]{1,0:T(8,128)(2,1)S(1)}, bf16[256,256]{1,0:T(8,128)(2,1)S(1)}, u32[]{:S(2)}, u32[]{:S(2)}) %collective-permute-start.11) | collective-permute-done | bytes 131104 | tf_op jit(solution)/shard_map/ppermute | solution.py:20
  26.1 1.3 %shard_map.90 = (f32[256,256]{1,0:T(8,128)}, f32[256,256]{1,0:T(8,128)}) custom-call(bf16[9,256,256]{2,1,0:T(8,128)(2,1)S(1)} %get-tuple-element.35.far_inter, f32[9,1,256]{2,1,0:T(1,128)S(1)} %get-tuple-element.36.far_factor, f32[256,256]{1,0:T(8,128)S(1)} %shard_map.89.start, bf16[256,256]{1,0:T(8,128)(2,1)S(1)} %collective-permute-done.9.refs_0_, ...), custom_call_target="tpu_custom_call" | custom-call | flops 201326592 | bytes 786432 | tf_op jit(solution)/shard_map/pallas_call | solution.py:179
  (5 shorter events, 0.0 us)
Async XLA Ops:
  2.3 17.5 %copy-start = (f32[1,256]{1,0:T(1,128)S(1)}, f32[1,256]{1,0:T(1,128)}, u32[]{:S(2)}) copy-start(f32[1,256]{1,0:T(1,128)} %energy.1) | copy-start | bytes 3076
  2.3 17.5 %copy-start.1 = (s32[1,16]{1,0:T(1,128)S(1)}, s32[1,16]{1,0:T(1,128)}, u32[]{:S(2)}) copy-start(s32[1,16]{1,0:T(1,128)} %neighbours.1) | copy-start | bytes 196
  2.3 17.5 %copy-start.2 = (f32[1,16]{1,0:T(1,128)S(1)}, f32[1,16]{1,0:T(1,128)}, u32[]{:S(2)}) copy-start(f32[1,16]{1,0:T(1,128)} %couplings.1) | copy-start | bytes 196
  2.3 13.3 %collective-permute-start.4 = (bf16[256,256]{1,0:T(8,128)(2,1)S(1)}, bf16[256,256]{1,0:T(8,128)(2,1)S(1)}, u32[]{:S(2)}, u32[]{:S(2)}) collective-permute-start(bf16[256,256]{1,0:T(8,128)(2,1)S(1)} %shard_map.86.refs_2_.refs_4_), channel_id=1, source_target_pairs={{0,6},{1,7},{2,4},{3,5},{4,2},{5,3},{6,0},{7,1},{8,14},{9,15},{10,... | collective-permute-start | bytes 393224 | tf_op jit(solution)/shard_map/ppermute | solution.py:20
  6.3 8.2 %collective-permute-start.3 = (bf16[256,256]{1,0:T(8,128)(2,1)S(1)}, bf16[256,256]{1,0:T(8,128)(2,1)S(1)}, u32[]{:S(2)}, u32[]{:S(2)}) collective-permute-start(bf16[256,256]{1,0:T(8,128)(2,1)S(1)} %shard_map.86.refs_2_.refs_4_), channel_id=1, source_target_pairs={{0,8},{1,9},{2,10},{3,11},{4,12},{5,13},{6,14},{7,15},{8,16},{9,17... | collective-permute-start | bytes 393224 | tf_op jit(solution)/shard_map/ppermute | solution.py:20
  7.9 7.5 %collective-permute-start.2 = (bf16[256,256]{1,0:T(8,128)(2,1)S(1)}, bf16[256,256]{1,0:T(8,128)(2,1)S(1)}, u32[]{:S(2)}, u32[]{:S(2)}) collective-permute-start(bf16[256,256]{1,0:T(8,128)(2,1)S(1)} %shard_map.86.refs_2_.refs_4_), channel_id=1, source_target_pairs={{0,24},{1,25},{2,26},{3,27},{4,28},{5,29},{6,30},{7,31},{8,0},{9,1... | collective-permute-start | bytes 393224 | tf_op jit(solution)/shard_map/ppermute | solution.py:20
  10.1 5.2 %collective-permute-start.1 = (bf16[256,256]{1,0:T(8,128)(2,1)S(1)}, bf16[256,256]{1,0:T(8,128)(2,1)S(1)}, u32[]{:S(2)}, u32[]{:S(2)}) collective-permute-start(bf16[256,256]{1,0:T(8,128)(2,1)S(1)} %shard_map.86.refs_2_.refs_4_), channel_id=1, source_target_pairs={{0,4},{1,5},{2,6},{3,7},{4,0},{5,1},{6,2},{7,3},{8,12},{9,13},{10,... | collective-permute-start | bytes 393224 | tf_op jit(solution)/shard_map/ppermute | solution.py:20
  10.6 5.0 %collective-permute-start = (bf16[256,256]{1,0:T(8,128)(2,1)S(1)}, bf16[256,256]{1,0:T(8,128)(2,1)S(1)}, u32[]{:S(2)}, u32[]{:S(2)}) collective-permute-start(bf16[256,256]{1,0:T(8,128)(2,1)S(1)} %shard_map.86.refs_2_.refs_4_), channel_id=1, source_target_pairs={{0,2},{1,3},{2,0},{3,1},{4,6},{5,7},{6,4},{7,5},{8,10},{9,11},{10,... | collective-permute-start | bytes 393224 | tf_op jit(solution)/shard_map/ppermute | solution.py:20
  15.7 4.1 %collective-permute-start.8 = (bf16[5,256,256]{2,1,0:T(8,128)(2,1)S(1)}, bf16[5,256,256]{2,1,0:T(8,128)(2,1)S(1)}, u32[]{:S(2)}, u32[]{:S(2)}) collective-permute-start(bf16[5,256,256]{2,1,0:T(8,128)(2,1)S(1)} %get-tuple-element.30.mine), channel_id=1, source_target_pairs={{0,1},{1,0},{2,3},{3,2},{4,5},{5,4},{6,7},{7,6},{8,9},{9,8},{10,11... | collective-permute-start | bytes 1966088 | tf_op jit(solution)/shard_map/ppermute | solution.py:20
  15.7 8.5 %collective-permute-start.5 = (bf16[256,256]{1,0:T(8,128)(2,1)S(1)}, bf16[256,256]{1,0:T(8,128)(2,1)S(1)}, u32[]{:S(2)}, u32[]{:S(2)}) collective-permute-start(bf16[256,256]{1,0:T(8,128)(2,1)S(1)} %get-tuple-element.27), channel_id=1, source_target_pairs={{0,2},{1,3},{2,0},{3,1},{4,6},{5,7},{6,4},{7,5},{8,10},{9,11},{10,... | collective-permute-start | bytes 393224 | tf_op jit(solution)/shard_map/ppermute | solution.py:20
  16.3 7.9 %collective-permute-start.7 = (bf16[256,256]{1,0:T(8,128)(2,1)S(1)}, bf16[256,256]{1,0:T(8,128)(2,1)S(1)}, u32[]{:S(2)}, u32[]{:S(2)}) collective-permute-start(bf16[256,256]{1,0:T(8,128)(2,1)S(1)} %collective-permute-done.4.refs_5_), channel_id=1, source_target_pairs={{0,8},{1,9},{2,10},{3,11},{4,28},{5,29},{6,30},{7,31},{8,16},{9,17... | collective-permute-start | bytes 393224 | tf_op jit(solution)/shard_map/ppermute | solution.py:20
  17.2 7.0 %collective-permute-start.6 = (bf16[256,256]{1,0:T(8,128)(2,1)S(1)}, bf16[256,256]{1,0:T(8,128)(2,1)S(1)}, u32[]{:S(2)}, u32[]{:S(2)}) collective-permute-start(bf16[256,256]{1,0:T(8,128)(2,1)S(1)} %get-tuple-element.28), channel_id=1, source_target_pairs={{0,4},{1,5},{2,6},{3,7},{4,0},{5,1},{6,2},{7,3},{8,12},{9,13},{10,... | collective-permute-start | bytes 393224 | tf_op jit(solution)/shard_map/ppermute | solution.py:20
  24.2 1.4 %collective-permute-start.9 = (bf16[256,256]{1,0:T(8,128)(2,1)S(1)}, bf16[256,256]{1,0:T(8,128)(2,1)S(1)}, u32[]{:S(2)}, u32[]{:S(2)}) collective-permute-start(bf16[256,256]{1,0:T(8,128)(2,1)S(1)} %collective-permute-done.5.refs_3_), channel_id=1, source_target_pairs={{0,1},{1,0},{2,3},{3,2},{4,5},{5,4},{6,7},{7,6},{8,9},{9,8},{10,11... | collective-permute-start | bytes 393224 | tf_op jit(solution)/shard_map/ppermute | solution.py:20
  24.3 1.5 %collective-permute-start.10 = (bf16[256,256]{1,0:T(8,128)(2,1)S(1)}, bf16[256,256]{1,0:T(8,128)(2,1)S(1)}, u32[]{:S(2)}, u32[]{:S(2)}) collective-permute-start(bf16[256,256]{1,0:T(8,128)(2,1)S(1)} %collective-permute-done.6.refs_4_), channel_id=1, source_target_pairs={{0,1},{1,0},{2,3},{3,2},{4,5},{5,4},{6,7},{7,6},{8,9},{9,8},{10,11... | collective-permute-start | bytes 393224 | tf_op jit(solution)/shard_map/ppermute | solution.py:20
  24.8 1.3 %collective-permute-start.11 = (bf16[256,256]{1,0:T(8,128)(2,1)S(1)}, bf16[256,256]{1,0:T(8,128)(2,1)S(1)}, u32[]{:S(2)}, u32[]{:S(2)}) collective-permute-start(bf16[256,256]{1,0:T(8,128)(2,1)S(1)} %collective-permute-done.7.refs_5_), channel_id=1, source_target_pairs={{0,1},{1,0},{2,3},{3,2},{4,5},{5,4},{6,7},{7,6},{8,9},{9,8},{10,11... | collective-permute-start | bytes 393224 | tf_op jit(solution)/shard_map/ppermute | solution.py:20

commit v4 on v3

v4 whole, which is shorter than its diff:
```python
import functools

import jax
import jax.numpy as jnp
from jax import lax
from jax.experimental import pallas as pl
from jax.experimental.pallas import tpu as pltpu
from jax.sharding import PartitionSpec as P

WIN = 8
F32 = jnp.float32
BF16 = jnp.bfloat16
VMEM = pl.BlockSpec(memory_space=pltpu.VMEM)
CHUNKS = 5
SMEM = pl.BlockSpec(memory_space=pltpu.SMEM)
ANY = pl.BlockSpec(memory_space=pl.ANY)
PARAMS = pltpu.CompilerParams(vmem_limit_bytes=4 << 20)


def permuted(value, axis, target):
    count = lax.axis_size(axis)
    return lax.ppermute(value, axis, [(source, target(source)) for source in range(count)])


def swapped(value, axis, bits):
    return permuted(value, axis, lambda source: source ^ bits)


def shifted(value, axis, steps):
    count = lax.axis_size(axis)
    return permuted(value, axis, lambda source: (source + steps) % count)


def top_bit(number):
    return 1 << (number.bit_length() - 1)


def held(*arrays):
    return [pltpu.with_memory_space_constraint(array, pltpu.VMEM) for array in arrays]


def live_square(rank, shape):
    rows = lax.broadcasted_iota(jnp.int32, shape, 0)
    columns = lax.broadcasted_iota(jnp.int32, shape, 1)
    return jnp.maximum(rows, columns) < rank


def cost(count, width):
    return pl.CostEstimate(
        flops=4 * count * width**3, bytes_accessed=4 * count * width**2, transcendentals=0
    )


def mask_kernel(rank, amplitude, masked):
    square = live_square(rank[...], amplitude.shape)
    masked[...] = jnp.where(square, amplitude[...].astype(F32), 0.0).astype(BF16)


def mask(ranks, amplitude):
    return pl.pallas_call(
        mask_kernel,
        out_shape=pltpu.VMEM(amplitude.shape, BF16),
        in_specs=[VMEM, VMEM],
        out_specs=VMEM,
    )(ranks[None], amplitude)


def sides_kernel(axis, before, after, *sides):
    me = lax.axis_index(axis)
    for bits, side in zip((1, 2, 4), sides):
        side[...] = jnp.where((me & bits) != 0, before[...], after[...])


def sides_of(axis, before, after):
    return pl.pallas_call(
        functools.partial(sides_kernel, axis),
        out_shape=(pltpu.VMEM(before.shape, BF16),) * 3,
        in_specs=[VMEM] * 2,
        out_specs=(VMEM,) * 3,
        compiler_params=PARAMS,
    )(*held(before, after))


def stack_kernel(*refs):
    for position, block in enumerate(refs[:-1]):
        refs[-1][position] = block[...]


def stacked(*blocks):
    return pl.pallas_call(
        stack_kernel,
        out_shape=pltpu.VMEM((len(blocks), *blocks[0].shape), BF16),
        in_specs=[VMEM] * len(blocks),
        out_specs=VMEM,
        compiler_params=PARAMS,
    )(*held(*blocks))


def one_term(inter, block, factor):
    half = jnp.dot(inter, block, preferred_element_type=F32).astype(BF16)
    projected = lax.dot_general(
        half, inter, (((1,), (1,)), ((), ())), preferred_element_type=F32
    )
    return factor * projected


def stage_kernel(
    whole, axis, places, neighbours, couplings, rank, energy, masked, inter, integrals,
    total, scale, staged, factor, factors, used, held_integrals, sems, integral_sems,
):
    chunks, span = held_integrals.shape[1:3]
    integral_copies = [
        [
            pltpu.make_async_copy(
                integrals.at[side, pl.ds(chunk * span, span)],
                held_integrals.at[side, chunk],
                integral_sems.at[side, chunk],
            )
            for side in range(2)
        ]
        for chunk in range(chunks)
    ]
    for pair in integral_copies:
        for copy in pair:
            copy.start()
    count = lax.axis_size(axis)
    first = WIN - lax.axis_index(axis)
    slots, blocks = neighbours.shape[1], staged.shape[0]
    for position in range(blocks):
        factors[position] = jnp.float32(0)
        used[position] = 0
    copies = []
    for slot in range(slots):
        step = neighbours[0, slot] + first
        step = jnp.where(step < 0, step + count, step)
        position = places[jnp.where(step >= count, step - count, step)]
        factors[position] = couplings[0, slot]
        used[position] = 1
        copies.append(pltpu.make_async_copy(inter.at[slot], staged.at[position], sems.at[slot]))
        copies[-1].start()
    along = jnp.broadcast_to(energy[...], total.shape)
    denominator = along + along.T
    sum_now = jnp.zeros(total.shape, F32)
    if whole:
        sum_now = denominator * masked[...].astype(F32)
    scale[...] = jnp.where(live_square(rank[...], total.shape), 1.0 / denominator, 0.0)
    for position in range(blocks):

        @pl.when(used[position] == 0)
        def _():
            staged[position] = jnp.zeros(staged.shape[1:], BF16)

        factor[position] = jnp.full(factor.shape[1:], factors[position], F32)
    for chunk, pair in enumerate(integral_copies):
        for copy in pair:
            copy.wait()
        sum_now = sum_now + lax.dot_general(
            held_integrals[0, chunk], held_integrals[1, chunk], (((0,), (0,)), ((), ())),
            preferred_element_type=F32,
        )
    total[...] = sum_now
    for copy in copies:
        copy.wait()


def stage(whole, axis, places, neighbours, couplings, ranks, energies, masked, inter, integrals):
    blocks, width = places.shape[0], masked.shape[0]
    square = pltpu.VMEM((width, width), F32)
    energies, neighbours, couplings, inter, integrals = (
        pltpu.with_memory_space_constraint(array, pltpu.HBM)
        for array in (energies, neighbours, couplings, inter, integrals)
    )
    rows = integrals.shape[1]
    chunks = CHUNKS
    return pl.pallas_call(
        functools.partial(stage_kernel, whole, axis),
        out_shape=(
            square,
            square,
            pltpu.VMEM((blocks, width, width), BF16),
            pltpu.VMEM((blocks, 1, width), F32),
        ),
        in_specs=[SMEM] * 3 + [VMEM] * 3 + [ANY] * 2,
        out_specs=(VMEM,) * 4,
        scratch_shapes=[
            pltpu.SMEM((blocks,), F32),
            pltpu.SMEM((blocks,), jnp.int32),
            pltpu.VMEM((2, chunks, rows // chunks, width), BF16),
            pltpu.SemaphoreType.DMA((neighbours.shape[1],)),
            pltpu.SemaphoreType.DMA((2, chunks)),
        ],
        compiler_params=pltpu.CompilerParams(vmem_limit_bytes=9 << 20),
        cost_estimate=cost(WIN, width),
    )(places, neighbours, couplings, ranks[None], energies, *held(masked), inter, integrals)


def sum_kernel(first, picks, starts, inter, factors, *refs):
    sum_now = refs[0][...]
    for ref in refs[1:starts]:
        sum_now = sum_now + ref[...]
    refs = refs[starts:]
    position = first
    for ref, pick in zip(refs, picks):
        for index in pick:
            block = ref[...] if index is None else ref[index]
            sum_now = sum_now + one_term(inter[position], block, factors[position])
            position += 1
    refs = refs[len(picks) :]
    if len(refs) == 1:
        refs[0][...] = sum_now
    else:
        scale, masked, residual, updated = refs
        residual[...] = jnp.where(scale[...] > 0, sum_now, 0.0)
        updated[...] = masked[...].astype(F32) - sum_now * scale[...]


def block_sum(first, inter, factors, starts, blocks, ending=()):
    shape = starts[0].shape
    out_shape = pltpu.VMEM(shape, F32)
    if ending:
        out_shape = (jax.ShapeDtypeStruct(shape, F32),) * 2
    picks = [pick for _, pick in blocks]
    arrays = held(inter, factors, *starts, *(block for block, _ in blocks), *ending)
    return pl.pallas_call(
        functools.partial(sum_kernel, first, picks, len(starts)),
        out_shape=out_shape,
        in_specs=[VMEM] * len(arrays),
        out_specs=(VMEM, VMEM) if ending else VMEM,
        compiler_params=PARAMS,
        cost_estimate=cost(sum(map(len, picks)) * (1 if ending or first else 32), shape[0]),
    )(*arrays)


def shards(amplitudes, ranks, neighbours, intersections, couplings, energies, pair_factors):
    aux_count = lax.axis_size("aux")
    axis = "pair"
    count = lax.axis_size(axis)
    me = lax.axis_index(axis)
    masked = mask(ranks, amplitudes[0])
    cross = range(2, WIN, 2)

    def far_source(bits):
        other = me ^ bits
        return jnp.where(other > me, other - WIN + count, other + WIN) % count

    sources = [me ^ bits for bits in range(0, WIN, 2)]
    sources += [(me - WIN + count) % count, (me + WIN) % count]
    sources += [far_source(bits) for bits in cross]
    sources += [me ^ bits for bits in range(1, WIN, 2)]
    sources += [far_source(bits) for bits in range(1, WIN, 2)]
    steps = [(source - me + WIN + count) % count for source in sources]
    order = jnp.arange(len(sources), dtype=jnp.int32)
    places = jnp.sum(
        jnp.where(jnp.stack(steps)[:, None] == order[None, :], order[:, None], 0), axis=0
    ).astype(jnp.int32)

    own = {0: masked}
    for bits in reversed(cross):
        own[bits] = swapped(masked, axis, bits)
    after = shifted(masked, axis, -WIN)
    before = shifted(masked, axis, WIN)
    staged = stage(
        aux_count == 1, axis, places, neighbours, couplings, ranks, energies, masked, intersections[0], pair_factors[0]
    )
    before, after = lax.optimization_barrier((before, after))
    total, scale, inter, factors = staged
    side1, side2, side4 = sides_of(axis, before, after)
    far = {bits: swapped(side, axis, bits) for bits, side in ((2, side2), (4, side4), (6, side4))}
    mine = stacked(*(own[bits] for bits in (0, *cross)), side1)
    theirs = swapped(mine, axis, 1)
    one = (None,)
    direct = [own[bits] for bits in (0, *cross)] + [before, after] + [far[bits] for bits in cross]
    direct = [(block, one) for block in direct]
    swaps = [(theirs, tuple(range(WIN // 2 + 1)))]
    late = [(swapped(far[bits], axis, 1), one) for bits in cross]
    total = block_sum(0, inter, factors, [total], direct)
    total = block_sum(len(direct), inter, factors, [total], swaps)
    late_first = len(direct) + WIN // 2 + 1
    if aux_count == 1:
        residual, updated = block_sum(late_first, inter, factors, [total], late, (scale, masked))
        return residual[None], updated[None]

    partial_sum = block_sum(late_first, inter, factors, [total], late)[None]
    pno_width = amplitudes.shape[1]
    row_span = pno_width // aux_count
    first_row = lax.axis_index("aux") * row_span
    live_rows = jnp.arange(pno_width)[None, :] < ranks[:, None]
    square_mask = live_rows[:, :, None] & live_rows[:, None, :]
    summed = lax.psum_scatter(partial_sum, "aux", scatter_dimension=1, tiled=True)
    row_energy = lax.dynamic_slice_in_dim(energies, first_row, row_span, 1)
    denominator = row_energy[:, :, None] + energies[:, None, :]
    row_amp = lax.dynamic_slice_in_dim(masked[None], first_row, row_span, 1).astype(F32)
    row_mask = lax.dynamic_slice_in_dim(square_mask, first_row, row_span, 1)
    residual = jnp.where(row_mask, summed + denominator * row_amp, jnp.zeros((), F32))
    return (residual, row_amp - residual / denominator)


def solution(mesh):
    return jax.shard_map(
        shards,
        mesh=mesh,
        in_specs=(
            P("pair", None, None),
            P("pair"),
            P("pair", "aux"),
            P("pair", "aux", None, None),
            P("pair", "aux"),
            P("pair", None),
            P("pair", None, "aux", None),
        ),
        out_specs=(P("pair", "aux", None), P("pair", "aux", None)),
        check_vma=False,
    )
```

time: 27.6 us -> 26.1 us (0.946)
  matrix products: 3.4 us -> 0 us
  waiting for transfers between devices: 1.82 us -> 3.14 us
  Pallas kernels: 7.41 us -> 8.38 us
  starting transfers between devices: 13.2 us -> 12.9 us
    dot_general x1 -> x0, matrix products: 3.4 us -> none  [shards(): jnp.einsum('qa,qb->ab', factors[0, 0], factors[0, 1], preferred_element_t...]
    ppermute x12, waiting for transfers between devices: 1.82 us -> 3.14 us  [permuted(): lax.ppermute(value, axis, [(source, target(source)) for source in range(c...]
    pallas_call x4 -> x6, Pallas kernels: 6.4 us -> 7.36 us  [the longest x1 4.5 us: stage(): pl.pallas_call(functools.partial(stage_kernel, whole, axis), out_shape=(s...]
    ppermute x12, starting transfers between devices: 13.2 us -> 12.9 us  [permuted(): lax.ppermute(value, axis, [(source, target(source)) for source in range(c...]
  transfers between devices with their start and end apart: 12 -> 12, of which waited for: 6 -> 3; matrix products, arithmetic and copies ran while one was open for 13% -> 1% of each run, Pallas kernels for 18% -> 23%
where the time goes in v4:
time: 26.1 us; the launch traced here: 25.9 us
  starting transfers between devices  12.9 us (49%)
  Pallas kernels  8.38 us (32%)
  waiting for transfers between devices  3.14 us (12%)
  between operations  1.38 us (5%)
    ppermute x12, starting transfers between devices, permuted(): lax.ppermute(value, axis, [(source, target(source)) for source in range(c...  12.9 us
    pallas_call x1, Pallas kernels, stage(): pl.pallas_call(functools.partial(stage_kernel, whole, axis), out_shape=(s...  4.5 us
    ppermute x12, waiting for transfers between devices, permuted(): lax.ppermute(value, axis, [(source, target(source)) for source in range(c...  3.14 us
    pallas_call x3, Pallas kernels, block_sum(): pl.pallas_call(functools.partial(sum_kernel, first, picks, len(starts)),...  2.79 us
    pallas_call x1, Pallas kernels, mask(): pl.pallas_call(mask_kernel, out_shape=pltpu.VMEM(amplitude.shape, BF16),...  1.01 us
  transfers between devices with their start and end apart: 12, of which 3 were waited for; matrix products, arithmetic and copies ran while one was open for 1% of the time, Pallas kernels for 23%

profile of v4, /device:TPU:0, one launch (start us, length us, event | category | flops | bytes accessed | tf_op | source)
XLA Modules:
  0.0 25.9 jit_solution(18157655892793548977)
XLA Ops:
  1.3 1.0 %shard_map.86.masked.refs_1_.refs_0_.refs_5_ = bf16[256,256]{1,0:T(8,128)(2,1)S(1)} custom-call(s32[1,1]{1,0:T(1,128)} %bitcast.22.rank, bf16[256,256]{1,0:T(8,128)(2,1)} %bitcast.26), custom_call_target="tpu_custom_call" | custom-call | tf_op jit(solution)/shard_map/pallas_call | solution.py:60
  2.3 3.1 %collective-permute-start.3 = (bf16[256,256]{1,0:T(8,128)(2,1)S(1)}, bf16[256,256]{1,0:T(8,128)(2,1)S(1)}, u32[]{:S(2)}, u32[]{:S(2)}) collective-permute-start(bf16[256,256]{1,0:T(8,128)(2,1)S(1)} %shard_map.86.masked.refs_1_.refs_0_.refs_5_), channel_id=1, source_target_pairs={{0,8},{1,9},{2,10},{3,11},{4,12},{5,13},{6,14},{7,15},{8,16},{9,17... | collective-permute-start | bytes 393224 | tf_op jit(solution)/shard_map/ppermute | solution.py:22
  5.4 2.1 %collective-permute-start.4 = (bf16[256,256]{1,0:T(8,128)(2,1)S(1)}, bf16[256,256]{1,0:T(8,128)(2,1)S(1)}, u32[]{:S(2)}, u32[]{:S(2)}) collective-permute-start(bf16[256,256]{1,0:T(8,128)(2,1)S(1)} %shard_map.86.masked.refs_1_.refs_0_.refs_5_), channel_id=1, source_target_pairs={{0,24},{1,25},{2,26},{3,27},{4,28},{5,29},{6,30},{7,31},{8,0},{9,1... | collective-permute-start | bytes 393224 | tf_op jit(solution)/shard_map/ppermute | solution.py:22
  7.5 1.6 %collective-permute-start = (bf16[256,256]{1,0:T(8,128)(2,1)S(1)}, bf16[256,256]{1,0:T(8,128)(2,1)S(1)}, u32[]{:S(2)}, u32[]{:S(2)}) collective-permute-start(bf16[256,256]{1,0:T(8,128)(2,1)S(1)} %shard_map.86.masked.refs_1_.refs_0_.refs_5_), channel_id=1, source_target_pairs={{0,2},{1,3},{2,0},{3,1},{4,6},{5,7},{6,4},{7,5},{8,10},{9,11},{10,... | collective-permute-start | bytes 393224 | tf_op jit(solution)/shard_map/ppermute | solution.py:22
  9.1 1.5 %collective-permute-start.1 = (bf16[256,256]{1,0:T(8,128)(2,1)S(1)}, bf16[256,256]{1,0:T(8,128)(2,1)S(1)}, u32[]{:S(2)}, u32[]{:S(2)}) collective-permute-start(bf16[256,256]{1,0:T(8,128)(2,1)S(1)} %shard_map.86.masked.refs_1_.refs_0_.refs_5_), channel_id=1, source_target_pairs={{0,4},{1,5},{2,6},{3,7},{4,0},{5,1},{6,2},{7,3},{8,12},{9,13},{10,... | collective-permute-start | bytes 393224 | tf_op jit(solution)/shard_map/ppermute | solution.py:22
  10.6 0.3 %collective-permute-start.2 = (bf16[256,256]{1,0:T(8,128)(2,1)S(1)}, bf16[256,256]{1,0:T(8,128)(2,1)S(1)}, u32[]{:S(2)}, u32[]{:S(2)}) collective-permute-start(bf16[256,256]{1,0:T(8,128)(2,1)S(1)} %shard_map.86.masked.refs_1_.refs_0_.refs_5_), channel_id=1, source_target_pairs={{0,6},{1,7},{2,4},{3,5},{4,2},{5,3},{6,0},{7,1},{8,14},{9,15},{10,... | collective-permute-start | bytes 393224 | tf_op jit(solution)/shard_map/ppermute | solution.py:22
  10.9 0.1 stack.68
  11.0 0.7 %collective-permute-done.3.before.refs_5_ = bf16[256,256]{1,0:T(8,128)(2,1)S(1)} collective-permute-done((bf16[256,256]{1,0:T(8,128)(2,1)S(1)}, bf16[256,256]{1,0:T(8,128)(2,1)S(1)}, u32[]{:S(2)}, u32[]{:S(2)}) %collective-permute-start.3) | collective-permute-done | bytes 131104 | tf_op jit(solution)/shard_map/ppermute | solution.py:22
  11.7 1.4 %collective-permute-done.4.after.refs_6_ = bf16[256,256]{1,0:T(8,128)(2,1)S(1)} collective-permute-done((bf16[256,256]{1,0:T(8,128)(2,1)S(1)}, bf16[256,256]{1,0:T(8,128)(2,1)S(1)}, u32[]{:S(2)}, u32[]{:S(2)}) %collective-permute-start.4) | collective-permute-done | bytes 131104 | tf_op jit(solution)/shard_map/ppermute | solution.py:22
  13.2 1.6 %collective-permute-start.6 = (bf16[256,256]{1,0:T(8,128)(2,1)S(1)}, bf16[256,256]{1,0:T(8,128)(2,1)S(1)}, u32[]{:S(2)}, u32[]{:S(2)}) collective-permute-start(bf16[256,256]{1,0:T(8,128)(2,1)S(1)} %get-tuple-element.19), channel_id=1, source_target_pairs={{0,4},{1,5},{2,6},{3,7},{4,0},{5,1},{6,2},{7,3},{8,12},{9,13},{10,... | collective-permute-start | bytes 393224 | tf_op jit(solution)/shard_map/ppermute | solution.py:22
  14.8 1.4 %collective-permute-start.7 = (bf16[256,256]{1,0:T(8,128)(2,1)S(1)}, bf16[256,256]{1,0:T(8,128)(2,1)S(1)}, u32[]{:S(2)}, u32[]{:S(2)}) collective-permute-start(bf16[256,256]{1,0:T(8,128)(2,1)S(1)} %get-tuple-element.19), channel_id=1, source_target_pairs={{0,6},{1,7},{2,4},{3,5},{4,2},{5,3},{6,0},{7,1},{8,14},{9,15},{10,... | collective-permute-start | bytes 393224 | tf_op jit(solution)/shard_map/ppermute | solution.py:22
  16.2 0.0 collective-permute-done.refs_2_.refs_1_
  16.2 0.5 %collective-permute-start.5 = (bf16[256,256]{1,0:T(8,128)(2,1)S(1)}, bf16[256,256]{1,0:T(8,128)(2,1)S(1)}, u32[]{:S(2)}, u32[]{:S(2)}) collective-permute-start(bf16[256,256]{1,0:T(8,128)(2,1)S(1)} %get-tuple-element.18), channel_id=1, source_target_pairs={{0,2},{1,3},{2,0},{3,1},{4,6},{5,7},{6,4},{7,5},{8,10},{9,11},{10,... | collective-permute-start | bytes 393224 | tf_op jit(solution)/shard_map/ppermute | solution.py:22
  16.7 0.1 select_reduce_fusion.places
  16.8 4.5 %shard_map.87 = (f32[256,256]{1,0:T(8,128)S(1)}, f32[256,256]{1,0:T(8,128)S(1)}, bf16[17,256,256]{2,1,0:T(8,128)(2,1)S(1)}, f32[17,1,256]{2,1,0:T(1,128)S(1)}) custom-call(s32[17]{0:T(128)S(1)} %select_reduce_fusion.places, s32[1,16]{1,0:T(1,128)} %neighbours.1, f32[1,16]{1,0:T(1,128)} %couplings.1, s32[1,1]{1,0:T(1,128)} %bitcast.23.rank, f32[1,256]{1,0:T(1,128)} %energy.1, ...), custom_call_target="tpu_custom_call" | custom-call | flops 536870912 | bytes 2097152 | tf_op jit(solution)/shard_map/pallas_call | solution.py:175
  21.3 0.0 collective-permute-done.1.refs_3_.refs_2_
  21.3 0.0 collective-permute-done.2.refs_4_.refs_3_
  21.4 0.1 collective-permute-start.8
  21.5 1.0 %collective-permute-done.6.refs_8_ = bf16[256,256]{1,0:T(8,128)(2,1)S(1)} collective-permute-done((bf16[256,256]{1,0:T(8,128)(2,1)S(1)}, bf16[256,256]{1,0:T(8,128)(2,1)S(1)}, u32[]{:S(2)}, u32[]{:S(2)}) %collective-permute-start.6) | collective-permute-done | bytes 131104 | tf_op jit(solution)/shard_map/ppermute | solution.py:22
  22.5 0.0 collective-permute-start.10
  22.5 0.0 collective-permute-done.7.refs_9_
  22.5 0.5 %collective-permute-start.11 = (bf16[256,256]{1,0:T(8,128)(2,1)S(1)}, bf16[256,256]{1,0:T(8,128)(2,1)S(1)}, u32[]{:S(2)}, u32[]{:S(2)}) collective-permute-start(bf16[256,256]{1,0:T(8,128)(2,1)S(1)} %collective-permute-done.7.refs_9_), channel_id=1, source_target_pairs={{0,1},{1,0},{2,3},{3,2},{4,5},{5,4},{6,7},{7,6},{8,9},{9,8},{10,11... | collective-permute-start | bytes 393224 | tf_op jit(solution)/shard_map/ppermute | solution.py:22
  23.0 0.0 collective-permute-done.5.refs_7_
  23.0 0.1 collective-permute-start.9
  23.1 0.9 %shard_map.89.refs_0_ = f32[256,256]{1,0:T(8,128)S(1)} custom-call(bf16[17,256,256]{2,1,0:T(8,128)(2,1)S(1)} %get-tuple-element.13.inter, f32[17,1,256]{2,1,0:T(1,128)S(1)} %get-tuple-element.14.factors, f32[256,256]{1,0:T(8,128)S(1)} %get-tuple-element.15.refs_0_, bf16[256,256]{1,0:T(8,128)(2,1)S(1)} %shard_map.86.masked.refs_1_.refs_0_.refs_5_, ...), custom_call_target="tpu_custom_call" | custom-call | flops 19327352832 | bytes 75497472 | tf_op jit(solution)/shard_map/pallas_call | solution.py:224
  24.0 0.0 collective-permute-done.8.refs_1_
  24.0 0.6 %shard_map.91.refs_0_ = f32[256,256]{1,0:T(8,128)S(1)} custom-call(bf16[17,256,256]{2,1,0:T(8,128)(2,1)S(1)} %get-tuple-element.13.inter, f32[17,1,256]{2,1,0:T(1,128)S(1)} %get-tuple-element.14.factors, f32[256,256]{1,0:T(8,128)S(1)} %shard_map.89.refs_0_, bf16[5,256,256]{2,1,0:T(8,128)(2,1)S(1)} %collective-permute-done.8.refs_1_), custom_call_target="tpu_custom_call" | custom-call | flops 335544320 | bytes 1310720 | tf_op jit(solution)/shard_map/pallas_call | solution.py:224
  24.6 0.0 collective-permute-done.10.refs_2_
  24.6 0.0 collective-permute-done.11.refs_3_
  24.6 0.0 collective-permute-done.9.refs_1_
  24.7 1.3 %shard_map.92 = (f32[256,256]{1,0:T(8,128)}, f32[256,256]{1,0:T(8,128)}) custom-call(bf16[17,256,256]{2,1,0:T(8,128)(2,1)S(1)} %get-tuple-element.13.inter, f32[17,1,256]{2,1,0:T(1,128)S(1)} %get-tuple-element.14.factors, f32[256,256]{1,0:T(8,128)S(1)} %shard_map.91.refs_0_, bf16[256,256]{1,0:T(8,128)(2,1)S(1)} %collective-permute-done.9.refs_1_, ...), custom_call_target="tpu_custom_call" | custom-call | flops 201326592 | bytes 786432 | tf_op jit(solution)/shard_map/pallas_call | solution.py:224
  (2 shorter events, 0.1 us)
Async XLA Ops:
  2.3 9.4 %collective-permute-start.3 = (bf16[256,256]{1,0:T(8,128)(2,1)S(1)}, bf16[256,256]{1,0:T(8,128)(2,1)S(1)}, u32[]{:S(2)}, u32[]{:S(2)}) collective-permute-start(bf16[256,256]{1,0:T(8,128)(2,1)S(1)} %shard_map.86.masked.refs_1_.refs_0_.refs_5_), channel_id=1, source_target_pairs={{0,8},{1,9},{2,10},{3,11},{4,12},{5,13},{6,14},{7,15},{8,16},{9,17... | collective-permute-start | bytes 393224 | tf_op jit(solution)/shard_map/ppermute | solution.py:22
  5.4 7.8 %collective-permute-start.4 = (bf16[256,256]{1,0:T(8,128)(2,1)S(1)}, bf16[256,256]{1,0:T(8,128)(2,1)S(1)}, u32[]{:S(2)}, u32[]{:S(2)}) collective-permute-start(bf16[256,256]{1,0:T(8,128)(2,1)S(1)} %shard_map.86.masked.refs_1_.refs_0_.refs_5_), channel_id=1, source_target_pairs={{0,24},{1,25},{2,26},{3,27},{4,28},{5,29},{6,30},{7,31},{8,0},{9,1... | collective-permute-start | bytes 393224 | tf_op jit(solution)/shard_map/ppermute | solution.py:22
  7.5 8.7 %collective-permute-start = (bf16[256,256]{1,0:T(8,128)(2,1)S(1)}, bf16[256,256]{1,0:T(8,128)(2,1)S(1)}, u32[]{:S(2)}, u32[]{:S(2)}) collective-permute-start(bf16[256,256]{1,0:T(8,128)(2,1)S(1)} %shard_map.86.masked.refs_1_.refs_0_.refs_5_), channel_id=1, source_target_pairs={{0,2},{1,3},{2,0},{3,1},{4,6},{5,7},{6,4},{7,5},{8,10},{9,11},{10,... | collective-permute-start | bytes 393224 | tf_op jit(solution)/shard_map/ppermute | solution.py:22
  9.1 12.2 %collective-permute-start.1 = (bf16[256,256]{1,0:T(8,128)(2,1)S(1)}, bf16[256,256]{1,0:T(8,128)(2,1)S(1)}, u32[]{:S(2)}, u32[]{:S(2)}) collective-permute-start(bf16[256,256]{1,0:T(8,128)(2,1)S(1)} %shard_map.86.masked.refs_1_.refs_0_.refs_5_), channel_id=1, source_target_pairs={{0,4},{1,5},{2,6},{3,7},{4,0},{5,1},{6,2},{7,3},{8,12},{9,13},{10,... | collective-permute-start | bytes 393224 | tf_op jit(solution)/shard_map/ppermute | solution.py:22
  10.6 10.7 %collective-permute-start.2 = (bf16[256,256]{1,0:T(8,128)(2,1)S(1)}, bf16[256,256]{1,0:T(8,128)(2,1)S(1)}, u32[]{:S(2)}, u32[]{:S(2)}) collective-permute-start(bf16[256,256]{1,0:T(8,128)(2,1)S(1)} %shard_map.86.masked.refs_1_.refs_0_.refs_5_), channel_id=1, source_target_pairs={{0,6},{1,7},{2,4},{3,5},{4,2},{5,3},{6,0},{7,1},{8,14},{9,15},{10,... | collective-permute-start | bytes 393224 | tf_op jit(solution)/shard_map/ppermute | solution.py:22
  13.2 9.3 %collective-permute-start.6 = (bf16[256,256]{1,0:T(8,128)(2,1)S(1)}, bf16[256,256]{1,0:T(8,128)(2,1)S(1)}, u32[]{:S(2)}, u32[]{:S(2)}) collective-permute-start(bf16[256,256]{1,0:T(8,128)(2,1)S(1)} %get-tuple-element.19), channel_id=1, source_target_pairs={{0,4},{1,5},{2,6},{3,7},{4,0},{5,1},{6,2},{7,3},{8,12},{9,13},{10,... | collective-permute-start | bytes 393224 | tf_op jit(solution)/shard_map/ppermute | solution.py:22
  14.8 7.8 %collective-permute-start.7 = (bf16[256,256]{1,0:T(8,128)(2,1)S(1)}, bf16[256,256]{1,0:T(8,128)(2,1)S(1)}, u32[]{:S(2)}, u32[]{:S(2)}) collective-permute-start(bf16[256,256]{1,0:T(8,128)(2,1)S(1)} %get-tuple-element.19), channel_id=1, source_target_pairs={{0,6},{1,7},{2,4},{3,5},{4,2},{5,3},{6,0},{7,1},{8,14},{9,15},{10,... | collective-permute-start | bytes 393224 | tf_op jit(solution)/shard_map/ppermute | solution.py:22
  16.2 6.8 %collective-permute-start.5 = (bf16[256,256]{1,0:T(8,128)(2,1)S(1)}, bf16[256,256]{1,0:T(8,128)(2,1)S(1)}, u32[]{:S(2)}, u32[]{:S(2)}) collective-permute-start(bf16[256,256]{1,0:T(8,128)(2,1)S(1)} %get-tuple-element.18), channel_id=1, source_target_pairs={{0,2},{1,3},{2,0},{3,1},{4,6},{5,7},{6,4},{7,5},{8,10},{9,11},{10,... | collective-permute-start | bytes 393224 | tf_op jit(solution)/shard_map/ppermute | solution.py:22
  21.4 2.6 %collective-permute-start.8 = (bf16[5,256,256]{2,1,0:T(8,128)(2,1)S(1)}, bf16[5,256,256]{2,1,0:T(8,128)(2,1)S(1)}, u32[]{:S(2)}, u32[]{:S(2)}) collective-permute-start(bf16[5,256,256]{2,1,0:T(8,128)(2,1)S(1)} %shard_map.90), channel_id=1, source_target_pairs={{0,1},{1,0},{2,3},{3,2},{4,5},{5,4},{6,7},{7,6},{8,9},{9,8},{10,11... | collective-permute-start | bytes 1966088 | tf_op jit(solution)/shard_map/ppermute | solution.py:22
  22.5 2.1 %collective-permute-start.10 = (bf16[256,256]{1,0:T(8,128)(2,1)S(1)}, bf16[256,256]{1,0:T(8,128)(2,1)S(1)}, u32[]{:S(2)}, u32[]{:S(2)}) collective-permute-start(bf16[256,256]{1,0:T(8,128)(2,1)S(1)} %collective-permute-done.6.refs_8_), channel_id=1, source_target_pairs={{0,1},{1,0},{2,3},{3,2},{4,5},{5,4},{6,7},{7,6},{8,9},{9,8},{10,11... | collective-permute-start | bytes 393224 | tf_op jit(solution)/shard_map/ppermute | solution.py:22
  22.5 2.1 %collective-permute-start.11 = (bf16[256,256]{1,0:T(8,128)(2,1)S(1)}, bf16[256,256]{1,0:T(8,128)(2,1)S(1)}, u32[]{:S(2)}, u32[]{:S(2)}) collective-permute-start(bf16[256,256]{1,0:T(8,128)(2,1)S(1)} %collective-permute-done.7.refs_9_), channel_id=1, source_target_pairs={{0,1},{1,0},{2,3},{3,2},{4,5},{5,4},{6,7},{7,6},{8,9},{9,8},{10,11... | collective-permute-start | bytes 393224 | tf_op jit(solution)/shard_map/ppermute | solution.py:22
  23.0 1.6 %collective-permute-start.9 = (bf16[256,256]{1,0:T(8,128)(2,1)S(1)}, bf16[256,256]{1,0:T(8,128)(2,1)S(1)}, u32[]{:S(2)}, u32[]{:S(2)}) collective-permute-start(bf16[256,256]{1,0:T(8,128)(2,1)S(1)} %collective-permute-done.5.refs_7_), channel_id=1, source_target_pairs={{0,1},{1,0},{2,3},{3,2},{4,5},{5,4},{6,7},{7,6},{8,9},{9,8},{10,11... | collective-permute-start | bytes 393224 | tf_op jit(solution)/shard_map/ppermute | solution.py:22

commit v5 on v4

--- a/solution.py
+++ b/solution.py
@@ -12,6 +12,9 @@
 BF16 = jnp.bfloat16
 VMEM = pl.BlockSpec(memory_space=pltpu.VMEM)
 CHUNKS = 5
+STAGE_COST = 8
+EXCHANGE_COST = 8
+TILE = (8, 128)
 SMEM = pl.BlockSpec(memory_space=pltpu.SMEM)
 ANY = pl.BlockSpec(memory_space=pl.ANY)
 PARAMS = pltpu.CompilerParams(vmem_limit_bytes=4 << 20)
@@ -51,17 +54,18 @@
     )
 
 
-def mask_kernel(rank, amplitude, masked):
+def mask_kernel(rank, amplitude, masked, tile):
     square = live_square(rank[...], amplitude.shape)
     masked[...] = jnp.where(square, amplitude[...].astype(F32), 0.0).astype(BF16)
+    tile[...] = jnp.broadcast_to(rank[...], tile.shape)
 
 
 def mask(ranks, amplitude):
     return pl.pallas_call(
         mask_kernel,
-        out_shape=pltpu.VMEM(amplitude.shape, BF16),
+        out_shape=(pltpu.VMEM(amplitude.shape, BF16), pltpu.VMEM(TILE, jnp.int32)),
         in_specs=[VMEM, VMEM],
-        out_specs=VMEM,
+        out_specs=(VMEM, VMEM),
     )(ranks[None], amplitude)
 
 
@@ -79,6 +83,21 @@
         out_specs=(VMEM,) * 3,
         compiler_params=PARAMS,
     )(*held(before, after))
+
+
+def pass_kernel(block, again):
+    again[...] = block[...]
+
+
+def passed(block, weight):
+    return pl.pallas_call(
+        pass_kernel,
+        out_shape=pltpu.VMEM(block.shape, BF16),
+        in_specs=[VMEM],
+        out_specs=VMEM,
+        compiler_params=PARAMS,
+        cost_estimate=cost(weight, block.shape[0]),
+    )(*held(block))
 
 
 def stack_kernel(*refs):
@@ -104,54 +123,119 @@
     return factor * projected
 
 
+def far_step(me, bits):
+    other = me ^ bits
+    return jnp.where(other > me, other - me, other - me + 2 * WIN)
+
+
+def block_steps(me):
+    cross = range(2, WIN, 2)
+    steps = [(me ^ bits) - me + WIN for bits in (0, *cross)]
+    steps += [0, 2 * WIN]
+    steps += [far_step(me, bits) for bits in cross]
+    steps += [(me ^ bits) - me + WIN for bits in range(1, WIN, 2)]
+    return steps + [far_step(me, bits) for bits in range(1, WIN, 2)]
+
+
 def stage_kernel(
-    whole, axis, places, neighbours, couplings, rank, energy, masked, inter, integrals,
-    total, scale, staged, factor, factors, used, held_integrals, sems, integral_sems,
+    whole, axis, rank, masked, neighbours, couplings, energies, inter,
+    total, scale, staged, factor,
+    near, couple, energy, places, factors, used, small_sems, sems,
 ):
+    small_copies = [
+        pltpu.make_async_copy(source, target, small_sems.at[k])
+        for k, (source, target) in enumerate(
+            ((neighbours, near), (couplings, couple), (energies, energy))
+        )
+    ]
+    for copy in small_copies:
+        copy.start()
+    count = lax.axis_size(axis)
+    me = lax.axis_index(axis)
+    slots, blocks = near.shape[1], staged.shape[0]
+    for position, step in enumerate(block_steps(me)):
+        places[step] = position
+        factors[position] = jnp.float32(0)
+        used[position] = 0
+    for copy in small_copies:
+        copy.wait()
+    copies = []
+    for slot in range(slots):
+        step = near[0, slot] - me + WIN
+        step = jnp.where(step < 0, step + count, step)
+        position = places[jnp.where(step >= count, step - count, step)]
+        factors[position] = couple[0, slot]
+        used[position] = 1
+        copies.append(pltpu.make_async_copy(inter.at[slot], staged.at[position], sems.at[slot]))
+        copies[-1].start()
+    along = jnp.broadcast_to(energy[...], total.shape)
+    denominator = along + along.T
+    if whole:
+        total[...] = denominator * masked[...].astype(F32)
+    else:
+        total[...] = jnp.zeros_like(total)
+    scale[...] = jnp.where(live_square(rank[0:1, 0:1], total.shape), 1.0 / denominator, 0.0)
+    for position in range(blocks):
+
+        @pl.when(used[position] == 0)
+        def _():
+            staged[position] = jnp.zeros(staged.shape[1:], BF16)
+
+        factor[position] = jnp.full(factor.shape[1:], factors[position], F32)
+    for copy in copies:
+        copy.wait()
+
+
+def stage(whole, axis, rank, masked, neighbours, couplings, energies, inter):
+    blocks, width = 2 * WIN + 1, masked.shape[0]
+    square = pltpu.VMEM((width, width), F32)
+    arrays = [
+        pltpu.with_memory_space_constraint(array, pltpu.HBM)
+        for array in (neighbours, couplings, energies, inter)
+    ]
+    return pl.pallas_call(
+        functools.partial(stage_kernel, whole, axis),
+        out_shape=(
+            square,
+            square,
+            pltpu.VMEM((blocks, width, width), BF16),
+            pltpu.VMEM((blocks, 1, width), F32),
+        ),
+        in_specs=[VMEM] * 2 + [ANY] * len(arrays),
+        out_specs=(VMEM,) * 4,
+        scratch_shapes=[
+            pltpu.SMEM(neighbours.shape, jnp.int32),
+            pltpu.SMEM(couplings.shape, F32),
+            pltpu.VMEM(energies.shape, F32),
+            pltpu.SMEM((blocks,), jnp.int32),
+            pltpu.SMEM((blocks,), F32),
+            pltpu.SMEM((blocks,), jnp.int32),
+            pltpu.SemaphoreType.DMA((3,)),
+            pltpu.SemaphoreType.DMA((neighbours.shape[1],)),
+        ],
+        compiler_params=PARAMS,
+        cost_estimate=cost(STAGE_COST, width),
+    )(*held(rank, masked), *arrays)
+
+
+def exchange_kernel(integrals, total, held_integrals, sems):
     chunks, span = held_integrals.shape[1:3]
-    integral_copies = [
+    copies = [
         [
             pltpu.make_async_copy(
                 integrals.at[side, pl.ds(chunk * span, span)],
                 held_integrals.at[side, chunk],
-                integral_sems.at[side, chunk],
+                sems.at[side, chunk],
             )
             for side in range(2)
         ]
         for chunk in range(chunks)
     ]
-    for pair in integral_copies:
+    for pair in copies:
         for copy in pair:
             copy.start()
-    count = lax.axis_size(axis)
-    first = WIN - lax.axis_index(axis)
-    slots, blocks = neighbours.shape[1], staged.shape[0]
-    for position in range(blocks):
-        factors[position] = jnp.float32(0)
-        used[position] = 0
-    copies = []
-    for slot in range(slots):
-        step = neighbours[0, slot] + first
-        step = jnp.where(step < 0, step + count, step)
-        position = places[jnp.where(step >= count, step - count, step)]
-        factors[position] = couplings[0, slot]
-        used[position] = 1
-        copies.append(pltpu.make_async_copy(inter.at[slot], staged.at[position], sems.at[slot]))
-        copies[-1].start()
-    along = jnp.broadcast_to(energy[...], total.shape)
-    denominator = along + along.T
     sum_now = jnp.zeros(total.shape, F32)
-    if whole:
-        sum_now = denominator * masked[...].astype(F32)
-    scale[...] = jnp.where(live_square(rank[...], total.shape), 1.0 / denominator, 0.0)
-    for position in range(blocks):
-
-        @pl.when(used[position] == 0)
-        def _():
-            staged[position] = jnp.zeros(staged.shape[1:], BF16)
-
-        factor[position] = jnp.full(factor.shape[1:], factors[position], F32)
-    for chunk, pair in enumerate(integral_copies):
+    for chunk, pair in enumerate(copies):
         for copy in pair:
             copy.wait()
         sum_now = sum_now + lax.dot_general(
@@ -159,39 +243,23 @@
             preferred_element_type=F32,
         )
     total[...] = sum_now
-    for copy in copies:
-        copy.wait()
-
-
-def stage(whole, axis, places, neighbours, couplings, ranks, energies, masked, inter, integrals):
-    blocks, width = places.shape[0], masked.shape[0]
-    square = pltpu.VMEM((width, width), F32)
-    energies, neighbours, couplings, inter, integrals = (
-        pltpu.with_memory_space_constraint(array, pltpu.HBM)
-        for array in (energies, neighbours, couplings, inter, integrals)
-    )
-    rows = integrals.shape[1]
-    chunks = CHUNKS
-    return pl.pallas_call(
-        functools.partial(stage_kernel, whole, axis),
-        out_shape=(
-            square,
-            square,
-            pltpu.VMEM((blocks, width, width), BF16),
-            pltpu.VMEM((blocks, 1, width), F32),
-        ),
-        in_specs=[SMEM] * 3 + [VMEM] * 3 + [ANY] * 2,
-        out_specs=(VMEM,) * 4,
+
+
+def exchange_of(integrals):
+    rows, width = integrals.shape[1:]
+    integrals = pltpu.with_memory_space_constraint(integrals, pltpu.HBM)
+    return pl.pallas_call(
+        exchange_kernel,
+        out_shape=pltpu.VMEM((width, width), F32),
+        in_specs=[ANY],
+        out_specs=VMEM,
         scratch_shapes=[
-            pltpu.SMEM((blocks,), F32),
-            pltpu.SMEM((blocks,), jnp.int32),
-            pltpu.VMEM((2, chunks, rows // chunks, width), BF16),
-            pltpu.SemaphoreType.DMA((neighbours.shape[1],)),
-            pltpu.SemaphoreType.DMA((2, chunks)),
+            pltpu.VMEM((2, CHUNKS, rows // CHUNKS, width), BF16),
+            pltpu.SemaphoreType.DMA((2, CHUNKS)),
         ],
-        compiler_params=pltpu.CompilerParams(vmem_limit_bytes=9 << 20),
-        cost_estimate=cost(WIN, width),
-    )(places, neighbours, couplings, ranks[None], energies, *held(masked), inter, integrals)
+        compiler_params=pltpu.CompilerParams(vmem_limit_bytes=8 << 20),
+        cost_estimate=cost(EXCHANGE_COST, width),
+    )(integrals)
 
 
 def sum_kernel(first, picks, starts, inter, factors, *refs):
@@ -235,37 +303,24 @@
     aux_count = lax.axis_size("aux")
     axis = "pair"
     count = lax.axis_size(axis)
-    me = lax.axis_index(axis)
-    masked = mask(ranks, amplitudes[0])
+    masked, rank = mask(ranks, amplitudes[0])
     cross = range(2, WIN, 2)
-
-    def far_source(bits):
-        other = me ^ bits
-        return jnp.where(other > me, other - WIN + count, other + WIN) % count
-
-    sources = [me ^ bits for bits in range(0, WIN, 2)]
-    sources += [(me - WIN + count) % count, (me + WIN) % count]
-    sources += [far_source(bits) for bits in cross]
-    sources += [me ^ bits for bits in range(1, WIN, 2)]
-    sources += [far_source(bits) for bits in range(1, WIN, 2)]
-    steps = [(source - me + WIN + count) % count for source in sources]
-    order = jnp.arange(len(sources), dtype=jnp.int32)
-    places = jnp.sum(
-        jnp.where(jnp.stack(steps)[:, None] == order[None, :], order[:, None], 0), axis=0
-    ).astype(jnp.int32)
 
     own = {0: masked}
     for bits in reversed(cross):
         own[bits] = swapped(masked, axis, bits)
+    own[6] = passed(own[6], 4)
     after = shifted(masked, axis, -WIN)
     before = shifted(masked, axis, WIN)
     staged = stage(
-        aux_count == 1, axis, places, neighbours, couplings, ranks, energies, masked, intersections[0], pair_factors[0]
+        aux_count == 1, axis, rank, masked, neighbours, couplings, energies, intersections[0]
     )
-    before, after = lax.optimization_barrier((before, after))
+    exchange = exchange_of(pair_factors[0])
+    before, after, staged = lax.optimization_barrier((before, after, staged))
     total, scale, inter, factors = staged
     side1, side2, side4 = sides_of(axis, before, after)
     far = {bits: swapped(side, axis, bits) for bits, side in ((2, side2), (4, side4), (6, side4))}
+    far[6] = passed(far[6], 4)
     mine = stacked(*(own[bits] for bits in (0, *cross)), side1)
     theirs = swapped(mine, axis, 1)
     one = (None,)
@@ -273,7 +328,7 @@
     direct = [(block, one) for block in direct]
     swaps = [(theirs, tuple(range(WIN // 2 + 1)))]
     late = [(swapped(far[bits], axis, 1), one) for bits in cross]
-    total = block_sum(0, inter, factors, [total], direct)
+    total = block_sum(0, inter, factors, [exchange, total], direct)
     total = block_sum(len(direct), inter, factors, [total], swaps)
     late_first = len(direct) + WIN // 2 + 1
     if aux_count == 1:

time: 26.1 us -> 25.3 us (0.969)
  waiting for transfers between devices: 3.14 us -> 0.8 us
  Pallas kernels: 8.38 us -> 9.64 us
  starting transfers between devices: 12.9 us -> 13.3 us
    pallas_call x1 -> x4, Pallas kernels: 1.01 us -> 4.31 us  [the longest x1 3.28 us: exchange_of(): pl.pallas_call(exchange_kernel, out_shape=pltpu.VMEM((width, width), F32)...]
    ppermute x12, waiting for transfers between devices: 3.14 us -> 0.8 us  [permuted(): lax.ppermute(value, axis, [(source, target(source)) for source in range(c...]
    pallas_call x1, Pallas kernels: 4.5 us -> 2.48 us  [stage(): pl.pallas_call(functools.partial(stage_kernel, whole, axis), out_shape=(s...]
    ppermute x12, starting transfers between devices: 12.9 us -> 13.3 us  [permuted(): lax.ppermute(value, axis, [(source, target(source)) for source in range(c...]
  transfers between devices with their start and end apart: 12 -> 12, of which waited for: 3 -> 2; matrix products, arithmetic and copies ran while one was open for 1% -> 0% of each run, Pallas kernels for 23% -> 29%
where the time goes in v5:
time: 25.3 us; the launch traced here: 25.1 us
  starting transfers between devices  13.3 us (53%)
  Pallas kernels  9.64 us (38%)
  between operations  1.43 us (6%)
  waiting for transfers between devices  0.8 us (3%)
    ppermute x12, starting transfers between devices, permuted(): lax.ppermute(value, axis, [(source, target(source)) for source in range(c...  13.3 us
    pallas_call x1, Pallas kernels, exchange_of(): pl.pallas_call(exchange_kernel, out_shape=pltpu.VMEM((width, width), F32)...  3.28 us
    pallas_call x3, Pallas kernels, block_sum(): pl.pallas_call(functools.partial(sum_kernel, first, picks, len(starts)),...  2.77 us
    pallas_call x1, Pallas kernels, stage(): pl.pallas_call(functools.partial(stage_kernel, whole, axis), out_shape=(s...  2.48 us
    pallas_call x1, Pallas kernels, mask(): pl.pallas_call(mask_kernel, out_shape=(pltpu.VMEM(amplitude.shape, BF16),...  1.01 us
    ppermute x12, waiting for transfers between devices, permuted(): lax.ppermute(value, axis, [(source, target(source)) for source in range(c...  0.8 us
  transfers between devices with their start and end apart: 12, of which 2 were waited for; matrix products, arithmetic and copies ran while one was open for 0% of the time, Pallas kernels for 29%

profile of v5, /device:TPU:0, one launch (start us, length us, event | category | flops | bytes accessed | tf_op | source)
XLA Modules:
  0.0 25.1 jit_solution(9277193438181537529)
XLA Ops:
  1.3 1.0 %shard_map.86 = (bf16[256,256]{1,0:T(8,128)(2,1)S(1)}, s32[8,128]{1,0:T(8,128)S(1)}) custom-call(s32[1,1]{1,0:T(1,128)} %bitcast.6.rank, bf16[256,256]{1,0:T(8,128)(2,1)} %bitcast.9), custom_call_target="tpu_custom_call" | custom-call | tf_op jit(solution)/shard_map/pallas_call | solution.py:64
  2.3 3.1 %collective-permute-start = (bf16[256,256]{1,0:T(8,128)(2,1)S(1)}, bf16[256,256]{1,0:T(8,128)(2,1)S(1)}, u32[]{:S(2)}, u32[]{:S(2)}) collective-permute-start(bf16[256,256]{1,0:T(8,128)(2,1)S(1)} %get-tuple-element.19.masked.refs_2_.refs_0_.refs_5_), channel_id=1, source_target_pairs={{0,8},{1,9},{2,10},{3,11},{4,12},{5,13},{6,14},{7,15},{8,16},{9,17... | collective-permute-start | bytes 393224 | tf_op jit(solution)/shard_map/ppermute | solution.py:25
  5.4 2.1 %collective-permute-start.1 = (bf16[256,256]{1,0:T(8,128)(2,1)S(1)}, bf16[256,256]{1,0:T(8,128)(2,1)S(1)}, u32[]{:S(2)}, u32[]{:S(2)}) collective-permute-start(bf16[256,256]{1,0:T(8,128)(2,1)S(1)} %get-tuple-element.19.masked.refs_2_.refs_0_.refs_5_), channel_id=1, source_target_pairs={{0,24},{1,25},{2,26},{3,27},{4,28},{5,29},{6,30},{7,31},{8,0},{9,1... | collective-permute-start | bytes 393224 | tf_op jit(solution)/shard_map/ppermute | solution.py:25
  7.5 2.6 %collective-permute-start.4 = (bf16[256,256]{1,0:T(8,128)(2,1)S(1)}, bf16[256,256]{1,0:T(8,128)(2,1)S(1)}, u32[]{:S(2)}, u32[]{:S(2)}) collective-permute-start(bf16[256,256]{1,0:T(8,128)(2,1)S(1)} %get-tuple-element.19.masked.refs_2_.refs_0_.refs_5_), channel_id=1, source_target_pairs={{0,6},{1,7},{2,4},{3,5},{4,2},{5,3},{6,0},{7,1},{8,14},{9,15},{10,... | collective-permute-start | bytes 393224 | tf_op jit(solution)/shard_map/ppermute | solution.py:25
  10.1 0.5 %collective-permute-start.2 = (bf16[256,256]{1,0:T(8,128)(2,1)S(1)}, bf16[256,256]{1,0:T(8,128)(2,1)S(1)}, u32[]{:S(2)}, u32[]{:S(2)}) collective-permute-start(bf16[256,256]{1,0:T(8,128)(2,1)S(1)} %get-tuple-element.19.masked.refs_2_.refs_0_.refs_5_), channel_id=1, source_target_pairs={{0,2},{1,3},{2,0},{3,1},{4,6},{5,7},{6,4},{7,5},{8,10},{9,11},{10,... | collective-permute-start | bytes 393224 | tf_op jit(solution)/shard_map/ppermute | solution.py:25
  10.6 0.3 %collective-permute-start.3 = (bf16[256,256]{1,0:T(8,128)(2,1)S(1)}, bf16[256,256]{1,0:T(8,128)(2,1)S(1)}, u32[]{:S(2)}, u32[]{:S(2)}) collective-permute-start(bf16[256,256]{1,0:T(8,128)(2,1)S(1)} %get-tuple-element.19.masked.refs_2_.refs_0_.refs_5_), channel_id=1, source_target_pairs={{0,4},{1,5},{2,6},{3,7},{4,0},{5,1},{6,2},{7,3},{8,12},{9,13},{10,... | collective-permute-start | bytes 393224 | tf_op jit(solution)/shard_map/ppermute | solution.py:25
  10.9 2.5 %shard_map.87 = (f32[256,256]{1,0:T(8,128)S(1)}, f32[256,256]{1,0:T(8,128)S(1)}, bf16[17,256,256]{2,1,0:T(8,128)(2,1)S(1)}, f32[17,1,256]{2,1,0:T(1,128)S(1)}) custom-call(s32[8,128]{1,0:T(8,128)S(1)} %get-tuple-element.20.rank, bf16[256,256]{1,0:T(8,128)(2,1)S(1)} %get-tuple-element.19.masked.refs_2_.refs_0_.refs_5_, s32[1,16]{1,0:T(1,128)} %neighbours.1, ...), custom_call_target="tpu_custom_call" | custom-call | flops 536870912 | bytes 2097152 | tf_op jit(solution)/shard_map/pallas_call | solution.py:196
  13.4 0.0 collective-permute-done.before.refs_6_
  13.4 0.0 collective-permute-done.1.after.refs_7_
  13.5 2.7 %collective-permute-start.7 = (bf16[256,256]{1,0:T(8,128)(2,1)S(1)}, bf16[256,256]{1,0:T(8,128)(2,1)S(1)}, u32[]{:S(2)}, u32[]{:S(2)}) collective-permute-start(bf16[256,256]{1,0:T(8,128)(2,1)S(1)} %get-tuple-element.31), channel_id=1, source_target_pairs={{0,6},{1,7},{2,4},{3,5},{4,2},{5,3},{6,0},{7,1},{8,14},{9,15},{10,... | collective-permute-start | bytes 393224 | tf_op jit(solution)/shard_map/ppermute | solution.py:25
  16.2 0.5 %collective-permute-start.5 = (bf16[256,256]{1,0:T(8,128)(2,1)S(1)}, bf16[256,256]{1,0:T(8,128)(2,1)S(1)}, u32[]{:S(2)}, u32[]{:S(2)}) collective-permute-start(bf16[256,256]{1,0:T(8,128)(2,1)S(1)} %get-tuple-element.30), channel_id=1, source_target_pairs={{0,2},{1,3},{2,0},{3,1},{4,6},{5,7},{6,4},{7,5},{8,10},{9,11},{10,... | collective-permute-start | bytes 393224 | tf_op jit(solution)/shard_map/ppermute | solution.py:25
  16.7 0.0 collective-permute-done.4.block
  16.7 0.4 %collective-permute-start.6 = (bf16[256,256]{1,0:T(8,128)(2,1)S(1)}, bf16[256,256]{1,0:T(8,128)(2,1)S(1)}, u32[]{:S(2)}, u32[]{:S(2)}) collective-permute-start(bf16[256,256]{1,0:T(8,128)(2,1)S(1)} %get-tuple-element.31), channel_id=1, source_target_pairs={{0,4},{1,5},{2,6},{3,7},{4,0},{5,1},{6,2},{7,3},{8,12},{9,13},{10,... | collective-permute-start | bytes 393224 | tf_op jit(solution)/shard_map/ppermute | solution.py:25
  17.1 3.3 %shard_map.88.refs_0_ = f32[256,256]{1,0:T(8,128)S(1)} custom-call(bf16[2,5120,256]{2,1,0:T(8,128)(2,1)} %bitcast.7), custom_call_target="tpu_custom_call" | custom-call | flops 536870912 | bytes 2097152 | tf_op jit(solution)/shard_map/pallas_call | solution.py:251
  20.4 0.0 collective-permute-done.2.refs_3_.refs_1_
  20.4 0.0 collective-permute-done.3.refs_4_.refs_2_
  20.4 0.1 collective-permute-start.8
  20.5 0.0 collective-permute-done.7.block
  20.5 0.6 %collective-permute-start.11 = (bf16[256,256]{1,0:T(8,128)(2,1)S(1)}, bf16[256,256]{1,0:T(8,128)(2,1)S(1)}, u32[]{:S(2)}, u32[]{:S(2)}) collective-permute-start(bf16[256,256]{1,0:T(8,128)(2,1)S(1)} %shard_map.91.refs_10_), channel_id=1, source_target_pairs={{0,1},{1,0},{2,3},{3,2},{4,5},{5,4},{6,7},{7,6},{8,9},{9,8},{10,11... | collective-permute-start | bytes 393224 | tf_op jit(solution)/shard_map/ppermute | solution.py:25
  21.1 0.7 %collective-permute-done.5.refs_8_ = bf16[256,256]{1,0:T(8,128)(2,1)S(1)} collective-permute-done((bf16[256,256]{1,0:T(8,128)(2,1)S(1)}, bf16[256,256]{1,0:T(8,128)(2,1)S(1)}, u32[]{:S(2)}, u32[]{:S(2)}) %collective-permute-start.5) | collective-permute-done | bytes 131104 | tf_op jit(solution)/shard_map/ppermute | solution.py:25
  21.8 0.0 collective-permute-start.9
  21.8 0.1 collective-permute-done.6.refs_9_
  21.9 0.4 %collective-permute-start.10 = (bf16[256,256]{1,0:T(8,128)(2,1)S(1)}, bf16[256,256]{1,0:T(8,128)(2,1)S(1)}, u32[]{:S(2)}, u32[]{:S(2)}) collective-permute-start(bf16[256,256]{1,0:T(8,128)(2,1)S(1)} %collective-permute-done.6.refs_9_), channel_id=1, source_target_pairs={{0,1},{1,0},{2,3},{3,2},{4,5},{5,4},{6,7},{7,6},{8,9},{9,8},{10,11... | collective-permute-start | bytes 393224 | tf_op jit(solution)/shard_map/ppermute | solution.py:25
  22.3 0.9 %shard_map.92.refs_0_ = f32[256,256]{1,0:T(8,128)S(1)} custom-call(bf16[17,256,256]{2,1,0:T(8,128)(2,1)S(1)} %get-tuple-element.25.inter, f32[17,1,256]{2,1,0:T(1,128)S(1)} %get-tuple-element.26.factors, f32[256,256]{1,0:T(8,128)S(1)} %shard_map.88.refs_0_, f32[256,256]{1,0:T(8,128)S(1)} %get-tuple-element.27.refs_1_, ...), custom_call_target="tpu_custom_call" | custom-call | flops 19327352832 | bytes 75497472 | tf_op jit(solution)/shard_map/pallas_call | solution.py:292
  23.2 0.0 collective-permute-done.8.refs_1_
  23.2 0.6 %shard_map.94.refs_0_ = f32[256,256]{1,0:T(8,128)S(1)} custom-call(bf16[17,256,256]{2,1,0:T(8,128)(2,1)S(1)} %get-tuple-element.25.inter, f32[17,1,256]{2,1,0:T(1,128)S(1)} %get-tuple-element.26.factors, f32[256,256]{1,0:T(8,128)S(1)} %shard_map.92.refs_0_, bf16[5,256,256]{2,1,0:T(8,128)(2,1)S(1)} %collective-permute-done.8.refs_1_), custom_call_target="tpu_custom_call" | custom-call | flops 335544320 | bytes 1310720 | tf_op jit(solution)/shard_map/pallas_call | solution.py:292
  23.8 0.0 collective-permute-done.9.refs_1_
  23.9 0.0 collective-permute-done.10.refs_2_
  23.9 0.0 collective-permute-done.11.refs_3_
  23.9 1.3 %shard_map.95 = (f32[256,256]{1,0:T(8,128)}, f32[256,256]{1,0:T(8,128)}) custom-call(bf16[17,256,256]{2,1,0:T(8,128)(2,1)S(1)} %get-tuple-element.25.inter, f32[17,1,256]{2,1,0:T(1,128)S(1)} %get-tuple-element.26.factors, f32[256,256]{1,0:T(8,128)S(1)} %shard_map.94.refs_0_, bf16[256,256]{1,0:T(8,128)(2,1)S(1)} %collective-permute-done.9.refs_1_, ...), custom_call_target="tpu_custom_call" | custom-call | flops 201326592 | bytes 786432 | tf_op jit(solution)/shard_map/pallas_call | solution.py:292
  (4 shorter events, 0.1 us)
Async XLA Ops:
  2.3 11.1 %collective-permute-start = (bf16[256,256]{1,0:T(8,128)(2,1)S(1)}, bf16[256,256]{1,0:T(8,128)(2,1)S(1)}, u32[]{:S(2)}, u32[]{:S(2)}) collective-permute-start(bf16[256,256]{1,0:T(8,128)(2,1)S(1)} %get-tuple-element.19.masked.refs_2_.refs_0_.refs_5_), channel_id=1, source_target_pairs={{0,8},{1,9},{2,10},{3,11},{4,12},{5,13},{6,14},{7,15},{8,16},{9,17... | collective-permute-start | bytes 393224 | tf_op jit(solution)/shard_map/ppermute | solution.py:25
  5.4 8.1 %collective-permute-start.1 = (bf16[256,256]{1,0:T(8,128)(2,1)S(1)}, bf16[256,256]{1,0:T(8,128)(2,1)S(1)}, u32[]{:S(2)}, u32[]{:S(2)}) collective-permute-start(bf16[256,256]{1,0:T(8,128)(2,1)S(1)} %get-tuple-element.19.masked.refs_2_.refs_0_.refs_5_), channel_id=1, source_target_pairs={{0,24},{1,25},{2,26},{3,27},{4,28},{5,29},{6,30},{7,31},{8,0},{9,1... | collective-permute-start | bytes 393224 | tf_op jit(solution)/shard_map/ppermute | solution.py:25
  7.5 9.2 %collective-permute-start.4 = (bf16[256,256]{1,0:T(8,128)(2,1)S(1)}, bf16[256,256]{1,0:T(8,128)(2,1)S(1)}, u32[]{:S(2)}, u32[]{:S(2)}) collective-permute-start(bf16[256,256]{1,0:T(8,128)(2,1)S(1)} %get-tuple-element.19.masked.refs_2_.refs_0_.refs_5_), channel_id=1, source_target_pairs={{0,6},{1,7},{2,4},{3,5},{4,2},{5,3},{6,0},{7,1},{8,14},{9,15},{10,... | collective-permute-start | bytes 393224 | tf_op jit(solution)/shard_map/ppermute | solution.py:25
  10.1 10.3 %collective-permute-start.2 = (bf16[256,256]{1,0:T(8,128)(2,1)S(1)}, bf16[256,256]{1,0:T(8,128)(2,1)S(1)}, u32[]{:S(2)}, u32[]{:S(2)}) collective-permute-start(bf16[256,256]{1,0:T(8,128)(2,1)S(1)} %get-tuple-element.19.masked.refs_2_.refs_0_.refs_5_), channel_id=1, source_target_pairs={{0,2},{1,3},{2,0},{3,1},{4,6},{5,7},{6,4},{7,5},{8,10},{9,11},{10,... | collective-permute-start | bytes 393224 | tf_op jit(solution)/shard_map/ppermute | solution.py:25
  10.6 9.8 %collective-permute-start.3 = (bf16[256,256]{1,0:T(8,128)(2,1)S(1)}, bf16[256,256]{1,0:T(8,128)(2,1)S(1)}, u32[]{:S(2)}, u32[]{:S(2)}) collective-permute-start(bf16[256,256]{1,0:T(8,128)(2,1)S(1)} %get-tuple-element.19.masked.refs_2_.refs_0_.refs_5_), channel_id=1, source_target_pairs={{0,4},{1,5},{2,6},{3,7},{4,0},{5,1},{6,2},{7,3},{8,12},{9,13},{10,... | collective-permute-start | bytes 393224 | tf_op jit(solution)/shard_map/ppermute | solution.py:25
  13.5 7.0 %collective-permute-start.7 = (bf16[256,256]{1,0:T(8,128)(2,1)S(1)}, bf16[256,256]{1,0:T(8,128)(2,1)S(1)}, u32[]{:S(2)}, u32[]{:S(2)}) collective-permute-start(bf16[256,256]{1,0:T(8,128)(2,1)S(1)} %get-tuple-element.31), channel_id=1, source_target_pairs={{0,6},{1,7},{2,4},{3,5},{4,2},{5,3},{6,0},{7,1},{8,14},{9,15},{10,... | collective-permute-start | bytes 393224 | tf_op jit(solution)/shard_map/ppermute | solution.py:25
  16.2 5.6 %collective-permute-start.5 = (bf16[256,256]{1,0:T(8,128)(2,1)S(1)}, bf16[256,256]{1,0:T(8,128)(2,1)S(1)}, u32[]{:S(2)}, u32[]{:S(2)}) collective-permute-start(bf16[256,256]{1,0:T(8,128)(2,1)S(1)} %get-tuple-element.30), channel_id=1, source_target_pairs={{0,2},{1,3},{2,0},{3,1},{4,6},{5,7},{6,4},{7,5},{8,10},{9,11},{10,... | collective-permute-start | bytes 393224 | tf_op jit(solution)/shard_map/ppermute | solution.py:25
  16.7 5.2 %collective-permute-start.6 = (bf16[256,256]{1,0:T(8,128)(2,1)S(1)}, bf16[256,256]{1,0:T(8,128)(2,1)S(1)}, u32[]{:S(2)}, u32[]{:S(2)}) collective-permute-start(bf16[256,256]{1,0:T(8,128)(2,1)S(1)} %get-tuple-element.31), channel_id=1, source_target_pairs={{0,4},{1,5},{2,6},{3,7},{4,0},{5,1},{6,2},{7,3},{8,12},{9,13},{10,... | collective-permute-start | bytes 393224 | tf_op jit(solution)/shard_map/ppermute | solution.py:25
  20.4 2.8 %collective-permute-start.8 = (bf16[5,256,256]{2,1,0:T(8,128)(2,1)S(1)}, bf16[5,256,256]{2,1,0:T(8,128)(2,1)S(1)}, u32[]{:S(2)}, u32[]{:S(2)}) collective-permute-start(bf16[5,256,256]{2,1,0:T(8,128)(2,1)S(1)} %shard_map.93), channel_id=1, source_target_pairs={{0,1},{1,0},{2,3},{3,2},{4,5},{5,4},{6,7},{7,6},{8,9},{9,8},{10,11... | collective-permute-start | bytes 1966088 | tf_op jit(solution)/shard_map/ppermute | solution.py:25
  20.5 3.3 %collective-permute-start.11 = (bf16[256,256]{1,0:T(8,128)(2,1)S(1)}, bf16[256,256]{1,0:T(8,128)(2,1)S(1)}, u32[]{:S(2)}, u32[]{:S(2)}) collective-permute-start(bf16[256,256]{1,0:T(8,128)(2,1)S(1)} %shard_map.91.refs_10_), channel_id=1, source_target_pairs={{0,1},{1,0},{2,3},{3,2},{4,5},{5,4},{6,7},{7,6},{8,9},{9,8},{10,11... | collective-permute-start | bytes 393224 | tf_op jit(solution)/shard_map/ppermute | solution.py:25
  21.8 2.0 %collective-permute-start.9 = (bf16[256,256]{1,0:T(8,128)(2,1)S(1)}, bf16[256,256]{1,0:T(8,128)(2,1)S(1)}, u32[]{:S(2)}, u32[]{:S(2)}) collective-permute-start(bf16[256,256]{1,0:T(8,128)(2,1)S(1)} %collective-permute-done.5.refs_8_), channel_id=1, source_target_pairs={{0,1},{1,0},{2,3},{3,2},{4,5},{5,4},{6,7},{7,6},{8,9},{9,8},{10,11... | collective-permute-start | bytes 393224 | tf_op jit(solution)/shard_map/ppermute | solution.py:25
  21.9 2.0 %collective-permute-start.10 = (bf16[256,256]{1,0:T(8,128)(2,1)S(1)}, bf16[256,256]{1,0:T(8,128)(2,1)S(1)}, u32[]{:S(2)}, u32[]{:S(2)}) collective-permute-start(bf16[256,256]{1,0:T(8,128)(2,1)S(1)} %collective-permute-done.6.refs_9_), channel_id=1, source_target_pairs={{0,1},{1,0},{2,3},{3,2},{4,5},{5,4},{6,7},{7,6},{8,9},{9,8},{10,11... | collective-permute-start | bytes 393224 | tf_op jit(solution)/shard_map/ppermute | solution.py:25

commit v6 on v5

--- a/solution.py
+++ b/solution.py
@@ -132,7 +132,7 @@
     cross = range(2, WIN, 2)
     steps = [(me ^ bits) - me + WIN for bits in (0, *cross)]
     steps += [0, 2 * WIN]
-    steps += [far_step(me, bits) for bits in cross]
+    steps += [far_step(me, bits) for bits in (6, 2, 4)]
     steps += [(me ^ bits) - me + WIN for bits in range(1, WIN, 2)]
     return steps + [far_step(me, bits) for bits in range(1, WIN, 2)]
 
@@ -282,7 +282,7 @@
         updated[...] = masked[...].astype(F32) - sum_now * scale[...]
 
 
-def block_sum(first, inter, factors, starts, blocks, ending=()):
+def block_sum(first, inter, factors, starts, blocks, weight=1, ending=()):
     shape = starts[0].shape
     out_shape = pltpu.VMEM(shape, F32)
     if ending:
@@ -295,7 +295,7 @@
         in_specs=[VMEM] * len(arrays),
         out_specs=(VMEM, VMEM) if ending else VMEM,
         compiler_params=PARAMS,
-        cost_estimate=cost(sum(map(len, picks)) * (1 if ending or first else 32), shape[0]),
+        cost_estimate=cost(sum(map(len, picks)) * weight, shape[0]),
     )(*arrays)
 
 
@@ -316,7 +316,7 @@
         aux_count == 1, axis, rank, masked, neighbours, couplings, energies, intersections[0]
     )
     exchange = exchange_of(pair_factors[0])
-    before, after, staged = lax.optimization_barrier((before, after, staged))
+    after, before, staged = lax.optimization_barrier((after, before, staged))
     total, scale, inter, factors = staged
     side1, side2, side4 = sides_of(axis, before, after)
     far = {bits: swapped(side, axis, bits) for bits, side in ((2, side2), (4, side4), (6, side4))}
@@ -324,15 +324,16 @@
     mine = stacked(*(own[bits] for bits in (0, *cross)), side1)
     theirs = swapped(mine, axis, 1)
     one = (None,)
-    direct = [own[bits] for bits in (0, *cross)] + [before, after] + [far[bits] for bits in cross]
-    direct = [(block, one) for block in direct]
-    swaps = [(theirs, tuple(range(WIN // 2 + 1)))]
+    near = [own[bits] for bits in (0, *cross)] + [before, after, far[6]]
+    near = [(block, one) for block in near]
+    total = block_sum(0, inter, factors, [exchange, total], near, 1)
+    far[2], far[4], total = lax.optimization_barrier((far[2], far[4], total))
     late = [(swapped(far[bits], axis, 1), one) for bits in cross]
-    total = block_sum(0, inter, factors, [exchange, total], direct)
-    total = block_sum(len(direct), inter, factors, [total], swaps)
-    late_first = len(direct) + WIN // 2 + 1
+    total = block_sum(len(near), inter, factors, [total], [(far[2], one), (far[4], one)], 64)
+    total = block_sum(len(near) + 2, inter, factors, [total], [(theirs, tuple(range(WIN // 2 + 1)))], 32)
+    late_first = len(near) + 2 + WIN // 2 + 1
     if aux_count == 1:
-        residual, updated = block_sum(late_first, inter, factors, [total], late, (scale, masked))
+        residual, updated = block_sum(late_first, inter, factors, [total], late, ending=(scale, masked))
         return residual[None], updated[None]
 
     partial_sum = block_sum(late_first, inter, factors, [total], late)[None]

time: 25.3 us -> 25.2 us (level)
  waiting for transfers between devices: 0.8 us -> 0.28 us
  Pallas kernels: 9.64 us -> 9.91 us
    ppermute x12, waiting for transfers between devices: 0.8 us -> 0.28 us  [permuted(): lax.ppermute(value, axis, [(source, target(source)) for source in range(c...]
    pallas_call x3 -> x4, Pallas kernels: 2.77 us -> 3.04 us  [block_sum(): pl.pallas_call(functools.partial(sum_kernel, first, picks, len(starts)),...]
  transfers between devices with their start and end apart: 12 -> 12, of which waited for: 2 -> 1; matrix products, arithmetic and copies ran while one was open for 0% -> 0% of each run, Pallas kernels for 29% -> 30%
where the time goes in v6:
time: 25.2 us; the launch traced here: 25 us
  starting transfers between devices  13.3 us (53%)
  Pallas kernels  9.91 us (39%)
  between operations  1.44 us (6%)
  waiting for transfers between devices  0.28 us (1%)
    ppermute x12, starting transfers between devices, permuted(): lax.ppermute(value, axis, [(source, target(source)) for source in range(c...  13.3 us
    pallas_call x1, Pallas kernels, exchange_of(): pl.pallas_call(exchange_kernel, out_shape=pltpu.VMEM((width, width), F32)...  3.28 us
    pallas_call x4, Pallas kernels, block_sum(): pl.pallas_call(functools.partial(sum_kernel, first, picks, len(starts)),...  3.04 us
    pallas_call x1, Pallas kernels, stage(): pl.pallas_call(functools.partial(stage_kernel, whole, axis), out_shape=(s...  2.48 us
    pallas_call x1, Pallas kernels, mask(): pl.pallas_call(mask_kernel, out_shape=(pltpu.VMEM(amplitude.shape, BF16),...  1.01 us
  transfers between devices with their start and end apart: 12, of which 1 were waited for; matrix products, arithmetic and copies ran while one was open for 0% of the time, Pallas kernels for 30%

profile of v6, /device:TPU:0, one launch (start us, length us, event | category | flops | bytes accessed | tf_op | source)
XLA Modules:
  0.0 25.0 jit_solution(5851361165235531279)
XLA Ops:
  1.3 1.0 %shard_map.86 = (bf16[256,256]{1,0:T(8,128)(2,1)S(1)}, s32[8,128]{1,0:T(8,128)S(1)}) custom-call(s32[1,1]{1,0:T(1,128)} %bitcast.6.rank, bf16[256,256]{1,0:T(8,128)(2,1)} %bitcast.9), custom_call_target="tpu_custom_call" | custom-call | tf_op jit(solution)/shard_map/pallas_call | solution.py:64
  2.3 3.1 %collective-permute-start.1 = (bf16[256,256]{1,0:T(8,128)(2,1)S(1)}, bf16[256,256]{1,0:T(8,128)(2,1)S(1)}, u32[]{:S(2)}, u32[]{:S(2)}) collective-permute-start(bf16[256,256]{1,0:T(8,128)(2,1)S(1)} %get-tuple-element.22.masked.refs_2_.refs_0_.refs_5_), channel_id=1, source_target_pairs={{0,8},{1,9},{2,10},{3,11},{4,12},{5,13},{6,14},{7,15},{8,16},{9,17... | collective-permute-start | bytes 393224 | tf_op jit(solution)/shard_map/ppermute | solution.py:25
  5.4 2.1 %collective-permute-start = (bf16[256,256]{1,0:T(8,128)(2,1)S(1)}, bf16[256,256]{1,0:T(8,128)(2,1)S(1)}, u32[]{:S(2)}, u32[]{:S(2)}) collective-permute-start(bf16[256,256]{1,0:T(8,128)(2,1)S(1)} %get-tuple-element.22.masked.refs_2_.refs_0_.refs_5_), channel_id=1, source_target_pairs={{0,24},{1,25},{2,26},{3,27},{4,28},{5,29},{6,30},{7,31},{8,0},{9,1... | collective-permute-start | bytes 393224 | tf_op jit(solution)/shard_map/ppermute | solution.py:25
  7.5 2.6 %collective-permute-start.6 = (bf16[256,256]{1,0:T(8,128)(2,1)S(1)}, bf16[256,256]{1,0:T(8,128)(2,1)S(1)}, u32[]{:S(2)}, u32[]{:S(2)}) collective-permute-start(bf16[256,256]{1,0:T(8,128)(2,1)S(1)} %get-tuple-element.22.masked.refs_2_.refs_0_.refs_5_), channel_id=1, source_target_pairs={{0,6},{1,7},{2,4},{3,5},{4,2},{5,3},{6,0},{7,1},{8,14},{9,15},{10,... | collective-permute-start | bytes 393224 | tf_op jit(solution)/shard_map/ppermute | solution.py:25
  10.1 0.5 %collective-permute-start.5 = (bf16[256,256]{1,0:T(8,128)(2,1)S(1)}, bf16[256,256]{1,0:T(8,128)(2,1)S(1)}, u32[]{:S(2)}, u32[]{:S(2)}) collective-permute-start(bf16[256,256]{1,0:T(8,128)(2,1)S(1)} %get-tuple-element.22.masked.refs_2_.refs_0_.refs_5_), channel_id=1, source_target_pairs={{0,4},{1,5},{2,6},{3,7},{4,0},{5,1},{6,2},{7,3},{8,12},{9,13},{10,... | collective-permute-start | bytes 393224 | tf_op jit(solution)/shard_map/ppermute | solution.py:25
  10.6 0.4 %collective-permute-start.4 = (bf16[256,256]{1,0:T(8,128)(2,1)S(1)}, bf16[256,256]{1,0:T(8,128)(2,1)S(1)}, u32[]{:S(2)}, u32[]{:S(2)}) collective-permute-start(bf16[256,256]{1,0:T(8,128)(2,1)S(1)} %get-tuple-element.22.masked.refs_2_.refs_0_.refs_5_), channel_id=1, source_target_pairs={{0,2},{1,3},{2,0},{3,1},{4,6},{5,7},{6,4},{7,5},{8,10},{9,11},{10,... | collective-permute-start | bytes 393224 | tf_op jit(solution)/shard_map/ppermute | solution.py:25
  10.9 2.5 %shard_map.87 = (f32[256,256]{1,0:T(8,128)S(1)}, f32[256,256]{1,0:T(8,128)S(1)}, bf16[17,256,256]{2,1,0:T(8,128)(2,1)S(1)}, f32[17,1,256]{2,1,0:T(1,128)S(1)}) custom-call(s32[8,128]{1,0:T(8,128)S(1)} %get-tuple-element.23.rank, bf16[256,256]{1,0:T(8,128)(2,1)S(1)} %get-tuple-element.22.masked.refs_2_.refs_0_.refs_5_, s32[1,16]{1,0:T(1,128)} %neighbours.1, ...), custom_call_target="tpu_custom_call" | custom-call | flops 536870912 | bytes 2097152 | tf_op jit(solution)/shard_map/pallas_call | solution.py:196
  13.4 0.0 collective-permute-done.1.before.refs_6_
  13.4 0.0 collective-permute-done.after.refs_7_
  13.5 2.7 %collective-permute-start.7 = (bf16[256,256]{1,0:T(8,128)(2,1)S(1)}, bf16[256,256]{1,0:T(8,128)(2,1)S(1)}, u32[]{:S(2)}, u32[]{:S(2)}) collective-permute-start(bf16[256,256]{1,0:T(8,128)(2,1)S(1)} %get-tuple-element.33), channel_id=1, source_target_pairs={{0,6},{1,7},{2,4},{3,5},{4,2},{5,3},{6,0},{7,1},{8,14},{9,15},{10,... | collective-permute-start | bytes 393224 | tf_op jit(solution)/shard_map/ppermute | solution.py:25
  16.2 0.5 %collective-permute-start.3 = (bf16[256,256]{1,0:T(8,128)(2,1)S(1)}, bf16[256,256]{1,0:T(8,128)(2,1)S(1)}, u32[]{:S(2)}, u32[]{:S(2)}) collective-permute-start(bf16[256,256]{1,0:T(8,128)(2,1)S(1)} %get-tuple-element.33), channel_id=1, source_target_pairs={{0,4},{1,5},{2,6},{3,7},{4,0},{5,1},{6,2},{7,3},{8,12},{9,13},{10,... | collective-permute-start | bytes 393224 | tf_op jit(solution)/shard_map/ppermute | solution.py:25
  16.7 0.0 collective-permute-done.6.block
  16.7 0.4 %collective-permute-start.2 = (bf16[256,256]{1,0:T(8,128)(2,1)S(1)}, bf16[256,256]{1,0:T(8,128)(2,1)S(1)}, u32[]{:S(2)}, u32[]{:S(2)}) collective-permute-start(bf16[256,256]{1,0:T(8,128)(2,1)S(1)} %get-tuple-element.32), channel_id=1, source_target_pairs={{0,2},{1,3},{2,0},{3,1},{4,6},{5,7},{6,4},{7,5},{8,10},{9,11},{10,... | collective-permute-start | bytes 393224 | tf_op jit(solution)/shard_map/ppermute | solution.py:25
  17.1 3.3 %shard_map.89.refs_0_ = f32[256,256]{1,0:T(8,128)S(1)} custom-call(bf16[2,5120,256]{2,1,0:T(8,128)(2,1)} %bitcast.7), custom_call_target="tpu_custom_call" | custom-call | flops 536870912 | bytes 2097152 | tf_op jit(solution)/shard_map/pallas_call | solution.py:251
  20.4 0.0 collective-permute-done.5.refs_4_.refs_2_
  20.4 0.0 collective-permute-done.4.refs_3_.refs_1_
  20.4 0.1 collective-permute-start.8
  20.5 0.0 collective-permute-done.7.block
  20.5 0.6 %collective-permute-start.11 = (bf16[256,256]{1,0:T(8,128)(2,1)S(1)}, bf16[256,256]{1,0:T(8,128)(2,1)S(1)}, u32[]{:S(2)}, u32[]{:S(2)}) collective-permute-start(bf16[256,256]{1,0:T(8,128)(2,1)S(1)} %shard_map.91.refs_8_), channel_id=1, source_target_pairs={{0,1},{1,0},{2,3},{3,2},{4,5},{5,4},{6,7},{7,6},{8,9},{9,8},{10,11... | collective-permute-start | bytes 393224 | tf_op jit(solution)/shard_map/ppermute | solution.py:25
  21.1 0.7 %shard_map.92.refs_0_ = f32[256,256]{1,0:T(8,128)S(1)} custom-call(bf16[17,256,256]{2,1,0:T(8,128)(2,1)S(1)} %get-tuple-element.28.inter, f32[17,1,256]{2,1,0:T(1,128)S(1)} %get-tuple-element.29.factors, f32[256,256]{1,0:T(8,128)S(1)} %shard_map.89.refs_0_, f32[256,256]{1,0:T(8,128)S(1)} %get-tuple-element.34.refs_1_, ...), custom_call_target="tpu_custom_call" | custom-call | flops 469762048 | bytes 1835008 | tf_op jit(solution)/shard_map/pallas_call | solution.py:292
  21.9 0.0 collective-permute-done.2.refs_1_
  21.9 0.3 %collective-permute-done.3.refs_2_ = bf16[256,256]{1,0:T(8,128)(2,1)S(1)} collective-permute-done((bf16[256,256]{1,0:T(8,128)(2,1)S(1)}, bf16[256,256]{1,0:T(8,128)(2,1)S(1)}, u32[]{:S(2)}, u32[]{:S(2)}) %collective-permute-start.3) | collective-permute-done | bytes 131104 | tf_op jit(solution)/shard_map/ppermute | solution.py:25
  22.1 0.0 collective-permute-start.9
  22.1 0.5 %collective-permute-start.10 = (bf16[256,256]{1,0:T(8,128)(2,1)S(1)}, bf16[256,256]{1,0:T(8,128)(2,1)S(1)}, u32[]{:S(2)}, u32[]{:S(2)}) collective-permute-start(bf16[256,256]{1,0:T(8,128)(2,1)S(1)} %collective-permute-done.3.refs_2_), channel_id=1, source_target_pairs={{0,1},{1,0},{2,3},{3,2},{4,5},{5,4},{6,7},{7,6},{8,9},{9,8},{10,11... | collective-permute-start | bytes 393224 | tf_op jit(solution)/shard_map/ppermute | solution.py:25
  22.6 0.4 %shard_map.93.refs_0_ = f32[256,256]{1,0:T(8,128)S(1)} custom-call(bf16[17,256,256]{2,1,0:T(8,128)(2,1)S(1)} %get-tuple-element.28.inter, f32[17,1,256]{2,1,0:T(1,128)S(1)} %get-tuple-element.29.factors, f32[256,256]{1,0:T(8,128)S(1)} %shard_map.92.refs_0_, bf16[256,256]{1,0:T(8,128)(2,1)S(1)} %collective-permute-done.2.refs_1_, ...), custom_call_target="tpu_custom_call" | custom-call | flops 8589934592 | bytes 33554432 | tf_op jit(solution)/shard_map/pallas_call | solution.py:292
  23.0 0.0 collective-permute-done.8.refs_1_
  23.1 0.6 %shard_map.95.refs_0_ = f32[256,256]{1,0:T(8,128)S(1)} custom-call(bf16[17,256,256]{2,1,0:T(8,128)(2,1)S(1)} %get-tuple-element.28.inter, f32[17,1,256]{2,1,0:T(1,128)S(1)} %get-tuple-element.29.factors, f32[256,256]{1,0:T(8,128)S(1)} %shard_map.93.refs_0_, bf16[5,256,256]{2,1,0:T(8,128)(2,1)S(1)} %collective-permute-done.8.refs_1_), custom_call_target="tpu_custom_call" | custom-call | flops 10737418240 | bytes 41943040 | tf_op jit(solution)/shard_map/pallas_call | solution.py:292
  23.7 0.0 collective-permute-done.11.refs_3_
  23.7 0.0 collective-permute-done.9.refs_1_
  23.7 0.0 collective-permute-done.10.refs_2_
  23.7 1.3 %shard_map.96 = (f32[256,256]{1,0:T(8,128)}, f32[256,256]{1,0:T(8,128)}) custom-call(bf16[17,256,256]{2,1,0:T(8,128)(2,1)S(1)} %get-tuple-element.28.inter, f32[17,1,256]{2,1,0:T(1,128)S(1)} %get-tuple-element.29.factors, f32[256,256]{1,0:T(8,128)S(1)} %shard_map.95.refs_0_, bf16[256,256]{1,0:T(8,128)(2,1)S(1)} %collective-permute-done.9.refs_1_, ...), custom_call_target="tpu_custom_call" | custom-call | flops 201326592 | bytes 786432 | tf_op jit(solution)/shard_map/pallas_call | solution.py:292
  (4 shorter events, 0.1 us)
Async XLA Ops:
  2.3 11.1 %collective-permute-start.1 = (bf16[256,256]{1,0:T(8,128)(2,1)S(1)}, bf16[256,256]{1,0:T(8,128)(2,1)S(1)}, u32[]{:S(2)}, u32[]{:S(2)}) collective-permute-start(bf16[256,256]{1,0:T(8,128)(2,1)S(1)} %get-tuple-element.22.masked.refs_2_.refs_0_.refs_5_), channel_id=1, source_target_pairs={{0,8},{1,9},{2,10},{3,11},{4,12},{5,13},{6,14},{7,15},{8,16},{9,17... | collective-permute-start | bytes 393224 | tf_op jit(solution)/shard_map/ppermute | solution.py:25
  5.4 8.1 %collective-permute-start = (bf16[256,256]{1,0:T(8,128)(2,1)S(1)}, bf16[256,256]{1,0:T(8,128)(2,1)S(1)}, u32[]{:S(2)}, u32[]{:S(2)}) collective-permute-start(bf16[256,256]{1,0:T(8,128)(2,1)S(1)} %get-tuple-element.22.masked.refs_2_.refs_0_.refs_5_), channel_id=1, source_target_pairs={{0,24},{1,25},{2,26},{3,27},{4,28},{5,29},{6,30},{7,31},{8,0},{9,1... | collective-permute-start | bytes 393224 | tf_op jit(solution)/shard_map/ppermute | solution.py:25
  7.5 9.2 %collective-permute-start.6 = (bf16[256,256]{1,0:T(8,128)(2,1)S(1)}, bf16[256,256]{1,0:T(8,128)(2,1)S(1)}, u32[]{:S(2)}, u32[]{:S(2)}) collective-permute-start(bf16[256,256]{1,0:T(8,128)(2,1)S(1)} %get-tuple-element.22.masked.refs_2_.refs_0_.refs_5_), channel_id=1, source_target_pairs={{0,6},{1,7},{2,4},{3,5},{4,2},{5,3},{6,0},{7,1},{8,14},{9,15},{10,... | collective-permute-start | bytes 393224 | tf_op jit(solution)/shard_map/ppermute | solution.py:25
  10.1 10.3 %collective-permute-start.5 = (bf16[256,256]{1,0:T(8,128)(2,1)S(1)}, bf16[256,256]{1,0:T(8,128)(2,1)S(1)}, u32[]{:S(2)}, u32[]{:S(2)}) collective-permute-start(bf16[256,256]{1,0:T(8,128)(2,1)S(1)} %get-tuple-element.22.masked.refs_2_.refs_0_.refs_5_), channel_id=1, source_target_pairs={{0,4},{1,5},{2,6},{3,7},{4,0},{5,1},{6,2},{7,3},{8,12},{9,13},{10,... | collective-permute-start | bytes 393224 | tf_op jit(solution)/shard_map/ppermute | solution.py:25
  10.6 9.8 %collective-permute-start.4 = (bf16[256,256]{1,0:T(8,128)(2,1)S(1)}, bf16[256,256]{1,0:T(8,128)(2,1)S(1)}, u32[]{:S(2)}, u32[]{:S(2)}) collective-permute-start(bf16[256,256]{1,0:T(8,128)(2,1)S(1)} %get-tuple-element.22.masked.refs_2_.refs_0_.refs_5_), channel_id=1, source_target_pairs={{0,2},{1,3},{2,0},{3,1},{4,6},{5,7},{6,4},{7,5},{8,10},{9,11},{10,... | collective-permute-start | bytes 393224 | tf_op jit(solution)/shard_map/ppermute | solution.py:25
  13.5 7.0 %collective-permute-start.7 = (bf16[256,256]{1,0:T(8,128)(2,1)S(1)}, bf16[256,256]{1,0:T(8,128)(2,1)S(1)}, u32[]{:S(2)}, u32[]{:S(2)}) collective-permute-start(bf16[256,256]{1,0:T(8,128)(2,1)S(1)} %get-tuple-element.33), channel_id=1, source_target_pairs={{0,6},{1,7},{2,4},{3,5},{4,2},{5,3},{6,0},{7,1},{8,14},{9,15},{10,... | collective-permute-start | bytes 393224 | tf_op jit(solution)/shard_map/ppermute | solution.py:25
  16.2 5.9 %collective-permute-start.3 = (bf16[256,256]{1,0:T(8,128)(2,1)S(1)}, bf16[256,256]{1,0:T(8,128)(2,1)S(1)}, u32[]{:S(2)}, u32[]{:S(2)}) collective-permute-start(bf16[256,256]{1,0:T(8,128)(2,1)S(1)} %get-tuple-element.33), channel_id=1, source_target_pairs={{0,4},{1,5},{2,6},{3,7},{4,0},{5,1},{6,2},{7,3},{8,12},{9,13},{10,... | collective-permute-start | bytes 393224 | tf_op jit(solution)/shard_map/ppermute | solution.py:25
  16.7 5.2 %collective-permute-start.2 = (bf16[256,256]{1,0:T(8,128)(2,1)S(1)}, bf16[256,256]{1,0:T(8,128)(2,1)S(1)}, u32[]{:S(2)}, u32[]{:S(2)}) collective-permute-start(bf16[256,256]{1,0:T(8,128)(2,1)S(1)} %get-tuple-element.32), channel_id=1, source_target_pairs={{0,2},{1,3},{2,0},{3,1},{4,6},{5,7},{6,4},{7,5},{8,10},{9,11},{10,... | collective-permute-start | bytes 393224 | tf_op jit(solution)/shard_map/ppermute | solution.py:25
  20.4 2.6 %collective-permute-start.8 = (bf16[5,256,256]{2,1,0:T(8,128)(2,1)S(1)}, bf16[5,256,256]{2,1,0:T(8,128)(2,1)S(1)}, u32[]{:S(2)}, u32[]{:S(2)}) collective-permute-start(bf16[5,256,256]{2,1,0:T(8,128)(2,1)S(1)} %shard_map.94), channel_id=1, source_target_pairs={{0,1},{1,0},{2,3},{3,2},{4,5},{5,4},{6,7},{7,6},{8,9},{9,8},{10,11... | collective-permute-start | bytes 1966088 | tf_op jit(solution)/shard_map/ppermute | solution.py:25
  20.5 3.1 %collective-permute-start.11 = (bf16[256,256]{1,0:T(8,128)(2,1)S(1)}, bf16[256,256]{1,0:T(8,128)(2,1)S(1)}, u32[]{:S(2)}, u32[]{:S(2)}) collective-permute-start(bf16[256,256]{1,0:T(8,128)(2,1)S(1)} %shard_map.91.refs_8_), channel_id=1, source_target_pairs={{0,1},{1,0},{2,3},{3,2},{4,5},{5,4},{6,7},{7,6},{8,9},{9,8},{10,11... | collective-permute-start | bytes 393224 | tf_op jit(solution)/shard_map/ppermute | solution.py:25
  22.1 1.6 %collective-permute-start.9 = (bf16[256,256]{1,0:T(8,128)(2,1)S(1)}, bf16[256,256]{1,0:T(8,128)(2,1)S(1)}, u32[]{:S(2)}, u32[]{:S(2)}) collective-permute-start(bf16[256,256]{1,0:T(8,128)(2,1)S(1)} %collective-permute-done.2.refs_1_), channel_id=1, source_target_pairs={{0,1},{1,0},{2,3},{3,2},{4,5},{5,4},{6,7},{7,6},{8,9},{9,8},{10,11... | collective-permute-start | bytes 393224 | tf_op jit(solution)/shard_map/ppermute | solution.py:25
  22.1 1.6 %collective-permute-start.10 = (bf16[256,256]{1,0:T(8,128)(2,1)S(1)}, bf16[256,256]{1,0:T(8,128)(2,1)S(1)}, u32[]{:S(2)}, u32[]{:S(2)}) collective-permute-start(bf16[256,256]{1,0:T(8,128)(2,1)S(1)} %collective-permute-done.3.refs_2_), channel_id=1, source_target_pairs={{0,1},{1,0},{2,3},{3,2},{4,5},{5,4},{6,7},{7,6},{8,9},{9,8},{10,11... | collective-permute-start | bytes 393224 | tf_op jit(solution)/shard_map/ppermute | solution.py:25

commit v7 on v6

--- a/solution.py
+++ b/solution.py
@@ -134,7 +134,7 @@
     steps += [0, 2 * WIN]
     steps += [far_step(me, bits) for bits in (6, 2, 4)]
     steps += [(me ^ bits) - me + WIN for bits in range(1, WIN, 2)]
-    return steps + [far_step(me, bits) for bits in range(1, WIN, 2)]
+    return steps + [far_step(me, bits) for bits in (1, 7, 3, 5)]
 
 
 def stage_kernel(
@@ -328,10 +328,12 @@
     near = [(block, one) for block in near]
     total = block_sum(0, inter, factors, [exchange, total], near, 1)
     far[2], far[4], total = lax.optimization_barrier((far[2], far[4], total))
-    late = [(swapped(far[bits], axis, 1), one) for bits in cross]
+    pair_now = swapped(stacked(far[2], far[4]), axis, 1)
+    late = [(pair_now, (0, 1))]
+    diagonal = swapped(far[6], axis, 1)
     total = block_sum(len(near), inter, factors, [total], [(far[2], one), (far[4], one)], 64)
-    total = block_sum(len(near) + 2, inter, factors, [total], [(theirs, tuple(range(WIN // 2 + 1)))], 32)
-    late_first = len(near) + 2 + WIN // 2 + 1
+    total = block_sum(len(near) + 2, inter, factors, [total], [(theirs, tuple(range(WIN // 2 + 1))), (diagonal, one)], 1)
+    late_first = len(near) + 2 + WIN // 2 + 2
     if aux_count == 1:
         residual, updated = block_sum(late_first, inter, factors, [total], late, ending=(scale, masked))
         return residual[None], updated[None]

time: 25.2 us -> 25.1 us (level)
  waiting for transfers between devices: 0.28 us -> 0.69 us
  starting transfers between devices: 13.3 us -> 12.9 us
    ppermute x12 -> x11, starting transfers between devices: 13.3 us -> 12.9 us  [permuted(): lax.ppermute(value, axis, [(source, target(source)) for source in range(c...]
    ppermute x12 -> x11, waiting for transfers between devices: 0.28 us -> 0.69 us  [permuted(): lax.ppermute(value, axis, [(source, target(source)) for source in range(c...]
  transfers between devices with their start and end apart: 12 -> 11, of which waited for: 1 -> 3; matrix products, arithmetic and copies ran while one was open for 0% -> 0% of each run, Pallas kernels for 30% -> 31%
where the time goes in v7:
time: 25.1 us; the launch traced here: 24.9 us
  starting transfers between devices  12.9 us (51%)
  Pallas kernels  9.93 us (40%)
  between operations  1.42 us (6%)
  waiting for transfers between devices  0.69 us (3%)
    ppermute x11, starting transfers between devices, permuted(): lax.ppermute(value, axis, [(source, target(source)) for source in range(c...  12.9 us
    pallas_call x1, Pallas kernels, exchange_of(): pl.pallas_call(exchange_kernel, out_shape=pltpu.VMEM((width, width), F32)...  3.28 us
    pallas_call x4, Pallas kernels, block_sum(): pl.pallas_call(functools.partial(sum_kernel, first, picks, len(starts)),...  3.04 us
    pallas_call x1, Pallas kernels, stage(): pl.pallas_call(functools.partial(stage_kernel, whole, axis), out_shape=(s...  2.48 us
    pallas_call x1, Pallas kernels, mask(): pl.pallas_call(mask_kernel, out_shape=(pltpu.VMEM(amplitude.shape, BF16),...  1.01 us
    ppermute x11, waiting for transfers between devices, permuted(): lax.ppermute(value, axis, [(source, target(source)) for source in range(c...  0.69 us
  transfers between devices with their start and end apart: 11, of which 3 were waited for; matrix products, arithmetic and copies ran while one was open for 0% of the time, Pallas kernels for 31%

profile of v7, /device:TPU:0, one launch (start us, length us, event | category | flops | bytes accessed | tf_op | source)
XLA Modules:
  0.0 24.9 jit_solution(4023271047882342714)
XLA Ops:
  1.3 1.0 %shard_map.86 = (bf16[256,256]{1,0:T(8,128)(2,1)S(1)}, s32[8,128]{1,0:T(8,128)S(1)}) custom-call(s32[1,1]{1,0:T(1,128)} %bitcast.6.rank, bf16[256,256]{1,0:T(8,128)(2,1)} %bitcast.9), custom_call_target="tpu_custom_call" | custom-call | tf_op jit(solution)/shard_map/pallas_call | solution.py:64
  2.3 3.1 %collective-permute-start.1 = (bf16[256,256]{1,0:T(8,128)(2,1)S(1)}, bf16[256,256]{1,0:T(8,128)(2,1)S(1)}, u32[]{:S(2)}, u32[]{:S(2)}) collective-permute-start(bf16[256,256]{1,0:T(8,128)(2,1)S(1)} %get-tuple-element.22.masked.refs_2_.refs_0_.refs_3_), channel_id=1, source_target_pairs={{0,8},{1,9},{2,10},{3,11},{4,12},{5,13},{6,14},{7,15},{8,16},{9,17... | collective-permute-start | bytes 393224 | tf_op jit(solution)/shard_map/ppermute | solution.py:25
  5.4 2.1 %collective-permute-start = (bf16[256,256]{1,0:T(8,128)(2,1)S(1)}, bf16[256,256]{1,0:T(8,128)(2,1)S(1)}, u32[]{:S(2)}, u32[]{:S(2)}) collective-permute-start(bf16[256,256]{1,0:T(8,128)(2,1)S(1)} %get-tuple-element.22.masked.refs_2_.refs_0_.refs_3_), channel_id=1, source_target_pairs={{0,24},{1,25},{2,26},{3,27},{4,28},{5,29},{6,30},{7,31},{8,0},{9,1... | collective-permute-start | bytes 393224 | tf_op jit(solution)/shard_map/ppermute | solution.py:25
  7.5 2.6 %collective-permute-start.6 = (bf16[256,256]{1,0:T(8,128)(2,1)S(1)}, bf16[256,256]{1,0:T(8,128)(2,1)S(1)}, u32[]{:S(2)}, u32[]{:S(2)}) collective-permute-start(bf16[256,256]{1,0:T(8,128)(2,1)S(1)} %get-tuple-element.22.masked.refs_2_.refs_0_.refs_3_), channel_id=1, source_target_pairs={{0,6},{1,7},{2,4},{3,5},{4,2},{5,3},{6,0},{7,1},{8,14},{9,15},{10,... | collective-permute-start | bytes 393224 | tf_op jit(solution)/shard_map/ppermute | solution.py:25
  10.1 0.5 %collective-permute-start.5 = (bf16[256,256]{1,0:T(8,128)(2,1)S(1)}, bf16[256,256]{1,0:T(8,128)(2,1)S(1)}, u32[]{:S(2)}, u32[]{:S(2)}) collective-permute-start(bf16[256,256]{1,0:T(8,128)(2,1)S(1)} %get-tuple-element.22.masked.refs_2_.refs_0_.refs_3_), channel_id=1, source_target_pairs={{0,4},{1,5},{2,6},{3,7},{4,0},{5,1},{6,2},{7,3},{8,12},{9,13},{10,... | collective-permute-start | bytes 393224 | tf_op jit(solution)/shard_map/ppermute | solution.py:25
  10.6 0.4 %collective-permute-start.4 = (bf16[256,256]{1,0:T(8,128)(2,1)S(1)}, bf16[256,256]{1,0:T(8,128)(2,1)S(1)}, u32[]{:S(2)}, u32[]{:S(2)}) collective-permute-start(bf16[256,256]{1,0:T(8,128)(2,1)S(1)} %get-tuple-element.22.masked.refs_2_.refs_0_.refs_3_), channel_id=1, source_target_pairs={{0,2},{1,3},{2,0},{3,1},{4,6},{5,7},{6,4},{7,5},{8,10},{9,11},{10,... | collective-permute-start | bytes 393224 | tf_op jit(solution)/shard_map/ppermute | solution.py:25
  10.9 2.5 %shard_map.87 = (f32[256,256]{1,0:T(8,128)S(1)}, f32[256,256]{1,0:T(8,128)S(1)}, bf16[17,256,256]{2,1,0:T(8,128)(2,1)S(1)}, f32[17,1,256]{2,1,0:T(1,128)S(1)}) custom-call(s32[8,128]{1,0:T(8,128)S(1)} %get-tuple-element.23.rank, bf16[256,256]{1,0:T(8,128)(2,1)S(1)} %get-tuple-element.22.masked.refs_2_.refs_0_.refs_3_, s32[1,16]{1,0:T(1,128)} %neighbours.1, ...), custom_call_target="tpu_custom_call" | custom-call | flops 536870912 | bytes 2097152 | tf_op jit(solution)/shard_map/pallas_call | solution.py:196
  13.4 0.0 collective-permute-done.1.before.refs_6_
  13.4 0.0 collective-permute-done.after.refs_7_
  13.5 2.7 %collective-permute-start.7 = (bf16[256,256]{1,0:T(8,128)(2,1)S(1)}, bf16[256,256]{1,0:T(8,128)(2,1)S(1)}, u32[]{:S(2)}, u32[]{:S(2)}) collective-permute-start(bf16[256,256]{1,0:T(8,128)(2,1)S(1)} %get-tuple-element.33), channel_id=1, source_target_pairs={{0,6},{1,7},{2,4},{3,5},{4,2},{5,3},{6,0},{7,1},{8,14},{9,15},{10,... | collective-permute-start | bytes 393224 | tf_op jit(solution)/shard_map/ppermute | solution.py:25
  16.2 0.5 %collective-permute-start.3 = (bf16[256,256]{1,0:T(8,128)(2,1)S(1)}, bf16[256,256]{1,0:T(8,128)(2,1)S(1)}, u32[]{:S(2)}, u32[]{:S(2)}) collective-permute-start(bf16[256,256]{1,0:T(8,128)(2,1)S(1)} %get-tuple-element.33), channel_id=1, source_target_pairs={{0,4},{1,5},{2,6},{3,7},{4,0},{5,1},{6,2},{7,3},{8,12},{9,13},{10,... | collective-permute-start | bytes 393224 | tf_op jit(solution)/shard_map/ppermute | solution.py:25
  16.7 0.0 collective-permute-done.6.block
  16.7 0.4 %collective-permute-start.2 = (bf16[256,256]{1,0:T(8,128)(2,1)S(1)}, bf16[256,256]{1,0:T(8,128)(2,1)S(1)}, u32[]{:S(2)}, u32[]{:S(2)}) collective-permute-start(bf16[256,256]{1,0:T(8,128)(2,1)S(1)} %get-tuple-element.32), channel_id=1, source_target_pairs={{0,2},{1,3},{2,0},{3,1},{4,6},{5,7},{6,4},{7,5},{8,10},{9,11},{10,... | collective-permute-start | bytes 393224 | tf_op jit(solution)/shard_map/ppermute | solution.py:25
  17.1 3.3 %shard_map.89.refs_0_ = f32[256,256]{1,0:T(8,128)S(1)} custom-call(bf16[2,5120,256]{2,1,0:T(8,128)(2,1)} %bitcast.7), custom_call_target="tpu_custom_call" | custom-call | flops 536870912 | bytes 2097152 | tf_op jit(solution)/shard_map/pallas_call | solution.py:251
  20.4 0.0 collective-permute-done.5.refs_4_.refs_2_
  20.4 0.0 collective-permute-done.4.refs_3_.refs_1_
  20.4 0.1 collective-permute-start.8
  20.5 0.0 collective-permute-done.7.block
  20.5 0.6 %collective-permute-start.9 = (bf16[256,256]{1,0:T(8,128)(2,1)S(1)}, bf16[256,256]{1,0:T(8,128)(2,1)S(1)}, u32[]{:S(2)}, u32[]{:S(2)}) collective-permute-start(bf16[256,256]{1,0:T(8,128)(2,1)S(1)} %shard_map.91.refs_8_), channel_id=1, source_target_pairs={{0,1},{1,0},{2,3},{3,2},{4,5},{5,4},{6,7},{7,6},{8,9},{9,8},{10,11... | collective-permute-start | bytes 393224 | tf_op jit(solution)/shard_map/ppermute | solution.py:25
  21.1 0.7 %shard_map.92.refs_0_ = f32[256,256]{1,0:T(8,128)S(1)} custom-call(bf16[17,256,256]{2,1,0:T(8,128)(2,1)S(1)} %get-tuple-element.28.inter, f32[17,1,256]{2,1,0:T(1,128)S(1)} %get-tuple-element.29.factors, f32[256,256]{1,0:T(8,128)S(1)} %shard_map.89.refs_0_, f32[256,256]{1,0:T(8,128)S(1)} %get-tuple-element.34.refs_1_, ...), custom_call_target="tpu_custom_call" | custom-call | flops 469762048 | bytes 1835008 | tf_op jit(solution)/shard_map/pallas_call | solution.py:292
  21.8 0.0 collective-permute-done.2.refs_1_.refs_0_
  21.9 0.3 %collective-permute-done.3.refs_2_.refs_1_ = bf16[256,256]{1,0:T(8,128)(2,1)S(1)} collective-permute-done((bf16[256,256]{1,0:T(8,128)(2,1)S(1)}, bf16[256,256]{1,0:T(8,128)(2,1)S(1)}, u32[]{:S(2)}, u32[]{:S(2)}) %collective-permute-start.3) | collective-permute-done | bytes 131104 | tf_op jit(solution)/shard_map/ppermute | solution.py:25
  22.1 0.1 collective-permute-start.10
  22.2 0.4 %shard_map.93.refs_0_ = f32[256,256]{1,0:T(8,128)S(1)} custom-call(bf16[17,256,256]{2,1,0:T(8,128)(2,1)S(1)} %get-tuple-element.28.inter, f32[17,1,256]{2,1,0:T(1,128)S(1)} %get-tuple-element.29.factors, f32[256,256]{1,0:T(8,128)S(1)} %shard_map.92.refs_0_, bf16[256,256]{1,0:T(8,128)(2,1)S(1)} %collective-permute-done.2.refs_1_.refs_0_, ...), custom_call_target="tpu_custom_call" | custom-call | flops 8589934592 | bytes 33554432 | tf_op jit(solution)/shard_map/pallas_call | solution.py:292
  22.6 0.2 collective-permute-done.9.refs_2_
  22.8 0.0 collective-permute-done.8.refs_1_
  22.8 0.7 %shard_map.95.refs_0_ = f32[256,256]{1,0:T(8,128)S(1)} custom-call(bf16[17,256,256]{2,1,0:T(8,128)(2,1)S(1)} %get-tuple-element.28.inter, f32[17,1,256]{2,1,0:T(1,128)S(1)} %get-tuple-element.29.factors, f32[256,256]{1,0:T(8,128)S(1)} %shard_map.93.refs_0_, bf16[5,256,256]{2,1,0:T(8,128)(2,1)S(1)} %collective-permute-done.8.refs_1_, ...), custom_call_target="tpu_custom_call" | custom-call | flops 402653184 | bytes 1572864 | tf_op jit(solution)/shard_map/pallas_call | solution.py:292
  23.5 0.3 %collective-permute-done.10.refs_1_ = bf16[2,256,256]{2,1,0:T(8,128)(2,1)S(1)} collective-permute-done((bf16[2,256,256]{2,1,0:T(8,128)(2,1)S(1)}, bf16[2,256,256]{2,1,0:T(8,128)(2,1)S(1)}, u32[]{:S(2)}, u32[]{:S(2)}) %collective-permute-start.10) | collective-permute-done | bytes 262176 | tf_op jit(solution)/shard_map/ppermute | solution.py:25
  23.7 1.2 %shard_map.97 = (f32[256,256]{1,0:T(8,128)}, f32[256,256]{1,0:T(8,128)}) custom-call(bf16[17,256,256]{2,1,0:T(8,128)(2,1)S(1)} %get-tuple-element.28.inter, f32[17,1,256]{2,1,0:T(1,128)S(1)} %get-tuple-element.29.factors, f32[256,256]{1,0:T(8,128)S(1)} %shard_map.95.refs_0_, bf16[2,256,256]{2,1,0:T(8,128)(2,1)S(1)} %collective-permute-done.10.refs_1_, ...), custom_call_target="tpu_custom_call" | custom-call | flops 134217728 | bytes 524288 | tf_op jit(solution)/shard_map/pallas_call | solution.py:292
  (5 shorter events, 0.1 us)
Async XLA Ops:
  2.3 11.1 %collective-permute-start.1 = (bf16[256,256]{1,0:T(8,128)(2,1)S(1)}, bf16[256,256]{1,0:T(8,128)(2,1)S(1)}, u32[]{:S(2)}, u32[]{:S(2)}) collective-permute-start(bf16[256,256]{1,0:T(8,128)(2,1)S(1)} %get-tuple-element.22.masked.refs_2_.refs_0_.refs_3_), channel_id=1, source_target_pairs={{0,8},{1,9},{2,10},{3,11},{4,12},{5,13},{6,14},{7,15},{8,16},{9,17... | collective-permute-start | bytes 393224 | tf_op jit(solution)/shard_map/ppermute | solution.py:25
  5.4 8.1 %collective-permute-start = (bf16[256,256]{1,0:T(8,128)(2,1)S(1)}, bf16[256,256]{1,0:T(8,128)(2,1)S(1)}, u32[]{:S(2)}, u32[]{:S(2)}) collective-permute-start(bf16[256,256]{1,0:T(8,128)(2,1)S(1)} %get-tuple-element.22.masked.refs_2_.refs_0_.refs_3_), channel_id=1, source_target_pairs={{0,24},{1,25},{2,26},{3,27},{4,28},{5,29},{6,30},{7,31},{8,0},{9,1... | collective-permute-start | bytes 393224 | tf_op jit(solution)/shard_map/ppermute | solution.py:25
  7.5 9.2 %collective-permute-start.6 = (bf16[256,256]{1,0:T(8,128)(2,1)S(1)}, bf16[256,256]{1,0:T(8,128)(2,1)S(1)}, u32[]{:S(2)}, u32[]{:S(2)}) collective-permute-start(bf16[256,256]{1,0:T(8,128)(2,1)S(1)} %get-tuple-element.22.masked.refs_2_.refs_0_.refs_3_), channel_id=1, source_target_pairs={{0,6},{1,7},{2,4},{3,5},{4,2},{5,3},{6,0},{7,1},{8,14},{9,15},{10,... | collective-permute-start | bytes 393224 | tf_op jit(solution)/shard_map/ppermute | solution.py:25
  10.1 10.3 %collective-permute-start.5 = (bf16[256,256]{1,0:T(8,128)(2,1)S(1)}, bf16[256,256]{1,0:T(8,128)(2,1)S(1)}, u32[]{:S(2)}, u32[]{:S(2)}) collective-permute-start(bf16[256,256]{1,0:T(8,128)(2,1)S(1)} %get-tuple-element.22.masked.refs_2_.refs_0_.refs_3_), channel_id=1, source_target_pairs={{0,4},{1,5},{2,6},{3,7},{4,0},{5,1},{6,2},{7,3},{8,12},{9,13},{10,... | collective-permute-start | bytes 393224 | tf_op jit(solution)/shard_map/ppermute | solution.py:25
  10.6 9.8 %collective-permute-start.4 = (bf16[256,256]{1,0:T(8,128)(2,1)S(1)}, bf16[256,256]{1,0:T(8,128)(2,1)S(1)}, u32[]{:S(2)}, u32[]{:S(2)}) collective-permute-start(bf16[256,256]{1,0:T(8,128)(2,1)S(1)} %get-tuple-element.22.masked.refs_2_.refs_0_.refs_3_), channel_id=1, source_target_pairs={{0,2},{1,3},{2,0},{3,1},{4,6},{5,7},{6,4},{7,5},{8,10},{9,11},{10,... | collective-permute-start | bytes 393224 | tf_op jit(solution)/shard_map/ppermute | solution.py:25
  13.5 7.0 %collective-permute-start.7 = (bf16[256,256]{1,0:T(8,128)(2,1)S(1)}, bf16[256,256]{1,0:T(8,128)(2,1)S(1)}, u32[]{:S(2)}, u32[]{:S(2)}) collective-permute-start(bf16[256,256]{1,0:T(8,128)(2,1)S(1)} %get-tuple-element.33), channel_id=1, source_target_pairs={{0,6},{1,7},{2,4},{3,5},{4,2},{5,3},{6,0},{7,1},{8,14},{9,15},{10,... | collective-permute-start | bytes 393224 | tf_op jit(solution)/shard_map/ppermute | solution.py:25
  16.2 5.9 %collective-permute-start.3 = (bf16[256,256]{1,0:T(8,128)(2,1)S(1)}, bf16[256,256]{1,0:T(8,128)(2,1)S(1)}, u32[]{:S(2)}, u32[]{:S(2)}) collective-permute-start(bf16[256,256]{1,0:T(8,128)(2,1)S(1)} %get-tuple-element.33), channel_id=1, source_target_pairs={{0,4},{1,5},{2,6},{3,7},{4,0},{5,1},{6,2},{7,3},{8,12},{9,13},{10,... | collective-permute-start | bytes 393224 | tf_op jit(solution)/shard_map/ppermute | solution.py:25
  16.7 5.2 %collective-permute-start.2 = (bf16[256,256]{1,0:T(8,128)(2,1)S(1)}, bf16[256,256]{1,0:T(8,128)(2,1)S(1)}, u32[]{:S(2)}, u32[]{:S(2)}) collective-permute-start(bf16[256,256]{1,0:T(8,128)(2,1)S(1)} %get-tuple-element.32), channel_id=1, source_target_pairs={{0,2},{1,3},{2,0},{3,1},{4,6},{5,7},{6,4},{7,5},{8,10},{9,11},{10,... | collective-permute-start | bytes 393224 | tf_op jit(solution)/shard_map/ppermute | solution.py:25
  20.4 2.4 %collective-permute-start.8 = (bf16[5,256,256]{2,1,0:T(8,128)(2,1)S(1)}, bf16[5,256,256]{2,1,0:T(8,128)(2,1)S(1)}, u32[]{:S(2)}, u32[]{:S(2)}) collective-permute-start(bf16[5,256,256]{2,1,0:T(8,128)(2,1)S(1)} %shard_map.94), channel_id=1, source_target_pairs={{0,1},{1,0},{2,3},{3,2},{4,5},{5,4},{6,7},{7,6},{8,9},{9,8},{10,11... | collective-permute-start | bytes 1966088 | tf_op jit(solution)/shard_map/ppermute | solution.py:25
  20.5 2.2 %collective-permute-start.9 = (bf16[256,256]{1,0:T(8,128)(2,1)S(1)}, bf16[256,256]{1,0:T(8,128)(2,1)S(1)}, u32[]{:S(2)}, u32[]{:S(2)}) collective-permute-start(bf16[256,256]{1,0:T(8,128)(2,1)S(1)} %shard_map.91.refs_8_), channel_id=1, source_target_pairs={{0,1},{1,0},{2,3},{3,2},{4,5},{5,4},{6,7},{7,6},{8,9},{9,8},{10,11... | collective-permute-start | bytes 393224 | tf_op jit(solution)/shard_map/ppermute | solution.py:25
  22.1 1.6 %collective-permute-start.10 = (bf16[2,256,256]{2,1,0:T(8,128)(2,1)S(1)}, bf16[2,256,256]{2,1,0:T(8,128)(2,1)S(1)}, u32[]{:S(2)}, u32[]{:S(2)}) collective-permute-start(bf16[2,256,256]{2,1,0:T(8,128)(2,1)S(1)} %shard_map.96), channel_id=1, source_target_pairs={{0,1},{1,0},{2,3},{3,2},{4,5},{5,4},{6,7},{7,6},{8,9},{9,8},{10,11... | collective-permute-start | bytes 786440 | tf_op jit(solution)/shard_map/ppermute | solution.py:25

commit v8 on v7

--- a/solution.py
+++ b/solution.py
@@ -315,14 +315,15 @@
     staged = stage(
         aux_count == 1, axis, rank, masked, neighbours, couplings, energies, intersections[0]
     )
-    exchange = exchange_of(pair_factors[0])
-    after, before, staged = lax.optimization_barrier((after, before, staged))
+    before, after, staged = lax.optimization_barrier((before, after, staged))
     total, scale, inter, factors = staged
     side1, side2, side4 = sides_of(axis, before, after)
     far = {bits: swapped(side, axis, bits) for bits, side in ((2, side2), (4, side4), (6, side4))}
     far[6] = passed(far[6], 4)
     mine = stacked(*(own[bits] for bits in (0, *cross)), side1)
+    mine, pair_factors = lax.optimization_barrier((mine, pair_factors))
     theirs = swapped(mine, axis, 1)
+    exchange = exchange_of(pair_factors[0])
     one = (None,)
     near = [own[bits] for bits in (0, *cross)] + [before, after, far[6]]
     near = [(block, one) for block in near]

time: 25.1 us -> 24.9 us (level)
  waiting for transfers between devices: 0.69 us -> 0.41 us
    ppermute x11, waiting for transfers between devices: 0.69 us -> 0.41 us  [permuted(): lax.ppermute(value, axis, [(source, target(source)) for source in range(c...]
  transfers between devices with their start and end apart: 11 -> 11, of which waited for: 3 -> 1; matrix products, arithmetic and copies ran while one was open for 0% -> 0% of each run, Pallas kernels for 31% -> 31%
where the time goes in v8:
time: 24.9 us; the launch traced here: 24.7 us
  starting transfers between devices  12.9 us (52%)
  Pallas kernels  9.94 us (40%)
  between operations  1.44 us (6%)
  waiting for transfers between devices  0.41 us (2%)
    ppermute x11, starting transfers between devices, permuted(): lax.ppermute(value, axis, [(source, target(source)) for source in range(c...  12.9 us
    pallas_call x1, Pallas kernels, exchange_of(): pl.pallas_call(exchange_kernel, out_shape=pltpu.VMEM((width, width), F32)...  3.28 us
    pallas_call x4, Pallas kernels, block_sum(): pl.pallas_call(functools.partial(sum_kernel, first, picks, len(starts)),...  3.05 us
    pallas_call x1, Pallas kernels, stage(): pl.pallas_call(functools.partial(stage_kernel, whole, axis), out_shape=(s...  2.48 us
    pallas_call x1, Pallas kernels, mask(): pl.pallas_call(mask_kernel, out_shape=(pltpu.VMEM(amplitude.shape, BF16),...  1.01 us
  transfers between devices with their start and end apart: 11, of which 1 were waited for; matrix products, arithmetic and copies ran while one was open for 0% of the time, Pallas kernels for 31%

profile of v8, /device:TPU:0, one launch (start us, length us, event | category | flops | bytes accessed | tf_op | source)
XLA Modules:
  0.0 24.7 jit_solution(12785406312523140416)
XLA Ops:
  1.3 1.0 %shard_map.86 = (bf16[256,256]{1,0:T(8,128)(2,1)S(1)}, s32[8,128]{1,0:T(8,128)S(1)}) custom-call(s32[1,1]{1,0:T(1,128)} %bitcast.6.rank, bf16[256,256]{1,0:T(8,128)(2,1)} %bitcast.9), custom_call_target="tpu_custom_call" | custom-call | tf_op jit(solution)/shard_map/pallas_call | solution.py:64
  2.3 3.1 %collective-permute-start = (bf16[256,256]{1,0:T(8,128)(2,1)S(1)}, bf16[256,256]{1,0:T(8,128)(2,1)S(1)}, u32[]{:S(2)}, u32[]{:S(2)}) collective-permute-start(bf16[256,256]{1,0:T(8,128)(2,1)S(1)} %get-tuple-element.24.masked.refs_0_.refs_2_.refs_3_), channel_id=1, source_target_pairs={{0,8},{1,9},{2,10},{3,11},{4,12},{5,13},{6,14},{7,15},{8,16},{9,17... | collective-permute-start | bytes 393224 | tf_op jit(solution)/shard_map/ppermute | solution.py:25
  5.4 2.1 %collective-permute-start.1 = (bf16[256,256]{1,0:T(8,128)(2,1)S(1)}, bf16[256,256]{1,0:T(8,128)(2,1)S(1)}, u32[]{:S(2)}, u32[]{:S(2)}) collective-permute-start(bf16[256,256]{1,0:T(8,128)(2,1)S(1)} %get-tuple-element.24.masked.refs_0_.refs_2_.refs_3_), channel_id=1, source_target_pairs={{0,24},{1,25},{2,26},{3,27},{4,28},{5,29},{6,30},{7,31},{8,0},{9,1... | collective-permute-start | bytes 393224 | tf_op jit(solution)/shard_map/ppermute | solution.py:25
  7.5 2.6 %collective-permute-start.6 = (bf16[256,256]{1,0:T(8,128)(2,1)S(1)}, bf16[256,256]{1,0:T(8,128)(2,1)S(1)}, u32[]{:S(2)}, u32[]{:S(2)}) collective-permute-start(bf16[256,256]{1,0:T(8,128)(2,1)S(1)} %get-tuple-element.24.masked.refs_0_.refs_2_.refs_3_), channel_id=1, source_target_pairs={{0,6},{1,7},{2,4},{3,5},{4,2},{5,3},{6,0},{7,1},{8,14},{9,15},{10,... | collective-permute-start | bytes 393224 | tf_op jit(solution)/shard_map/ppermute | solution.py:25
  10.1 0.5 %collective-permute-start.4 = (bf16[256,256]{1,0:T(8,128)(2,1)S(1)}, bf16[256,256]{1,0:T(8,128)(2,1)S(1)}, u32[]{:S(2)}, u32[]{:S(2)}) collective-permute-start(bf16[256,256]{1,0:T(8,128)(2,1)S(1)} %get-tuple-element.24.masked.refs_0_.refs_2_.refs_3_), channel_id=1, source_target_pairs={{0,2},{1,3},{2,0},{3,1},{4,6},{5,7},{6,4},{7,5},{8,10},{9,11},{10,... | collective-permute-start | bytes 393224 | tf_op jit(solution)/shard_map/ppermute | solution.py:25
  10.6 0.3 %collective-permute-start.5 = (bf16[256,256]{1,0:T(8,128)(2,1)S(1)}, bf16[256,256]{1,0:T(8,128)(2,1)S(1)}, u32[]{:S(2)}, u32[]{:S(2)}) collective-permute-start(bf16[256,256]{1,0:T(8,128)(2,1)S(1)} %get-tuple-element.24.masked.refs_0_.refs_2_.refs_3_), channel_id=1, source_target_pairs={{0,4},{1,5},{2,6},{3,7},{4,0},{5,1},{6,2},{7,3},{8,12},{9,13},{10,... | collective-permute-start | bytes 393224 | tf_op jit(solution)/shard_map/ppermute | solution.py:25
  10.9 2.5 %shard_map.87 = (f32[256,256]{1,0:T(8,128)S(1)}, f32[256,256]{1,0:T(8,128)S(1)}, bf16[17,256,256]{2,1,0:T(8,128)(2,1)S(1)}, f32[17,1,256]{2,1,0:T(1,128)S(1)}) custom-call(s32[8,128]{1,0:T(8,128)S(1)} %get-tuple-element.25.rank, bf16[256,256]{1,0:T(8,128)(2,1)S(1)} %get-tuple-element.24.masked.refs_0_.refs_2_.refs_3_, s32[1,16]{1,0:T(1,128)} %neighbours.1, ...), custom_call_target="tpu_custom_call" | custom-call | flops 536870912 | bytes 2097152 | tf_op jit(solution)/shard_map/pallas_call | solution.py:196
  13.4 0.0 collective-permute-done.before.refs_6_
  13.4 0.0 collective-permute-done.1.after.refs_7_
  13.5 2.7 %collective-permute-start.7 = (bf16[256,256]{1,0:T(8,128)(2,1)S(1)}, bf16[256,256]{1,0:T(8,128)(2,1)S(1)}, u32[]{:S(2)}, u32[]{:S(2)}) collective-permute-start(bf16[256,256]{1,0:T(8,128)(2,1)S(1)} %get-tuple-element.35), channel_id=1, source_target_pairs={{0,6},{1,7},{2,4},{3,5},{4,2},{5,3},{6,0},{7,1},{8,14},{9,15},{10,... | collective-permute-start | bytes 393224 | tf_op jit(solution)/shard_map/ppermute | solution.py:25
  16.2 0.5 %collective-permute-start.3 = (bf16[256,256]{1,0:T(8,128)(2,1)S(1)}, bf16[256,256]{1,0:T(8,128)(2,1)S(1)}, u32[]{:S(2)}, u32[]{:S(2)}) collective-permute-start(bf16[256,256]{1,0:T(8,128)(2,1)S(1)} %get-tuple-element.35), channel_id=1, source_target_pairs={{0,4},{1,5},{2,6},{3,7},{4,0},{5,1},{6,2},{7,3},{8,12},{9,13},{10,... | collective-permute-start | bytes 393224 | tf_op jit(solution)/shard_map/ppermute | solution.py:25
  16.7 0.0 collective-permute-done.6.block
  16.7 0.4 %collective-permute-start.2 = (bf16[256,256]{1,0:T(8,128)(2,1)S(1)}, bf16[256,256]{1,0:T(8,128)(2,1)S(1)}, u32[]{:S(2)}, u32[]{:S(2)}) collective-permute-start(bf16[256,256]{1,0:T(8,128)(2,1)S(1)} %get-tuple-element.34), channel_id=1, source_target_pairs={{0,2},{1,3},{2,0},{3,1},{4,6},{5,7},{6,4},{7,5},{8,10},{9,11},{10,... | collective-permute-start | bytes 393224 | tf_op jit(solution)/shard_map/ppermute | solution.py:25
  17.1 0.0 collective-permute-done.4.refs_1_.refs_3_
  17.1 0.0 collective-permute-done.5.refs_2_.refs_4_
  17.1 0.1 collective-permute-start.8
  17.2 3.3 %shard_map.91.refs_0_ = f32[256,256]{1,0:T(8,128)S(1)} custom-call(bf16[2,5120,256]{2,1,0:T(8,128)(2,1)} %bitcast.7), custom_call_target="tpu_custom_call" | custom-call | flops 536870912 | bytes 2097152 | tf_op jit(solution)/shard_map/pallas_call | solution.py:251
  20.5 0.0 collective-permute-done.7.block
  20.5 0.6 %collective-permute-start.9 = (bf16[256,256]{1,0:T(8,128)(2,1)S(1)}, bf16[256,256]{1,0:T(8,128)(2,1)S(1)}, u32[]{:S(2)}, u32[]{:S(2)}) collective-permute-start(bf16[256,256]{1,0:T(8,128)(2,1)S(1)} %shard_map.92.refs_8_), channel_id=1, source_target_pairs={{0,1},{1,0},{2,3},{3,2},{4,5},{5,4},{6,7},{7,6},{8,9},{9,8},{10,11... | collective-permute-start | bytes 393224 | tf_op jit(solution)/shard_map/ppermute | solution.py:25
  21.1 0.7 %shard_map.93.refs_0_ = f32[256,256]{1,0:T(8,128)S(1)} custom-call(bf16[17,256,256]{2,1,0:T(8,128)(2,1)S(1)} %get-tuple-element.30.inter, f32[17,1,256]{2,1,0:T(1,128)S(1)} %get-tuple-element.31.factors, f32[256,256]{1,0:T(8,128)S(1)} %shard_map.91.refs_0_, f32[256,256]{1,0:T(8,128)S(1)} %get-tuple-element.38.refs_1_, ...), custom_call_target="tpu_custom_call" | custom-call | flops 469762048 | bytes 1835008 | tf_op jit(solution)/shard_map/pallas_call | solution.py:292
  21.9 0.0 collective-permute-done.2.refs_1_.refs_0_
  21.9 0.0 collective-permute-done.3.refs_2_.refs_1_
  21.9 0.1 collective-permute-start.10
  22.0 0.4 %shard_map.94.refs_0_ = f32[256,256]{1,0:T(8,128)S(1)} custom-call(bf16[17,256,256]{2,1,0:T(8,128)(2,1)S(1)} %get-tuple-element.30.inter, f32[17,1,256]{2,1,0:T(1,128)S(1)} %get-tuple-element.31.factors, f32[256,256]{1,0:T(8,128)S(1)} %shard_map.93.refs_0_, bf16[256,256]{1,0:T(8,128)(2,1)S(1)} %collective-permute-done.2.refs_1_.refs_0_, ...), custom_call_target="tpu_custom_call" | custom-call | flops 8589934592 | bytes 33554432 | tf_op jit(solution)/shard_map/pallas_call | solution.py:292
  22.4 0.0 collective-permute-done.9.refs_2_
  22.4 0.0 collective-permute-done.8.refs_1_
  22.4 0.7 %shard_map.95.refs_0_ = f32[256,256]{1,0:T(8,128)S(1)} custom-call(bf16[17,256,256]{2,1,0:T(8,128)(2,1)S(1)} %get-tuple-element.30.inter, f32[17,1,256]{2,1,0:T(1,128)S(1)} %get-tuple-element.31.factors, f32[256,256]{1,0:T(8,128)S(1)} %shard_map.94.refs_0_, bf16[5,256,256]{2,1,0:T(8,128)(2,1)S(1)} %collective-permute-done.8.refs_1_, ...), custom_call_target="tpu_custom_call" | custom-call | flops 402653184 | bytes 1572864 | tf_op jit(solution)/shard_map/pallas_call | solution.py:292
  23.1 0.4 %collective-permute-done.10.refs_1_ = bf16[2,256,256]{2,1,0:T(8,128)(2,1)S(1)} collective-permute-done((bf16[2,256,256]{2,1,0:T(8,128)(2,1)S(1)}, bf16[2,256,256]{2,1,0:T(8,128)(2,1)S(1)}, u32[]{:S(2)}, u32[]{:S(2)}) %collective-permute-start.10) | collective-permute-done | bytes 262176 | tf_op jit(solution)/shard_map/ppermute | solution.py:25
  23.5 1.2 %shard_map.97 = (f32[256,256]{1,0:T(8,128)}, f32[256,256]{1,0:T(8,128)}) custom-call(bf16[17,256,256]{2,1,0:T(8,128)(2,1)S(1)} %get-tuple-element.30.inter, f32[17,1,256]{2,1,0:T(1,128)S(1)} %get-tuple-element.31.factors, f32[256,256]{1,0:T(8,128)S(1)} %shard_map.95.refs_0_, bf16[2,256,256]{2,1,0:T(8,128)(2,1)S(1)} %collective-permute-done.10.refs_1_, ...), custom_call_target="tpu_custom_call" | custom-call | flops 134217728 | bytes 524288 | tf_op jit(solution)/shard_map/pallas_call | solution.py:292
  (5 shorter events, 0.1 us)
Async XLA Ops:
  2.3 11.1 %collective-permute-start = (bf16[256,256]{1,0:T(8,128)(2,1)S(1)}, bf16[256,256]{1,0:T(8,128)(2,1)S(1)}, u32[]{:S(2)}, u32[]{:S(2)}) collective-permute-start(bf16[256,256]{1,0:T(8,128)(2,1)S(1)} %get-tuple-element.24.masked.refs_0_.refs_2_.refs_3_), channel_id=1, source_target_pairs={{0,8},{1,9},{2,10},{3,11},{4,12},{5,13},{6,14},{7,15},{8,16},{9,17... | collective-permute-start | bytes 393224 | tf_op jit(solution)/shard_map/ppermute | solution.py:25
  5.4 8.1 %collective-permute-start.1 = (bf16[256,256]{1,0:T(8,128)(2,1)S(1)}, bf16[256,256]{1,0:T(8,128)(2,1)S(1)}, u32[]{:S(2)}, u32[]{:S(2)}) collective-permute-start(bf16[256,256]{1,0:T(8,128)(2,1)S(1)} %get-tuple-element.24.masked.refs_0_.refs_2_.refs_3_), channel_id=1, source_target_pairs={{0,24},{1,25},{2,26},{3,27},{4,28},{5,29},{6,30},{7,31},{8,0},{9,1... | collective-permute-start | bytes 393224 | tf_op jit(solution)/shard_map/ppermute | solution.py:25
  7.5 9.2 %collective-permute-start.6 = (bf16[256,256]{1,0:T(8,128)(2,1)S(1)}, bf16[256,256]{1,0:T(8,128)(2,1)S(1)}, u32[]{:S(2)}, u32[]{:S(2)}) collective-permute-start(bf16[256,256]{1,0:T(8,128)(2,1)S(1)} %get-tuple-element.24.masked.refs_0_.refs_2_.refs_3_), channel_id=1, source_target_pairs={{0,6},{1,7},{2,4},{3,5},{4,2},{5,3},{6,0},{7,1},{8,14},{9,15},{10,... | collective-permute-start | bytes 393224 | tf_op jit(solution)/shard_map/ppermute | solution.py:25
  10.1 7.0 %collective-permute-start.4 = (bf16[256,256]{1,0:T(8,128)(2,1)S(1)}, bf16[256,256]{1,0:T(8,128)(2,1)S(1)}, u32[]{:S(2)}, u32[]{:S(2)}) collective-permute-start(bf16[256,256]{1,0:T(8,128)(2,1)S(1)} %get-tuple-element.24.masked.refs_0_.refs_2_.refs_3_), channel_id=1, source_target_pairs={{0,2},{1,3},{2,0},{3,1},{4,6},{5,7},{6,4},{7,5},{8,10},{9,11},{10,... | collective-permute-start | bytes 393224 | tf_op jit(solution)/shard_map/ppermute | solution.py:25
  10.6 6.5 %collective-permute-start.5 = (bf16[256,256]{1,0:T(8,128)(2,1)S(1)}, bf16[256,256]{1,0:T(8,128)(2,1)S(1)}, u32[]{:S(2)}, u32[]{:S(2)}) collective-permute-start(bf16[256,256]{1,0:T(8,128)(2,1)S(1)} %get-tuple-element.24.masked.refs_0_.refs_2_.refs_3_), channel_id=1, source_target_pairs={{0,4},{1,5},{2,6},{3,7},{4,0},{5,1},{6,2},{7,3},{8,12},{9,13},{10,... | collective-permute-start | bytes 393224 | tf_op jit(solution)/shard_map/ppermute | solution.py:25
  13.5 7.0 %collective-permute-start.7 = (bf16[256,256]{1,0:T(8,128)(2,1)S(1)}, bf16[256,256]{1,0:T(8,128)(2,1)S(1)}, u32[]{:S(2)}, u32[]{:S(2)}) collective-permute-start(bf16[256,256]{1,0:T(8,128)(2,1)S(1)} %get-tuple-element.35), channel_id=1, source_target_pairs={{0,6},{1,7},{2,4},{3,5},{4,2},{5,3},{6,0},{7,1},{8,14},{9,15},{10,... | collective-permute-start | bytes 393224 | tf_op jit(solution)/shard_map/ppermute | solution.py:25
  16.2 5.7 %collective-permute-start.3 = (bf16[256,256]{1,0:T(8,128)(2,1)S(1)}, bf16[256,256]{1,0:T(8,128)(2,1)S(1)}, u32[]{:S(2)}, u32[]{:S(2)}) collective-permute-start(bf16[256,256]{1,0:T(8,128)(2,1)S(1)} %get-tuple-element.35), channel_id=1, source_target_pairs={{0,4},{1,5},{2,6},{3,7},{4,0},{5,1},{6,2},{7,3},{8,12},{9,13},{10,... | collective-permute-start | bytes 393224 | tf_op jit(solution)/shard_map/ppermute | solution.py:25
  16.7 5.2 %collective-permute-start.2 = (bf16[256,256]{1,0:T(8,128)(2,1)S(1)}, bf16[256,256]{1,0:T(8,128)(2,1)S(1)}, u32[]{:S(2)}, u32[]{:S(2)}) collective-permute-start(bf16[256,256]{1,0:T(8,128)(2,1)S(1)} %get-tuple-element.34), channel_id=1, source_target_pairs={{0,2},{1,3},{2,0},{3,1},{4,6},{5,7},{6,4},{7,5},{8,10},{9,11},{10,... | collective-permute-start | bytes 393224 | tf_op jit(solution)/shard_map/ppermute | solution.py:25
  17.1 5.3 %collective-permute-start.8 = (bf16[5,256,256]{2,1,0:T(8,128)(2,1)S(1)}, bf16[5,256,256]{2,1,0:T(8,128)(2,1)S(1)}, u32[]{:S(2)}, u32[]{:S(2)}) collective-permute-start(bf16[5,256,256]{2,1,0:T(8,128)(2,1)S(1)} %shard_map.90), channel_id=1, source_target_pairs={{0,1},{1,0},{2,3},{3,2},{4,5},{5,4},{6,7},{7,6},{8,9},{9,8},{10,11... | collective-permute-start | bytes 1966088 | tf_op jit(solution)/shard_map/ppermute | solution.py:25
  20.5 1.9 %collective-permute-start.9 = (bf16[256,256]{1,0:T(8,128)(2,1)S(1)}, bf16[256,256]{1,0:T(8,128)(2,1)S(1)}, u32[]{:S(2)}, u32[]{:S(2)}) collective-permute-start(bf16[256,256]{1,0:T(8,128)(2,1)S(1)} %shard_map.92.refs_8_), channel_id=1, source_target_pairs={{0,1},{1,0},{2,3},{3,2},{4,5},{5,4},{6,7},{7,6},{8,9},{9,8},{10,11... | collective-permute-start | bytes 393224 | tf_op jit(solution)/shard_map/ppermute | solution.py:25
  21.9 1.6 %collective-permute-start.10 = (bf16[2,256,256]{2,1,0:T(8,128)(2,1)S(1)}, bf16[2,256,256]{2,1,0:T(8,128)(2,1)S(1)}, u32[]{:S(2)}, u32[]{:S(2)}) collective-permute-start(bf16[2,256,256]{2,1,0:T(8,128)(2,1)S(1)} %shard_map.96), channel_id=1, source_target_pairs={{0,1},{1,0},{2,3},{3,2},{4,5},{5,4},{6,7},{7,6},{8,9},{9,8},{10,11... | collective-permute-start | bytes 786440 | tf_op jit(solution)/shard_map/ppermute | solution.py:25
